TPU v7x, 32 devices: a whole 2x2x4 slice. The times are simulated.
32 devices in a mesh: row: 4 (over x, core), col: 8 (over z, y).
Axes of the slice: x: 2, y: 2, z: 4, core: 2. Of those that a mesh axis runs over, the one named last changes fastest.
Arguments:
- region: bfloat16 [64, 256, 256], P('row', 'col'), may hold values from -6 to 6
- reduce_weight: bfloat16 [256, 512], P(None, 'col'), may hold values from -0.375 to 0.375
- group_weight: bfloat16 [144, 512], P(None, 'col'), may hold values from -0.5 to 0.5
- expand_weight: bfloat16 [512, 512], P(None, 'col'), may hold values from -0.25 to 0.25
- shortcut_weight: bfloat16 [256, 512], P(None, 'col'), may hold values from -0.375 to 0.375
- cotangent: bfloat16 [32, 128, 512], P('row', 'col'), may hold values from -6 to 6
Outputs:
- block_out: bfloat16 [32, 128, 512], P('row', 'col')
- region_grad: bfloat16 [64, 256, 256], P('row', 'col')
- reduce_grad: float32 [256, 512], P(None, 'col')
- group_grad: float32 [144, 512], P(None, 'col')
- expand_grad: float32 [512, 512], P(None, 'col')
- shortcut_grad: float32 [256, 512], P(None, 'col')
All inputs are finite; a program needn't handle non-finite values.
Results may differ from a plain program's by a relative error of at most 0.0061.
Values may be sent and summed in bfloat16 or wider, within the bound.
No kernel may reach another device: no remote copies, remote signals or barrier semaphores. Data moves between devices by JAX's collectives and lax.ppermute only.
A program may use at most 128 MiB of HBM per device.

v0:
```python
import jax
import jax.numpy as jnp
from jax import lax
from jax.sharding import PartitionSpec as P

GROUPS = 32
GW = 16


def shifted(x, axis, by):
    devices = lax.axis_size(axis)
    pairs = [(i, i + by) for i in range(devices) if 0 <= i + by < devices]
    return lax.ppermute(x, axis, pairs)


def activate(value):
    return value * jax.nn.sigmoid(value)


def slope(value):
    sigma = jax.nn.sigmoid(value)
    return sigma * (1.0 + value * (1.0 - sigma))


def tap_patch(padded, row_step, col_step, half_rows, half_cols):
    width_mid = padded.shape[2]
    patch = lax.slice(
        padded,
        (row_step, col_step, 0),
        (row_step + 2 * half_rows - 1, col_step + 2 * half_cols - 1, width_mid),
        (2, 2, 1),
    )
    return patch.reshape(half_rows, half_cols, GROUPS, GW)


def per_device(region, reduce_weight, group_weight, expand_weight, shortcut_weight, cotangent):
    tile_rows, tile_cols, in_chans = region.shape
    half_rows = tile_rows // 2
    half_cols = tile_cols // 2
    full_reduce, full_group, full_expand, full_short = (
        lax.all_gather(reduce_weight, "col", axis=1, tiled=True),
        lax.all_gather(group_weight, "col", axis=1, tiled=True),
        lax.all_gather(expand_weight, "col", axis=1, tiled=True),
        lax.all_gather(shortcut_weight, "col", axis=1, tiled=True),
    )
    width_mid = full_reduce.shape[1]
    width_out = full_expand.shape[1]
    flat = region.reshape(-1, in_chans)
    pre_one = jnp.dot(flat, full_reduce, preferred_element_type=jnp.float32).reshape(
        tile_rows, tile_cols, width_mid
    )
    hidden_one = activate(pre_one).astype(jnp.bfloat16)
    upper_rim = shifted(hidden_one[-1:], "row", 1)
    extended = jnp.concatenate([upper_rim, hidden_one], axis=0)
    left_rim = shifted(extended[:, -1:], "col", 1)
    padded = jnp.concatenate([left_rim, extended], axis=1)
    patches = []
    kernels = []
    accum = jnp.zeros((GROUPS, half_rows, half_cols, GW), jnp.float32)
    for offset in range(9):
        row_step, col_step = divmod(offset, 3)
        patch = tap_patch(padded, row_step, col_step, half_rows, half_cols)
        kernel = full_group[offset * GW : (offset + 1) * GW].reshape(GW, GROUPS, GW)
        patches.append(patch)
        kernels.append(kernel)
        accum = accum + lax.dot_general(
            patch, kernel, (((3,), (0,)), ((2,), (1,))), preferred_element_type=jnp.float32
        )
    pre_two = jnp.transpose(accum, (1, 2, 0, 3)).reshape(-1, width_mid)
    hidden_two = activate(pre_two).astype(jnp.bfloat16)
    strided = region[::2, ::2].reshape(-1, in_chans)
    summed = jnp.dot(hidden_two, full_expand, preferred_element_type=jnp.float32) + jnp.dot(
        strided, full_short, preferred_element_type=jnp.float32
    )
    block_out = activate(summed).astype(jnp.bfloat16).reshape(half_rows, half_cols, width_out)
    grad_sum = (cotangent.reshape(-1, width_out).astype(jnp.float32) * slope(summed)).astype(
        jnp.bfloat16
    )
    contract_rows = (((0,), (0,)), ((), ()))
    contract_cols = (((1,), (1,)), ((), ()))
    expand_term = lax.dot_general(
        hidden_two, grad_sum, contract_rows, preferred_element_type=jnp.float32
    )
    short_term = lax.dot_general(
        strided, grad_sum, contract_rows, preferred_element_type=jnp.float32
    )
    grad_two = lax.dot_general(
        grad_sum, full_expand, contract_cols, preferred_element_type=jnp.float32
    )
    grad_two = (
        (grad_two * slope(pre_two)).astype(jnp.bfloat16).reshape(half_rows, half_cols, GROUPS, GW)
    )
    spread = jnp.zeros((half_rows + 1, 2, half_cols + 1, 2, width_mid), jnp.float32)
    pieces = []
    for offset in range(9):
        row_step, col_step = divmod(offset, 3)
        piece = lax.dot_general(
            patches[offset],
            grad_two,
            (((0, 1), (0, 1)), ((2,), (2,))),
            preferred_element_type=jnp.float32,
        )
        pieces.append(jnp.transpose(piece, (1, 0, 2)).reshape(GW, width_mid))
        backed = lax.dot_general(
            grad_two,
            kernels[offset],
            (((3,), (2,)), ((2,), (1,))),
            preferred_element_type=jnp.float32,
        )
        backed = jnp.transpose(backed, (1, 2, 0, 3)).reshape(half_rows, half_cols, width_mid)
        row_base = row_step // 2
        col_base = col_step // 2
        spread = spread.at[
            row_base : row_base + half_rows,
            row_step % 2,
            col_base : col_base + half_cols,
            col_step % 2,
        ].add(backed)
    group_term = jnp.concatenate(pieces, axis=0)
    spread = spread.reshape(2 * half_rows + 2, 2 * half_cols + 2, width_mid)[
        : tile_rows + 1, : tile_cols + 1
    ]
    from_right = shifted(spread[:, :1].astype(jnp.bfloat16), "col", -1).astype(jnp.float32)
    folded = spread[:, 1:]
    folded = folded.at[:, -1:].add(from_right)
    from_below = shifted(folded[:1].astype(jnp.bfloat16), "row", -1).astype(jnp.float32)
    folded = folded[1:]
    folded = folded.at[-1:].add(from_below)
    grad_one = (folded * slope(pre_one)).astype(jnp.bfloat16).reshape(-1, width_mid)
    reduce_term = lax.dot_general(flat, grad_one, contract_rows, preferred_element_type=jnp.float32)
    region_grad = lax.dot_general(
        grad_one, full_reduce, contract_cols, preferred_element_type=jnp.float32
    )
    short_back = lax.dot_general(
        grad_sum, full_short, contract_cols, preferred_element_type=jnp.float32
    )
    region_grad = region_grad.reshape(half_rows, 2, half_cols, 2, in_chans)
    region_grad = region_grad.at[:, 0, :, 0].add(short_back.reshape(half_rows, half_cols, in_chans))
    region_grad = region_grad.reshape(tile_rows, tile_cols, in_chans).astype(jnp.bfloat16)
    shards = (
        lax.psum_scatter(reduce_term, "col", scatter_dimension=1, tiled=True),
        lax.psum_scatter(group_term, "col", scatter_dimension=1, tiled=True),
        lax.psum_scatter(expand_term, "col", scatter_dimension=1, tiled=True),
        lax.psum_scatter(short_term, "col", scatter_dimension=1, tiled=True),
    )
    reduce_grad, group_grad, expand_grad, shortcut_grad = lax.psum(
        (shards[0], shards[1], shards[2], shards[3]), "row"
    )
    return (block_out, region_grad, reduce_grad, group_grad, expand_grad, shortcut_grad)


def solution(mesh):
    in_specs = (
        P("row", "col", None),
        P(None, "col"),
        P(None, "col"),
        P(None, "col"),
        P(None, "col"),
        P("row", "col", None),
    )
    out_specs = (
        P("row", "col", None),
        P("row", "col", None),
        P(None, "col"),
        P(None, "col"),
        P(None, "col"),
        P(None, "col"),
    )
    return jax.shard_map(
        per_device, mesh=mesh, in_specs=in_specs, out_specs=out_specs, check_vma=False
    )
```

profile of v0, /device:TPU:0, one launch (start us, length us, event | category | flops | bytes accessed | tf_op | source)
XLA Modules:
  0.0 577.9 jit_solution(15111253715819097140)
XLA Ops:
  7.2 32.7 %all_gather.12 = bf16[256,512]{0,1:T(8,128)(2,1)S(1)} all-gather(bf16[256,64]{0,1:T(8,128)(2,1)} %param.31), channel_id=1, replica_groups=mesh['row'=4,'col'=8] {'col'}, dimensions={1}, use_global_device_ids=true | all-gather | bytes 294912 | tf_op jit(solution)/shard_map/all_gather | solution.py:41
  40.0 2.5 multiply_convert_fusion.1
  45.3 30.7 %all_gather.13 = bf16[144,512]{0,1:T(8,128)(2,1)S(1)} all-gather(bf16[144,64]{0,1:T(8,128)(2,1)S(1)} %copy-done.57), channel_id=1, replica_groups=mesh['row'=4,'col'=8] {'col'}, dimensions={1}, use_global_device_ids=true | all-gather | bytes 165888 | tf_op jit(solution)/shard_map/all_gather | solution.py:42
  76.1 33.6 %all_gather.14 = bf16[512,512]{0,1:T(8,128)(2,1)} all-gather(bf16[512,64]{0,1:T(8,128)(2,1)S(1)} %copy-done.56), channel_id=1, replica_groups=mesh['row'=4,'col'=8] {'col'}, dimensions={1}, use_global_device_ids=true | all-gather | bytes 589824 | tf_op jit(solution)/shard_map/all_gather | solution.py:43
  111.6 1.8 copy.205
  114.3 1.9 copy.208
  117.0 1.9 copy.214
  122.5 1.9 fusion.39
  124.4 32.8 %all_gather.15 = bf16[256,512]{0,1:T(8,128)(2,1)} all-gather(bf16[256,64]{0,1:T(8,128)(2,1)S(1)} %copy-done.58), channel_id=1, replica_groups=mesh['row'=4,'col'=8] {'col'}, dimensions={1}, use_global_device_ids=true | all-gather | bytes 294912 | tf_op jit(solution)/shard_map/all_gather | solution.py:44
  157.2 3.1 slice.577
  162.6 2.8 copy.217
  165.4 2.6 slice.563
  167.9 2.5 slice.561
  170.5 4.3 collective-permute-start.1
  174.8 2.8 reshape.622
  177.6 2.8 copy.196
  182.2 2.8 copy.199
  185.1 3.2 fusion.37
  188.3 1.9 fusion.36
  191.1 2.6 slice.571
  193.7 2.5 slice.565
  198.3 2.1 copy.193
  202.3 2.8 copy.202
  205.1 2.7 reshape.632
  207.8 3.3 copy.211
  211.1 1.9 fusion.41
  213.0 1.9 fusion.38
  221.1 1.9 fusion.8
  225.1 1.9 convolution_bitcast_fusion.7
  227.0 1.9 convolution_bitcast_fusion.6
  228.9 2.1 convolution_bitcast_fusion.5
  231.0 1.9 convolution_bitcast_fusion.4
  232.9 2.0 convolution_bitcast_fusion.3
  234.9 2.0 convolution_bitcast_fusion.2
  236.8 1.9 convolution_bitcast_fusion.1
  238.8 2.0 convolution_bitcast_fusion
  241.4 4.1 copy.168
  245.5 3.8 add.180
  249.3 4.1 copy.171
  253.4 3.7 reshape.642
  257.1 4.1 copy.174
  261.2 3.1 reshape.643
  264.3 4.2 copy.177
  268.6 3.7 reshape.644
  272.2 4.1 copy.180
  276.3 3.9 reshape.645
  280.2 4.2 copy.183
  284.4 3.7 reshape.646
  288.0 4.2 copy.186
  292.2 3.7 reshape.647
  295.9 4.2 copy.189
  300.1 3.7 reshape.648
  303.7 2.6 copy.165
  306.3 4.0 add.179
  319.0 2.0 copy.190
  321.1 2.1 reshape.649
  325.8 3.3 collective-permute-done.2
  329.1 2.0 scatter-add.55
  349.5 2.0 convolution_bitcast_fusion.16
  358.2 44.5 %reduce-scatter.7.cloned.1.call-done = f32[256,64]{0,1:T(8,128)} async-done(((f32[256,512]{0,1:T(8,128)}), f32[256,64]{0,1:T(8,128)}) %reduce-scatter.7.cloned.1.call-update) | async-done | bytes 65552 | tf_op jit(solution)/shard_map/reduce_scatter | solution.py:141
  402.7 65.9 %reduce-scatter.9.cloned.1.call-done = f32[512,64]{0,1:T(8,128)} async-done(((f32[512,512]{0,1:T(8,128)}), f32[512,64]{0,1:T(8,128)}) %reduce-scatter.9.cloned.1.call-update) | async-done | bytes 131088 | tf_op jit(solution)/shard_map/reduce_scatter | solution.py:143
  469.7 63.3 %reduce-scatter.13.cloned.1.call-done = f32[64,144]{1,0:T(8,128)} async-done(((f32[512,144]{1,0:T(8,128)}), f32[64,144]{1,0:T(8,128)}) %reduce-scatter.13.cloned.1.call-update) | async-done | bytes 36880
  534.0 11.0 %psum.29 = f32[144,64]{1,0:T(8,128)S(1)} all-reduce(f32[144,64]{1,0:T(8,128)S(1)} %copy.313), channel_id=1, replica_groups=mesh['row'=4,'col'=8] {'row'}, use_global_device_ids=true, to_apply=%region_3.0 | all-reduce | flops 9216 | bytes 73728 | tf_op jit(solution)/shard_map/psum | solution.py:146
  545.7 21.0 %all-reduce.4.cloned.1.call-done = (f32[256,64]{0,1:T(8,128)}, f32[512,64]{0,1:T(8,128)}, f32[256,64]{0,1:T(8,128)}) async-done(((f32[256,64]{0,1:T(8,128)}, f32[512,64]{0,1:T(8,128)}, f32[256,64]{0,1:T(8,128)}), (f32[256,64]{0,1:T(8,128)}, f32[512,64]{0,1:T(8,128)}, f32[256,64]{0,1:T(8,128)})) %all-reduce.4.cloned.1.call-update) | async-done | bytes 262160 | tf_op jit(solution)/shard_map/psum | solution.py:146
  (234 shorter events, 71.1 us)
Async XLA Ops:
  7.2 351.0 %reduce-scatter.11.cloned.1.call-start = ((), (), s32[]{:S(2)}) async-start(), calls=%async_computation.6 | async-start | bytes 589824 | tf_op jit(solution)/shard_map/reduce_scatter | solution.py:144
  40.0 2.5 copy-start.39
  40.0 5.4 copy-start.57
  40.0 36.1 %copy-start.56 = (bf16[512,64]{0,1:T(8,128)(2,1)S(1)}, bf16[512,64]{0,1:T(8,128)(2,1)}, u32[]{:S(2)}) copy-start(bf16[512,64]{0,1:T(8,128)(2,1)} %param.33) | copy-start | bytes 196612
  43.0 122.3 %collective-permute-start = (bf16[1,32,512]{2,1,0:T(8,128)(2,1)}, bf16[1,32,512]{2,1,0:T(8,128)(2,1)S(1)}, u32[]{:S(2)}, u32[]{:S(2)}) collective-permute-start(bf16[1,32,512]{2,1,0:T(8,128)(2,1)} %slice.592), channel_id=1, source_target_pairs={{0,8},{8,16},{16,24},{1,9},{9,17},{17,25},{2,10},{10,18},{18,26},{... | collective-permute-start | bytes 98312 | tf_op jit(solution)/shard_map/ppermute | solution.py:13
  110.7 8.1 %copy-start.20 = (bf16[16,512]{0,1:T(8,128)(2,1)}, bf16[16,512]{0,1:T(8,128)(2,1)S(1)}, u32[]{:S(2)}) copy-start(bf16[16,512]{0,1:T(8,128)(2,1)S(1)} %get-tuple-element.168) | copy-start | bytes 49156
  110.7 9.9 %copy-start.24 = (bf16[16,512]{0,1:T(8,128)(2,1)}, bf16[16,512]{0,1:T(8,128)(2,1)S(1)}, u32[]{:S(2)}) copy-start(bf16[16,512]{0,1:T(8,128)(2,1)S(1)} %get-tuple-element.170) | copy-start | bytes 49156
  110.7 11.8 %copy-start.26 = (bf16[16,512]{0,1:T(8,128)(2,1)}, bf16[16,512]{0,1:T(8,128)(2,1)S(1)}, u32[]{:S(2)}) copy-start(bf16[16,512]{0,1:T(8,128)(2,1)S(1)} %get-tuple-element.171) | copy-start | bytes 49156
  110.7 74.4 %copy-start.30 = (bf16[16,512]{0,1:T(8,128)(2,1)}, bf16[16,512]{0,1:T(8,128)(2,1)S(1)}, u32[]{:S(2)}) copy-start(bf16[16,512]{0,1:T(8,128)(2,1)S(1)} %get-tuple-element.173) | copy-start | bytes 49156
  118.8 1.8 copy-start.8
  120.6 1.9 copy-start.4
  122.5 1.9 copy-start.58
  170.5 9.9 %copy-start.46 = (bf16[8,16,512]{2,1,0:T(8,128)(2,1)S(1)}, bf16[8,16,512]{2,1,0:T(8,128)(2,1)}, u32[]{:S(2)}) copy-start(bf16[8,16,512]{2,1,0:T(8,128)(2,1)} %slice.563) | copy-start | bytes 393220
  170.5 19.6 %collective-permute-start.1 = (bf16[17,1,512]{2,1,0:T(2,128)(2,1)S(1)}, bf16[17,1,512]{2,1,0:T(2,128)(2,1)}, u32[]{:S(2)}, u32[]{:S(2)}) collective-permute-start(bf16[17,1,512]{2,1,0:T(2,128)(2,1)S(1)} %fusion.13), channel_id=1, source_target_pairs={{0,1},{1,2},{2,3},{3,4},{4,5},{5,6},{6,7},{8,9},{9,10},{10,11},{11... | collective-permute-start | bytes 52232 | tf_op jit(solution)/shard_map/ppermute | solution.py:13
  185.1 3.2 copy-start.6
  185.1 3.2 copy-start.32
  196.5 3.9 copy-start.47
  200.5 14.5 %copy-start.11 = (bf16[8,16,32,16]{1,3,0,2:T(8,128)(2,1)}, bf16[8,16,32,16]{1,3,0,2:T(8,128)(2,1)S(1)}, u32[]{:S(2)}) copy-start(bf16[8,16,32,16]{1,3,0,2:T(8,128)(2,1)S(1)} %copy.193) | copy-start | bytes 393220
  205.0 6.1 %copy-start.22 = (bf16[16,512]{0,1:T(8,128)(2,1)S(1)}, bf16[16,512]{0,1:T(8,128)(2,1)}, u32[]{:S(2)}) copy-start(bf16[16,512]{0,1:T(8,128)(2,1)} %get-tuple-element.169) | copy-start | bytes 49156
  211.1 1.9 copy-start.28
  211.1 4.3 copy-start.3
  211.1 4.3 copy-start.14
  213.0 1.9 copy-start.19
  213.0 2.5 copy-start.1
  213.0 2.6 copy-start.2
  214.9 1.8 copy-start
  219.2 1.6 copy-start.48
  219.2 1.9 copy-start.42
  220.7 2.4 copy-start.44
  223.0 2.1 copy-start.33
  224.2 2.7 copy-start.31
  227.0 1.9 copy-start.29
  228.9 2.1 copy-start.27
  231.0 1.9 copy-start.25
  232.9 2.0 copy-start.23
  234.9 2.0 copy-start.21
  241.3 161.3 %reduce-scatter.7.cloned.1.call-start = ((), (), s32[]{:S(2)}) async-start(), calls=%async_computation.4 | async-start | bytes 589824 | tf_op jit(solution)/shard_map/reduce_scatter | solution.py:141
  306.3 5.3 copy-start.36
  312.3 5.2 copy-start.37
  313.6 4.0 copy-start.38
  323.2 5.8 %collective-permute-start.2 = (bf16[17,1,512]{2,1,0:T(2,128)(2,1)S(1)}, bf16[17,1,512]{2,1,0:T(2,128)(2,1)S(1)}, u32[]{:S(2)}, u32[]{:S(2)}) collective-permute-start(bf16[17,1,512]{2,1,0:T(2,128)(2,1)S(1)} %slice.649), channel_id=1, source_target_pairs={{1,0},{2,1},{3,2},{4,3},{5,4},{6,5},{7,6},{9,8},{10,9},{11,10},{12... | collective-permute-start | bytes 52232 | tf_op jit(solution)/shard_map/ppermute | solution.py:13
  331.9 6.5 %copy-start.59 = (bf16[16,32,256]{2,1,0:T(8,128)(2,1)S(1)}, bf16[16,32,256]{2,1,0:T(8,128)(2,1)}, u32[]{:S(2)}) copy-start(bf16[16,32,256]{2,1,0:T(8,128)(2,1)} %param.30) | copy-start | bytes 786436
  331.9 3.2 collective-permute-start.3
  339.6 1.7 copy-start.13
  339.6 128.9 %reduce-scatter.9.cloned.1.call-start = ((), (), s32[]{:S(2)}) async-start(), calls=%async_computation.5 | async-start | bytes 1179648 | tf_op jit(solution)/shard_map/reduce_scatter | solution.py:143
  340.4 2.5 copy-start.16
  342.1 2.5 copy-start.9
  343.7 2.5 copy-start.35
  343.7 2.5 copy-start.45
  345.4 2.4 copy-start.5
  347.6 185.4 %reduce-scatter.13.cloned.1.call-start = ((), (), s32[]{:S(2)}) async-start(), calls=%async_computation.7 | async-start | bytes 589824
  348.6 3.7 copy-start.10
  351.5 2.5 copy-start.7
  353.1 2.0 copy-start.12
  354.8 1.4 copy-start.55
  354.9 1.3 copy-start.53
  354.9 1.4 copy-start.52
  354.9 1.4 copy-start.51
  354.9 1.4 copy-start.50
  354.9 1.4 copy-start.49
  355.1 2.3 copy-start.43
  355.9 1.7 copy-start.18
  355.9 1.9 copy-start.40
  357.4 209.3 %all-reduce.4.cloned.1.call-start = ((), (), s32[]{:S(2)}) async-start(), calls=%async_computation.8 | async-start | bytes 524288 | tf_op jit(solution)/shard_map/psum | solution.py:146
  (5 other events, 5.9 us)
Sparse Core Ops, SparseCore 0:
  241.4 62.2 reduce-scatter.10
  339.7 62.9 reduce-scatter.6
  406.1 62.3 reduce-scatter.8
  472.1 60.8 reduce-scatter.12
  535.4 31.2 all-reduce.3
where the time goes:
time: 586 us; the launch traced here: 578 us
  waiting for transfers between devices  199 us (34%)
  local copies, waits for them, and re-layouts  157 us (27%)
  blocking collectives  141 us (24%)
  matrix products  49.3 us (8%)
  between operations  15 us (3%)
  starting transfers between devices  8.64 us (1%)
  other arithmetic  8.34 us (1%)
    reduce_scatter x1, waiting for transfers between devices, per_device(): lax.psum_scatter(expand_term, 'col', scatter_dimension=1, tiled=True)  65.9 us
    unnamed x6, waiting for transfers between devices  63.4 us
    reduce_scatter x1, waiting for transfers between devices, per_device(): lax.psum_scatter(reduce_term, 'col', scatter_dimension=1, tiled=True)  44.5 us
    reshape x18, local copies, waits for them, and re-layouts, tap_patch(): return patch.reshape(half_rows, half_cols, GROUPS, GW)  37.4 us
    transpose x9, local copies, waits for them, and re-layouts, per_device(): jnp.transpose(backed, (1, 2, 0, 3)).reshape(half_rows, half_cols, width_mid)  35.8 us
    all_gather x1, blocking collectives, per_device(): lax.all_gather(expand_weight, 'col', axis=1, tiled=True)  33.6 us
    all_gather x1, blocking collectives, per_device(): lax.all_gather(shortcut_weight, 'col', axis=1, tiled=True)  32.8 us
    all_gather x1, blocking collectives, per_device(): lax.all_gather(reduce_weight, 'col', axis=1, tiled=True)  32.7 us
  transfers between devices with their start and end apart: 9, of which 6 were waited for; matrix products, arithmetic and copies ran while one was open for 26% of the time, Pallas kernels for 0%

commit v1 on v0

v1 whole, which is shorter than its diff:
```python
import functools

import jax
import jax.numpy as jnp
from jax import lax
from jax.experimental import pallas as pl
from jax.experimental.pallas import tpu as pltpu
from jax.sharding import PartitionSpec as P

GW = 16
TAPS = 9
HALF = 256
BACK = (4, 5, 3, 7, 1, 8, 2, 6, 0)
F32 = jnp.float32
BF16 = jnp.bfloat16
VMEM_LIMIT = 40 * 1024 * 1024


class Sizes:
    def __init__(self, tile_rows, tile_cols):
        self.tr, self.tc = tile_rows, tile_cols
        self.hr, self.hc = tile_rows // 2, tile_cols // 2
        self.odd = (self.hr + 2) * self.hc
        self.even = (self.hr + 1) * self.hc
        self.band = self.odd + self.even
        self.side = 3 * self.band
        self.pixels = self.side + TAPS * 16
        self.main = self.hr * self.hc
        self.wide = self.main + self.hc
        self.out = self.wide + 16

    def tap(self, tap):
        a, b = divmod(tap, 3)
        return b * self.band + (0, self.odd, self.hc)[a]

    def tap_side(self, tap):
        return self.side + tap * 16

    def planes(self):
        return (
            self.band + self.odd,
            2 * self.band + self.odd,
            self.band + self.hc,
            2 * self.band + self.hc,
        )


def dot(a, b, dims=((1,), (0,))):
    return lax.dot_general(a, b, (dims, ((), ())), preferred_element_type=F32)


def sigmoid(value):
    return 1.0 / (1.0 + jnp.exp(-value))


def place():
    col = lax.axis_index("col")
    return col // 2, lax.rem(col, 2), lax.rem(lax.axis_index("row"), 2)


def gathered_positions(halves):
    h, low, core = place()
    other = 1 - low
    mine = low + core - 2 * low * core
    theirs = 1 - mine
    spots = [2 * h + low, 2 * h + other]
    for j in range(1, halves):
        spots.append(2 * lax.rem(h - j + halves, halves) + mine)
    for j in range(1, halves):
        spots.append(2 * lax.rem(h - j + halves, halves) + theirs)
    return spots


def row_of(sizes, r, north, region, south):
    if r < 0:
        return north[0]
    if r < sizes.tr:
        return region[r]
    return south[r - sizes.tr]


def pack_kernel(sizes, region, north, south, cot, cot_south, to_right, to_left, cols, cots):
    cols[...] = jnp.zeros_like(cols)
    cots[...] = jnp.zeros_like(cots)
    for r in range(-1, sizes.tr + 2):
        source = row_of(sizes, r, north, region, south)
        head = source[:16].astype(F32)
        tail = source[sizes.tc - 16 :].astype(F32)
        cols[0, r + 1 : r + 2] = tail[15:16]
        cols[1, r + 1 : r + 2] = head[0:1]
        cols[2, r + 1 : r + 2] = head[1:2]
    for i in range(sizes.hr + 1):
        source = cot[i] if i < sizes.hr else cot_south[0]
        cots[i : i + 1] = source[:16].astype(F32)[0:1]
    to_right[...] = cols[0].astype(BF16)
    to_left[0:32] = cols[1].astype(BF16)
    to_left[32:64] = cols[2].astype(BF16)
    half = cots.shape[1] // 2
    to_left[64:80] = cots[:, :half].astype(BF16)
    to_left[80:96] = cots[:, half:].astype(BF16)


def spread_kernel(sizes, region, north, south, west, east, x, ext, cols):
    cols[:, :, 32:40] = jnp.zeros((3, cols.shape[1], 8, 128), F32)
    for v in range(ext.shape[0]):
        lanes = slice(v * 128, (v + 1) * 128)
        cols[0, v, 0:32] = west[:, lanes].astype(F32)
        for r in range(-1, sizes.tr + 2):
            source = row_of(sizes, r, north, region, south)[:, lanes].astype(F32)
            ext[v, r + 1, 8 : 8 + sizes.tc] = source
            ext[v, r + 1, 7:8] = cols[0, v, r + 1 : r + 2]
        cols[0, v, 0:32] = jnp.zeros((32, 128), F32)
        for r in range(sizes.tr + 3):
            cols[0, v, r : r + 1] = ext[v, r, 7 + sizes.tc : 8 + sizes.tc]
        cols[1, v, 0:32] = east[0:32, lanes].astype(F32)
        cols[2, v, 0:32] = east[32:64, lanes].astype(F32)
        for b in range(3):
            base = b * sizes.band
            for r in list(range(0, sizes.tr + 3, 2)) + list(range(1, sizes.tr + 3, 2)):
                picked = ext[v, r, pl.ds(7 + b, sizes.hc, stride=2)]
                x[base : base + sizes.hc, lanes] = picked.astype(BF16)
                base += sizes.hc
            for a in range(3):
                at = sizes.tap_side(3 * a + b)
                x[at : at + 16, lanes] = cols[b, v, pl.ds(a, 16, stride=2)].astype(BF16)


def first_kernel(sizes, halves, x, *refs):
    blocks = refs[: 2 * halves]
    hidden, slope_one, hidden_two, slope_two, back, reduce_t = refs[2 * halves : 2 * halves + 6]
    pre, group_t, group, front, pre_two = refs[2 * halves + 6 :]
    shard = blocks[0].shape[0]
    cin = reduce_t.shape[1]
    mid = reduce_t.shape[0]
    for block, spot in zip(blocks, gathered_positions(halves), strict=True):
        rows = pl.ds(pl.multiple_of(spot * shard, shard), shard)
        reduce_t[rows, :] = block[:, :cin]
        group_t[rows, :] = block[:, cin:]
    pre[...] = dot(x[...], reduce_t[...], ((1,), (1,)))
    group[...] = group_t[...].astype(F32).T.astype(BF16)
    row_group = lax.broadcasted_iota(jnp.int32, (HALF, HALF), 0) // GW
    lane_group = lax.broadcasted_iota(jnp.int32, (HALF, HALF), 1) // GW
    mask = jnp.where(row_group == lane_group, 1.0, 0.0).astype(BF16)
    for n in range(mid // HALF):
        for tap in range(TAPS):
            rows = group[tap * GW : (tap + 1) * GW, n * HALF : (n + 1) * HALF]
            dense = jnp.concatenate([rows] * (HALF // GW), axis=0) * mask
            front[n, tap * HALF : (tap + 1) * HALF] = dense
            spot = BACK.index(tap)
            back[n, :, spot * HALF : (spot + 1) * HALF] = dense

    def silu_rows(at, _):
        rows = pl.ds(pl.multiple_of(at * 16, 16), 16)
        value = pre[rows, :]
        hidden[rows, :] = (value * sigmoid(value)).astype(BF16)
        return 0

    def plane_rows(at, start, to):
        source = pl.ds(pl.multiple_of(start + at * 16, 16), 16)
        target = pl.ds(pl.multiple_of(to + at * 16, 16), 16)
        value = pre[source, :]
        sigma = sigmoid(value)
        active = value * sigma
        hidden[source, :] = active.astype(BF16)
        slope_one[target, :] = sigma + active * (1.0 - sigma)

    lax.fori_loop(0, sizes.pixels // 16, silu_rows, 0, unroll=2)
    for i, start in enumerate(sizes.planes()):

        def body(at, _, start=start, to=i * sizes.main):
            plane_rows(at, start, to)
            return 0

        lax.fori_loop(0, sizes.main // 16, body, 0, unroll=2)

    for n in range(mid // HALF):
        lanes = slice(n * HALF, (n + 1) * HALF)
        patches = []
        for tap in range(TAPS):
            at, side = sizes.tap(tap), sizes.tap_side(tap)
            patches.append(
                jnp.concatenate(
                    [hidden[at : at + sizes.wide, lanes], hidden[side : side + 16, lanes]], axis=0
                )
            )
        pre_two[:, lanes] = dot(jnp.concatenate(patches, axis=1), front[n])
    value = pre_two[...]
    sigma = sigmoid(value)
    active = value * sigma
    hidden_two[...] = active.astype(BF16)
    slope_two[...] = sigma + active * (1.0 - sigma)


def split_out(halves, total, shard, keeps, give):
    h, low, core = place()
    keep = low + core - 2 * low * core
    for j in range(halves):
        base = 2 * lax.rem(h + j, halves)
        mine = pl.ds(pl.multiple_of((base + keep) * shard, shard), shard)
        theirs = pl.ds(pl.multiple_of((base + 1 - keep) * shard, shard), shard)
        keeps[j][...] = total[mine, :]
        give[j] = total[theirs, :].astype(BF16)


def second_kernel(sizes, halves, x, hidden_two, slope_two, cot, cot_south, east, *refs):
    blocks = refs[: 2 * halves]
    refs = refs[2 * halves :]
    block_out, grad_two, grad_side, short_back, give = refs[:5]
    keeps = refs[5 : 5 + halves]
    expand_t, short_t, total, shift = refs[5 + halves :]
    shard = blocks[0].shape[0]
    mid = expand_t.shape[1]
    width = expand_t.shape[0]
    for block, spot in zip(blocks, gathered_positions(halves), strict=True):
        rows = pl.ds(pl.multiple_of(spot * shard, shard), shard)
        expand_t[rows, :] = block[:, :mid]
        short_t[rows, :] = block[:, mid:]
    at, side = sizes.tap(4), sizes.tap_side(4)
    strided = jnp.concatenate([x[at : at + sizes.wide], x[side : side + 16]], axis=0)
    summed = dot(hidden_two[...], expand_t[...], ((1,), (1,))) + dot(
        strided, short_t[...], ((1,), (1,))
    )
    sigma = sigmoid(summed)
    active = summed * sigma
    block_out[...] = (
        active[: sizes.main].astype(BF16).reshape(sizes.hr, sizes.hc, width)
    )
    cotangent = jnp.concatenate(
        [
            cot[...].reshape(sizes.main, width),
            cot_south[...].reshape(sizes.hc, width),
            jnp.concatenate([east[64:80], east[80:96]], axis=1),
        ],
        axis=0,
    )
    grad_sum = (cotangent.astype(F32) * (sigma + active * (1.0 - sigma))).astype(BF16)
    own = grad_sum[: sizes.main]
    flipped = own.astype(F32).T.astype(BF16)
    total[:, :mid] = dot(flipped, hidden_two[: sizes.main])
    total[:, mid:] = dot(flipped, strided[: sizes.main])
    split_out(halves, total, shard, keeps, give)
    short_back[...] = dot(own, short_t[...])
    back = dot(grad_sum, expand_t[...]) * slope_two[...]
    grad_two[...] = back[: sizes.wide].astype(BF16)
    for i in range(sizes.hr + 1):
        shift[i, : sizes.hc] = back[i * sizes.hc : (i + 1) * sizes.hc]
        shift[i, sizes.hc : sizes.hc + 1] = back[sizes.wide + i : sizes.wide + i + 1]
    for i in range(sizes.hr + 1):
        grad_side[i * sizes.hc : (i + 1) * sizes.hc] = shift[i, 1 : sizes.hc + 1].astype(BF16)


def third_kernel(
    sizes, halves, x, hidden, slope_one, back, reduce_t, grad_two, grad_side, short_back, *refs
):
    region_grad, give = refs[:2]
    keeps = refs[2 : 2 + halves]
    total, grad_one, planes, spread_out = refs[2 + halves :]
    mid, cin = reduce_t.shape
    main, hc = sizes.main, sizes.hc
    shard = keeps[0].shape[0]
    down = slice(hc, hc + main)
    own = slice(0, main)
    for n in range(mid // HALF):
        lanes = slice(n * HALF, (n + 1) * HALF)
        two, low = grad_two[own, lanes], grad_two[down, lanes]
        side, corner = grad_side[own, lanes], grad_side[down, lanes]
        first = 0
        for i, parts in enumerate(((two,), (two, side), (two, low), (two, low, side, corner))):
            left = jnp.concatenate(parts, axis=1)
            last = first + len(parts) * HALF
            spread = dot(left, back[n, :, first:last], ((1,), (1,)))
            first = last
            rows = slice(i * main, (i + 1) * main)
            grad_one[rows, lanes] = (spread * slope_one[rows, lanes]).astype(BF16)
    flat = jnp.concatenate([x[at : at + main] for at in sizes.planes()], axis=0)
    total[:, :cin] = dot(grad_one[...].astype(F32).T.astype(BF16), flat)
    flipped = grad_two[own, :].astype(F32).T.astype(BF16)
    lane = lax.broadcasted_iota(jnp.int32, (GW, 128), 1) // GW
    for n in range(mid // HALF):
        lanes = slice(n * HALF, (n + 1) * HALF)
        sums = [jnp.zeros((GW, 128), F32)] * (HALF // GW)
        for tap in range(TAPS):
            at = sizes.tap(tap)
            piece = dot(flipped[n * HALF : (n + 1) * HALF], hidden[at : at + main, lanes])
            for q in range(HALF // GW):
                tile = q // 8
                block = piece[q * GW : (q + 1) * GW, tile * 128 : (tile + 1) * 128]
                block = pltpu.roll(block, (GW * (tap - q)) % 128, 1)
                if tap < 8:
                    sums[q] = jnp.where(lane == tap, block, sums[q])
                else:
                    rows = slice(n * HALF + q * GW, n * HALF + (q + 1) * GW)
                    total[rows, cin : cin + 128] = sums[q]
                    total[rows, cin + 128 : cin + 256] = jnp.where(lane == 0, block, 0.0)
    split_out(halves, total, shard, keeps, give)
    planes[...] = dot(grad_one[...], reduce_t[...])
    planes[:main] += short_back[...]
    for i in range(4):
        for r in range(sizes.hr):
            at = i * main + r * hc
            for v in range(cin // 128):
                lanes = slice(v * 128, (v + 1) * 128)
                spread_out[v, 2 * r + i // 2, pl.ds(i % 2, hc, stride=2)] = planes[at : at + hc, lanes]
    for v in range(cin // 128):
        region_grad[:, :, v * 128 : (v + 1) * 128] = spread_out[v].astype(BF16)


def call(kernel, out_shape, scratch, *operands, flops=0):
    sizes = sum(o.size * o.dtype.itemsize for o in operands)
    sizes += sum(o.size * o.dtype.itemsize for o in jax.tree.leaves(out_shape))
    return pl.pallas_call(
        kernel,
        out_shape=out_shape,
        in_specs=[pl.BlockSpec(memory_space=pltpu.VMEM)] * len(operands),
        out_specs=jax.tree.map(lambda _: pl.BlockSpec(memory_space=pltpu.VMEM), out_shape),
        scratch_shapes=scratch,
        compiler_params=pltpu.CompilerParams(vmem_limit_bytes=VMEM_LIMIT),
        cost_estimate=pl.CostEstimate(flops=flops, bytes_accessed=sizes, transcendentals=0),
    )(*operands)


def both(rows, cols, target):
    pairs = []
    for r in range(rows):
        for c in range(cols):
            to = target(r % 2, c // 2, c % 2)
            if to is not None:
                pairs.append((r * cols + c, r * cols + 2 * to[0] + to[1]))
    return pairs


def shifted(x, axis, by):
    devices = lax.axis_size(axis)
    pairs = [(i, i + by) for i in range(devices) if 0 <= i + by < devices]
    return lax.ppermute(x, axis, pairs)


def core_swap(x):
    return lax.ppermute(x, "row", [(r, r ^ 1) for r in range(lax.axis_size("row"))])


def gather(message):
    rows, cols = lax.axis_size("row"), lax.axis_size("col")
    halves = cols // 2
    far = {}
    for j in range(halves - 1, 0, -1):
        pairs = both(rows, cols, lambda k, h, low: ((h + j) % halves, low ^ k))
        far[j] = lax.ppermute(message, ("row", "col"), pairs)
    beside = lax.ppermute(message, "col", [(c, c ^ 1) for c in range(cols)])
    order = range(1, halves)
    return [message, beside] + [far[j] for j in order] + [core_swap(far[j]) for j in order]


def reduce(keeps, give):
    rows, cols = lax.axis_size("row"), lax.axis_size("col")
    halves = cols // 2
    core = lax.axis_index("row") % 2
    other = core_swap(give)
    sums = [keeps[j] + other[j].astype(F32) for j in range(halves)]
    total = None
    for j in range(halves - 1, -1, -1):
        pairs = both(
            rows, cols, lambda k, h, low: None if j == k == 0 else ((h + j) % halves, low ^ k)
        )
        came = lax.ppermute(sums[j].astype(BF16), ("row", "col"), pairs).astype(F32)
        if j == 0:
            came = jnp.where(core == 0, sums[0], came)
        total = came if total is None else total + came
    if rows != 4:
        return lax.psum(total, "row")
    total = total + core_swap(total)
    total = total.astype(BF16)
    across = lax.ppermute(total, "row", [(r, r ^ 2) for r in range(4)])
    return total.astype(F32) + across.astype(F32)


def per_device(region, reduce_weight, group_weight, expand_weight, shortcut_weight, cotangent):
    tile_rows, tile_cols, cin = region.shape
    sizes = Sizes(tile_rows, tile_cols)
    halves = lax.axis_size("col") // 2
    mid, shard = expand_weight.shape
    width = shard * lax.axis_size("col")
    taps = group_weight.shape[0]
    pad = jnp.zeros((shard, 256 - taps), BF16)
    early = jnp.concatenate([reduce_weight.T, group_weight.T, pad], axis=1)
    late = jnp.concatenate([expand_weight.T, shortcut_weight.T], axis=1)
    early_blocks = gather(early)
    north = shifted(region[-1:], "row", 1)
    south = shifted(region[:2], "row", -1)
    cot_south = shifted(cotangent[:1], "row", -1)
    late_blocks = gather(late)

    def shape(dims, dtype=BF16):
        return jax.ShapeDtypeStruct(dims, dtype)

    to_right, to_left = call(
        functools.partial(pack_kernel, sizes),
        (shape((32, cin)), shape((96, cin))),
        [pltpu.VMEM((3, 32, cin), F32), pltpu.VMEM((16, width), F32)],
        region, north, south, cotangent, cot_south,
    )
    west = shifted(to_right, "col", 1)
    east = shifted(to_left, "col", -1)
    x = call(
        functools.partial(spread_kernel, sizes),
        shape((sizes.pixels, cin)),
        [
            pltpu.VMEM((cin // 128, tile_rows + 3, 8 + tile_cols, 128), F32),
            pltpu.VMEM((3, cin // 128, 40, 128), F32),
        ],
        region, north, south, west, east,
    )
    hidden, slope_one, hidden_two, slope_two, back, reduce_t = call(
        functools.partial(first_kernel, sizes, halves),
        (
            shape((sizes.pixels, mid)),
            shape((4 * sizes.main, mid), F32),
            shape((sizes.out, mid)),
            shape((sizes.out, mid), F32),
            shape((mid // HALF, HALF, TAPS * HALF)),
            shape((mid, cin)),
        ),
        [
            pltpu.VMEM((sizes.pixels, mid), F32),
            pltpu.VMEM((mid, 256), BF16),
            pltpu.VMEM((256, mid), BF16),
            pltpu.VMEM((mid // HALF, TAPS * HALF, HALF), BF16),
            pltpu.VMEM((sizes.out, mid), F32),
        ],
        x, *early_blocks,
        flops=2 * sizes.pixels * cin * mid + 2 * sizes.out * TAPS * HALF * mid,
    )
    block_out, grad_two, grad_side, short_back, give, *keeps = call(
        functools.partial(second_kernel, sizes, halves),
        (
            shape((sizes.hr, sizes.hc, width)),
            shape((sizes.wide, mid)),
            shape((sizes.wide, mid)),
            shape((sizes.main, cin), F32),
            shape((halves, shard, mid + cin)),
        )
        + (shape((shard, mid + cin), F32),) * halves,
        [
            pltpu.VMEM((width, mid), BF16),
            pltpu.VMEM((width, cin), BF16),
            pltpu.VMEM((width, mid + cin), F32),
            pltpu.VMEM((sizes.hr + 1, 24, mid), F32),
        ],
        x, hidden_two, slope_two, cotangent, cot_south, east, *late_blocks,
        flops=6 * sizes.out * width * (mid + cin),
    )
    late_sum = reduce(keeps, give)
    region_grad, give, *keeps = call(
        functools.partial(third_kernel, sizes, halves),
        (shape(region.shape), shape((halves, shard, cin + 256)))
        + (shape((shard, cin + 256), F32),) * halves,
        [
            pltpu.VMEM((mid, cin + 256), F32),
            pltpu.VMEM((4 * sizes.main, mid), BF16),
            pltpu.VMEM((4 * sizes.main, cin), F32),
            pltpu.VMEM((cin // 128, tile_rows, tile_cols, 128), F32),
        ],
        x, hidden, slope_one, back, reduce_t, grad_two, grad_side, short_back,
        flops=4 * 4 * sizes.main * cin * mid + 4 * sizes.main * TAPS * HALF * mid,
    )
    early_sum = reduce(keeps, give)
    return (
        block_out,
        region_grad,
        early_sum[:, :cin].T,
        early_sum[:, cin : cin + taps].T,
        late_sum[:, :mid].T,
        late_sum[:, mid:].T,
    )


def solution(mesh):
    tiles, split = P("row", "col", None), P(None, "col")
    return jax.shard_map(
        per_device,
        mesh=mesh,
        in_specs=(tiles, split, split, split, split, tiles),
        out_specs=(tiles, tiles, split, split, split, split),
        check_vma=False,
    )
```

time: 586 us -> 82.4 us (0.14); the launches traced: 578 us -> 81.9 us
  waiting for transfers between devices: 199 us -> 19.5 us
  local copies, waits for them, and re-layouts: 157 us -> 6.75 us
  blocking collectives: 141 us -> 0 us
  matrix products: 49.3 us -> 0 us
  starting transfers between devices: 8.64 us -> 44.9 us
  between operations: 15 us -> 0.87 us
  Pallas kernels: 0 us -> 7.88 us
  other arithmetic: 8.34 us -> 2 us
    all_gather x4 -> x0, blocking collectives: 130 us -> none  [the longest x1 33.6 us: per_device(): lax.all_gather(expand_weight, 'col', axis=1, tiled=True)]
    reduce_scatter x3 -> x0, waiting for transfers between devices: 110 us -> none  [the longest x1 65.9 us: per_device(): lax.psum_scatter(expand_term, 'col', scatter_dimension=1, tiled=True)]
    unnamed x6 -> x0, waiting for transfers between devices: 63.4 us -> none
    dot_general x36 -> x0, matrix products: 49.3 us -> none  [the longest x9 16.2 us: per_device(): lax.dot_general(grad_two, kernels[offset], (((3,), (2,)), ((2,), (1,))),...]
    reshape x30 -> x0, local copies, waits for them, and re-layouts: 47.6 us -> none  [the longest x18 37.4 us: tap_patch(): return patch.reshape(half_rows, half_cols, GROUPS, GW)]
    ppermute x0 -> x28, starting transfers between devices: none -> 35.6 us  [the longest x6 14.5 us: gather(): far[j] = lax.ppermute(message, ('row', 'col'), pairs)]
    transpose x18 -> x4, local copies, waits for them, and re-layouts: 36.7 us -> 2.57 us  [the longest x1 0.66 us: per_device(): late_sum[:, :mid]]
    another operation x7 -> x0, local copies, waits for them, and re-layouts: 25.2 us -> none
  transfers between devices with their start and end apart: 9 -> 33, of which waited for: 6 -> 8; matrix products, arithmetic and copies ran while one was open for 26% -> 6% of each run, Pallas kernels for 0% -> 4%
where the time goes in v1:
time: 82.4 us; the launch traced here: 81.9 us
  starting transfers between devices  44.9 us (54%)
  waiting for transfers between devices  19.5 us (24%)
  Pallas kernels  7.88 us (10%)
  local copies, waits for them, and re-layouts  6.75 us (8%)
  other arithmetic  2 us (2%)
  between operations  0.87 us (1%)
    ppermute x6, starting transfers between devices, gather(): far[j] = lax.ppermute(message, ('row', 'col'), pairs)  14.5 us
    ppermute x8, waiting for transfers between devices, reduce(): came = lax.ppermute(sums[j].astype(BF16), ('row', 'col'), pairs).astype(F32)  12.4 us
    ppermute x8, starting transfers between devices, reduce(): came = lax.ppermute(sums[j].astype(BF16), ('row', 'col'), pairs).astype(F32)  9.96 us
    ppermute x5, starting transfers between devices, shifted(): return lax.ppermute(x, axis, pairs)  9.27 us
    pallas_call x5, Pallas kernels, call(): pl.pallas_call(kernel, out_shape=out_shape, in_specs=[pl.BlockSpec(memory...  7.88 us
    ppermute x10, starting transfers between devices, core_swap(): lax.ppermute(x, 'row', [(r, r ^ 1) for r in range(lax.axis_size('row'))])  4.44 us
    ppermute x2, starting transfers between devices, gather(): beside = lax.ppermute(message, 'col', [(c, c ^ 1) for c in range(cols)])  3.74 us
    ppermute x2, starting transfers between devices, reduce(): across = lax.ppermute(total, 'row', [(r, r ^ 2) for r in range(4)])  2.95 us
  transfers between devices with their start and end apart: 33, of which 8 were waited for; matrix products, arithmetic and copies ran while one was open for 6% of the time, Pallas kernels for 4%

profile of v1, /device:TPU:0, one launch (start us, length us, event | category | flops | bytes accessed | tf_op | source)
XLA Modules:
  0.0 81.9 jit_solution(17108595866101093300)
XLA Ops:
  0.6 0.0 copy-start.2
  0.6 0.8 slice.46
  1.4 1.3 %collective-permute-start.1 = (bf16[2,32,256]{2,1,0:T(8,128)(2,1)S(1)}, bf16[2,32,256]{2,1,0:T(8,128)(2,1)S(1)}, u32[]{:S(2)}, u32[]{:S(2)}) collective-permute-start(bf16[2,32,256]{2,1,0:T(8,128)(2,1)S(1)} %slice.46), channel_id=1, source_target_pairs={{8,0},{16,8},{24,16},{9,1},{17,9},{25,17},{10,2},{18,10},{26,18},{... | collective-permute-start | bytes 98312 | tf_op jit(solution)/shard_map/ppermute | solution.py:335
  2.7 0.7 slice.45
  3.5 3.0 %collective-permute-start = (bf16[1,32,256]{2,1,0:T(8,128)(2,1)S(1)}, bf16[1,32,256]{2,1,0:T(8,128)(2,1)S(1)}, u32[]{:S(2)}, u32[]{:S(2)}) collective-permute-start(bf16[1,32,256]{2,1,0:T(8,128)(2,1)S(1)} %slice.45), channel_id=1, source_target_pairs={{0,8},{8,16},{16,24},{1,9},{9,17},{17,25},{2,10},{10,18},{18,26},{... | collective-permute-start | bytes 49160 | tf_op jit(solution)/shard_map/ppermute | solution.py:335
  6.5 0.7 slice.47
  7.2 1.3 %collective-permute-start.2 = (bf16[1,16,512]{2,1,0:T(8,128)(2,1)S(1)}, bf16[1,16,512]{2,1,0:T(8,128)(2,1)S(1)}, u32[]{:S(2)}, u32[]{:S(2)}) collective-permute-start(bf16[1,16,512]{2,1,0:T(8,128)(2,1)S(1)} %slice.47), channel_id=1, source_target_pairs={{8,0},{16,8},{24,16},{9,1},{17,9},{25,17},{10,2},{18,10},{26,18},{... | collective-permute-start | bytes 49160 | tf_op jit(solution)/shard_map/ppermute | solution.py:335
  8.5 0.1 pad.4.clone
  8.6 0.8 maximum_maximum_fusion.refs_0_
  9.4 4.1 %collective-permute-start.7 = (bf16[64,512]{1,0:T(8,128)(2,1)S(1)}, bf16[64,512]{1,0:T(8,128)(2,1)S(1)}, u32[]{:S(2)}, u32[]{:S(2)}) collective-permute-start(bf16[64,512]{1,0:T(8,128)(2,1)S(1)} %maximum_maximum_fusion.refs_0_), channel_id=1, source_target_pairs={{0,4},{1,5},{2,6},{3,7},{4,0},{5,1},{6,2},{7,3},{8,13},{9,12},{10,... | collective-permute-start | bytes 196616 | tf_op jit(solution)/shard_map/ppermute | solution.py:348
  13.5 1.3 %collective-permute-start.8 = (bf16[64,512]{1,0:T(8,128)(2,1)S(1)}, bf16[64,512]{1,0:T(8,128)(2,1)S(1)}, u32[]{:S(2)}, u32[]{:S(2)}) collective-permute-start(bf16[64,512]{1,0:T(8,128)(2,1)S(1)} %maximum_maximum_fusion.refs_0_), channel_id=1, source_target_pairs={{0,6},{1,7},{2,0},{3,1},{4,2},{5,3},{6,4},{7,5},{8,15},{9,14},{10,... | collective-permute-start | bytes 196616 | tf_op jit(solution)/shard_map/ppermute | solution.py:348
  14.8 0.7 collective-permute-start.6
  15.5 1.5 %collective-permute-start.5 = (bf16[64,512]{1,0:T(8,128)(2,1)S(1)}, bf16[64,512]{1,0:T(8,128)(2,1)S(1)}, u32[]{:S(2)}, u32[]{:S(2)}) collective-permute-start(bf16[64,512]{1,0:T(8,128)(2,1)S(1)} %maximum_maximum_fusion.refs_0_), channel_id=1, source_target_pairs={{0,1},{1,0},{2,3},{3,2},{4,5},{5,4},{6,7},{7,6},{8,9},{9,8},{10,11... | collective-permute-start | bytes 196616 | tf_op jit(solution)/shard_map/ppermute | solution.py:349
  17.0 0.0 collective-permute-done.1.south
  17.0 0.9 %copy-done = bf16[16,32,256]{2,1,0:T(8,128)(2,1)S(1)} copy-done((bf16[16,32,256]{2,1,0:T(8,128)(2,1)S(1)}, bf16[16,32,256]{2,1,0:T(8,128)(2,1)}, u32[]{:S(2)}) %copy-start) | copy-done | bytes 262168
  18.0 0.9 %copy-done.1 = bf16[8,16,512]{2,1,0:T(8,128)(2,1)S(1)} copy-done((bf16[8,16,512]{2,1,0:T(8,128)(2,1)S(1)}, bf16[8,16,512]{2,1,0:T(8,128)(2,1)}, u32[]{:S(2)}) %copy-start.1) | copy-done | bytes 131096
  18.9 0.1 shard_map.109
  18.9 2.4 %collective-permute-start.3 = (bf16[32,256]{1,0:T(8,128)(2,1)S(1)}, bf16[32,256]{1,0:T(8,128)(2,1)S(1)}, u32[]{:S(2)}, u32[]{:S(2)}) collective-permute-start(bf16[32,256]{1,0:T(8,128)(2,1)S(1)} %get-tuple-element.29), channel_id=1, source_target_pairs={{0,1},{1,2},{2,3},{3,4},{4,5},{5,6},{6,7},{8,9},{9,10},{10,11},{11... | collective-permute-start | bytes 49160 | tf_op jit(solution)/shard_map/ppermute | solution.py:335
  21.4 0.9 %pad_maximum_fusion.refs_0_ = bf16[64,768]{1,0:T(8,128)(2,1)S(1)} fusion(bf16[64,256]{1,0:T(8,128)(2,1)} %bitcast.59, bf16[64,512]{1,0:T(8,128)(2,1)} %bitcast.56), kind=kLoop, calls=%fused_computation.26 | loop fusion | flops 196608 | bytes 196608 | tf_op jit(solution)/shard_map/concatenate | solution.py:386
  22.2 0.6 collective-permute-done.3.west
  22.8 4.3 %collective-permute-start.13 = (bf16[64,768]{1,0:T(8,128)(2,1)S(1)}, bf16[64,768]{1,0:T(8,128)(2,1)S(1)}, u32[]{:S(2)}, u32[]{:S(2)}) collective-permute-start(bf16[64,768]{1,0:T(8,128)(2,1)S(1)} %pad_maximum_fusion.refs_0_), channel_id=1, source_target_pairs={{0,2},{1,3},{2,4},{3,5},{4,6},{5,7},{6,0},{7,1},{8,11},{9,10},{10,... | collective-permute-start | bytes 294920 | tf_op jit(solution)/shard_map/ppermute | solution.py:348
  27.1 0.0 collective-permute-done.7.refs_3_
  27.1 1.3 %collective-permute-start.4 = (bf16[96,256]{1,0:T(8,128)(2,1)S(1)}, bf16[96,256]{1,0:T(8,128)(2,1)S(1)}, u32[]{:S(2)}, u32[]{:S(2)}) collective-permute-start(bf16[96,256]{1,0:T(8,128)(2,1)S(1)} %get-tuple-element.30), channel_id=1, source_target_pairs={{1,0},{2,1},{3,2},{4,3},{5,4},{6,5},{7,6},{9,8},{10,9},{11,10},{12... | collective-permute-start | bytes 147464 | tf_op jit(solution)/shard_map/ppermute | solution.py:335
  28.4 2.8 %collective-permute-start.14 = (bf16[64,768]{1,0:T(8,128)(2,1)S(1)}, bf16[64,768]{1,0:T(8,128)(2,1)S(1)}, u32[]{:S(2)}, u32[]{:S(2)}) collective-permute-start(bf16[64,768]{1,0:T(8,128)(2,1)S(1)} %pad_maximum_fusion.refs_0_), channel_id=1, source_target_pairs={{0,4},{1,5},{2,6},{3,7},{4,0},{5,1},{6,2},{7,3},{8,13},{9,12},{10,... | collective-permute-start | bytes 294920 | tf_op jit(solution)/shard_map/ppermute | solution.py:348
  31.2 1.3 %collective-permute-start.15 = (bf16[64,768]{1,0:T(8,128)(2,1)S(1)}, bf16[64,768]{1,0:T(8,128)(2,1)S(1)}, u32[]{:S(2)}, u32[]{:S(2)}) collective-permute-start(bf16[64,768]{1,0:T(8,128)(2,1)S(1)} %pad_maximum_fusion.refs_0_), channel_id=1, source_target_pairs={{0,6},{1,7},{2,0},{3,1},{4,2},{5,3},{6,4},{7,5},{8,15},{9,14},{10,... | collective-permute-start | bytes 294920 | tf_op jit(solution)/shard_map/ppermute | solution.py:348
  32.5 0.0 collective-permute-done.5.refs_1_
  32.5 1.9 %collective-permute-start.10 = (bf16[64,512]{1,0:T(8,128)(2,1)S(1)}, bf16[64,512]{1,0:T(8,128)(2,1)S(1)}, u32[]{:S(2)}, u32[]{:S(2)}) collective-permute-start(bf16[64,512]{1,0:T(8,128)(2,1)S(1)} %collective-permute-done.7.refs_3_), channel_id=1, source_target_pairs={{0,8},{8,0},{16,24},{24,16},{1,9},{9,1},{17,25},{25,17},{2,10},{10... | collective-permute-start | bytes 196616 | tf_op jit(solution)/shard_map/ppermute | solution.py:339
  34.4 0.0 collective-permute-done.4.east
  34.4 0.1 collective-permute-start.11
  34.5 0.4 collective-permute-start.9
  34.9 2.0 %collective-permute-done.14.refs_3_ = bf16[64,768]{1,0:T(8,128)(2,1)S(1)} collective-permute-done((bf16[64,768]{1,0:T(8,128)(2,1)S(1)}, bf16[64,768]{1,0:T(8,128)(2,1)S(1)}, u32[]{:S(2)}, u32[]{:S(2)}) %collective-permute-start.14) | collective-permute-done | bytes 98336 | tf_op jit(solution)/shard_map/ppermute | solution.py:348
  37.0 2.2 %collective-permute-start.12 = (bf16[64,768]{1,0:T(8,128)(2,1)S(1)}, bf16[64,768]{1,0:T(8,128)(2,1)S(1)}, u32[]{:S(2)}, u32[]{:S(2)}) collective-permute-start(bf16[64,768]{1,0:T(8,128)(2,1)S(1)} %pad_maximum_fusion.refs_0_), channel_id=1, source_target_pairs={{0,1},{1,0},{2,3},{3,2},{4,5},{5,4},{6,7},{7,6},{8,9},{9,8},{10,11... | collective-permute-start | bytes 294920 | tf_op jit(solution)/shard_map/ppermute | solution.py:349
  39.2 0.5 collective-permute-start.17
  39.7 0.1 collective-permute-start.18
  39.8 0.2 shard_map.110.x
  39.9 3.1 %shard_map.111 = (bf16[1056,512]{1,0:T(8,128)(2,1)S(1)}, f32[512,512]{1,0:T(8,128)S(1)}, bf16[160,512]{1,0:T(8,128)(2,1)S(1)}, f32[160,512]{1,0:T(8,128)S(1)}, b...) custom-call(bf16[1056,256]{1,0:T(8,128)(2,1)S(1)} %shard_map.110.x, ...), custom_call_target="tpu_custom_call" | custom-call | flops 654311424 | bytes 6307840 | tf_op jit(solution)/shard_map/pallas_call | solution.py:311
  43.1 1.7 %shard_map.112 = (bf16[8,16,512]{2,1,0:T(8,128)(2,1)}, bf16[144,512]{1,0:T(8,128)(2,1)S(1)}, bf16[144,512]{1,0:T(8,128)(2,1)S(1)}, f32[128,256]{1,0:T(8,128)S(1)...) custom-call(bf16[1056,256]{1,0:T(8,128)(2,1)S(1)} %shard_map.110.x, ...), custom_call_target="tpu_custom_call" | custom-call | flops 377487360 | bytes 3751936 | tf_op jit(solution)/shard_map/pallas_call | solution.py:311
  44.8 2.8 %shard_map.113 = (bf16[16,32,256]{2,1,0:T(8,128)(2,1)}, bf16[4,64,512]{2,1,0:T(8,128)(2,1)S(1)}, f32[64,512]{1,0:T(8,128)S(1)}, f32[64,512]{1,0:T(8,128)S(1)}, f...) custom-call(bf16[1056,256]{1,0:T(8,128)(2,1)S(1)} %shard_map.110.x, bf16[1056,512]{1,0:T(8,128)(2,1)S(1)} %get-tuple-element.34.hidden, ...), custom_call_target="tpu_custom_call" | custom-call | flops 872415232 | bytes 6766592 | tf_op jit(solution)/shard_map/pallas_call | solution.py:311
  47.7 0.5 collective-permute-start.19
  48.1 0.1 collective-permute-start.26
  48.2 1.1 %collective-permute-done.19 = bf16[4,64,512]{2,1,0:T(8,128)(2,1)S(1)} collective-permute-done((bf16[4,64,512]{2,1,0:T(8,128)(2,1)S(1)}, bf16[4,64,512]{2,1,0:T(8,128)(2,1)S(1)}, u32[]{:S(2)}, u32[]{:S(2)}) %collective-permute-start.19) | collective-permute-done | bytes 262176 | tf_op jit(solution)/shard_map/ppermute | solution.py:339
  49.3 0.1 fusion.6
  49.4 4.3 %collective-permute-start.20 = (bf16[64,512]{1,0:T(8,128)(2,1)S(1)}, bf16[64,512]{1,0:T(8,128)(2,1)S(1)}, u32[]{:S(2)}, u32[]{:S(2)}) collective-permute-start(bf16[64,512]{1,0:T(8,128)(2,1)S(1)} %get-tuple-element.56), channel_id=1, source_target_pairs={{0,6},{1,7},{2,0},{3,1},{4,2},{5,3},{6,4},{7,5},{8,15},{9,14},{10,... | collective-permute-start | bytes 196616 | tf_op jit(solution)/shard_map/ppermute | solution.py:365
  53.6 0.6 collective-permute-start.22
  54.2 0.7 collective-permute-start.23
  54.9 1.2 %collective-permute-done.20 = bf16[64,512]{1,0:T(8,128)(2,1)S(1)} collective-permute-done((bf16[64,512]{1,0:T(8,128)(2,1)S(1)}, bf16[64,512]{1,0:T(8,128)(2,1)S(1)}, u32[]{:S(2)}, u32[]{:S(2)}) %collective-permute-start.20) | collective-permute-done | bytes 65568 | tf_op jit(solution)/shard_map/ppermute | solution.py:365
  56.1 4.5 %collective-permute-done.21 = bf16[64,512]{1,0:T(8,128)(2,1)S(1)} collective-permute-done((bf16[64,512]{1,0:T(8,128)(2,1)S(1)}, bf16[64,512]{1,0:T(8,128)(2,1)S(1)}, u32[]{:S(2)}, u32[]{:S(2)}) %collective-permute-start.21) | collective-permute-done | bytes 65568 | tf_op jit(solution)/shard_map/ppermute | solution.py:365
  60.7 0.6 collective-permute-start.24
  61.3 0.1 fusion.2
  61.4 1.8 %collective-permute-start.27 = (bf16[64,768]{1,0:T(8,128)(2,1)S(1)}, bf16[64,768]{1,0:T(8,128)(2,1)S(1)}, u32[]{:S(2)}, u32[]{:S(2)}) collective-permute-start(bf16[64,768]{1,0:T(8,128)(2,1)S(1)} %get-tuple-element.52), channel_id=1, source_target_pairs={{0,6},{1,7},{2,0},{3,1},{4,2},{5,3},{6,4},{7,5},{8,15},{9,14},{10,... | collective-permute-start | bytes 294920 | tf_op jit(solution)/shard_map/ppermute | solution.py:365
  63.2 1.5 %collective-permute-start.28 = (bf16[64,768]{1,0:T(8,128)(2,1)S(1)}, bf16[64,768]{1,0:T(8,128)(2,1)S(1)}, u32[]{:S(2)}, u32[]{:S(2)}) collective-permute-start(bf16[64,768]{1,0:T(8,128)(2,1)S(1)} %get-tuple-element.55), channel_id=1, source_target_pairs={{0,4},{1,5},{2,6},{3,7},{4,0},{5,1},{6,2},{7,3},{8,13},{9,12},{10,... | collective-permute-start | bytes 294920 | tf_op jit(solution)/shard_map/ppermute | solution.py:365
  64.7 0.4 collective-permute-start.29
  65.1 0.7 collective-permute-start.30
  65.8 1.4 %collective-permute-start.25 = (bf16[64,512]{1,0:T(8,128)(2,1)S(1)}, bf16[64,512]{1,0:T(8,128)(2,1)S(1)}, u32[]{:S(2)}, u32[]{:S(2)}) collective-permute-start(bf16[64,512]{1,0:T(8,128)(2,1)S(1)} %add_convert_fusion.1), channel_id=1, source_target_pairs={{0,16},{8,24},{16,0},{24,8},{1,17},{9,25},{17,1},{25,9},{2,18},{10... | collective-permute-start | bytes 196616 | tf_op jit(solution)/shard_map/ppermute | solution.py:373
  67.2 6.7 %collective-permute-done.28 = bf16[64,768]{1,0:T(8,128)(2,1)S(1)} collective-permute-done((bf16[64,768]{1,0:T(8,128)(2,1)S(1)}, bf16[64,768]{1,0:T(8,128)(2,1)S(1)}, u32[]{:S(2)}, u32[]{:S(2)}) %collective-permute-start.28) | collective-permute-done | bytes 98336 | tf_op jit(solution)/shard_map/ppermute | solution.py:365
  73.9 0.1 select_add_fusion
  74.0 0.3 collective-permute-start.31
  74.4 0.6 slice_bitcast_fusion.6
  75.0 0.5 collective-permute-done.31
  75.5 1.5 %collective-permute-start.32 = (bf16[64,768]{1,0:T(8,128)(2,1)S(1)}, bf16[64,768]{1,0:T(8,128)(2,1)S(1)}, u32[]{:S(2)}, u32[]{:S(2)}) collective-permute-start(bf16[64,768]{1,0:T(8,128)(2,1)S(1)} %add_convert_fusion), channel_id=1, source_target_pairs={{0,16},{8,24},{16,0},{24,8},{1,17},{9,25},{17,1},{25,9},{2,18},{10... | collective-permute-start | bytes 294920 | tf_op jit(solution)/shard_map/ppermute | solution.py:373
  77.1 0.6 slice_bitcast_fusion.7
  77.7 2.9 %collective-permute-done.32 = bf16[64,768]{1,0:T(8,128)(2,1)S(1)} collective-permute-done((bf16[64,768]{1,0:T(8,128)(2,1)S(1)}, bf16[64,768]{1,0:T(8,128)(2,1)S(1)}, u32[]{:S(2)}, u32[]{:S(2)}) %collective-permute-start.32) | collective-permute-done | bytes 98336 | tf_op jit(solution)/shard_map/ppermute | solution.py:373
  80.6 0.7 slice_bitcast_fusion
  81.3 0.6 slice_bitcast_fusion.5
  (32 shorter events, 0.2 us)
Async XLA Ops:
  0.6 42.5 %copy-start.2 = (bf16[8,16,512]{2,1,0:T(8,128)(2,1)S(1)}, bf16[8,16,512]{2,1,0:T(8,128)(2,1)}, u32[]{:S(2)}) copy-start(bf16[8,16,512]{2,1,0:T(8,128)(2,1)} %cot.3) | copy-start | bytes 393220
  1.4 15.6 %collective-permute-start.1 = (bf16[2,32,256]{2,1,0:T(8,128)(2,1)S(1)}, bf16[2,32,256]{2,1,0:T(8,128)(2,1)S(1)}, u32[]{:S(2)}, u32[]{:S(2)}) collective-permute-start(bf16[2,32,256]{2,1,0:T(8,128)(2,1)S(1)} %slice.46), channel_id=1, source_target_pairs={{8,0},{16,8},{24,16},{9,1},{17,9},{25,17},{10,2},{18,10},{26,18},{... | collective-permute-start | bytes 98312 | tf_op jit(solution)/shard_map/ppermute | solution.py:335
  3.5 11.4 %collective-permute-start = (bf16[1,32,256]{2,1,0:T(8,128)(2,1)S(1)}, bf16[1,32,256]{2,1,0:T(8,128)(2,1)S(1)}, u32[]{:S(2)}, u32[]{:S(2)}) collective-permute-start(bf16[1,32,256]{2,1,0:T(8,128)(2,1)S(1)} %slice.45), channel_id=1, source_target_pairs={{0,8},{8,16},{16,24},{1,9},{9,17},{17,25},{2,10},{10,18},{18,26},{... | collective-permute-start | bytes 49160 | tf_op jit(solution)/shard_map/ppermute | solution.py:335
  7.2 8.3 %collective-permute-start.2 = (bf16[1,16,512]{2,1,0:T(8,128)(2,1)S(1)}, bf16[1,16,512]{2,1,0:T(8,128)(2,1)S(1)}, u32[]{:S(2)}, u32[]{:S(2)}) collective-permute-start(bf16[1,16,512]{2,1,0:T(8,128)(2,1)S(1)} %slice.47), channel_id=1, source_target_pairs={{8,0},{16,8},{24,16},{9,1},{17,9},{25,17},{10,2},{18,10},{26,18},{... | collective-permute-start | bytes 49160 | tf_op jit(solution)/shard_map/ppermute | solution.py:335
  9.4 17.7 %collective-permute-start.7 = (bf16[64,512]{1,0:T(8,128)(2,1)S(1)}, bf16[64,512]{1,0:T(8,128)(2,1)S(1)}, u32[]{:S(2)}, u32[]{:S(2)}) collective-permute-start(bf16[64,512]{1,0:T(8,128)(2,1)S(1)} %maximum_maximum_fusion.refs_0_), channel_id=1, source_target_pairs={{0,4},{1,5},{2,6},{3,7},{4,0},{5,1},{6,2},{7,3},{8,13},{9,12},{10,... | collective-permute-start | bytes 196616 | tf_op jit(solution)/shard_map/ppermute | solution.py:348
  13.5 14.9 %collective-permute-start.8 = (bf16[64,512]{1,0:T(8,128)(2,1)S(1)}, bf16[64,512]{1,0:T(8,128)(2,1)S(1)}, u32[]{:S(2)}, u32[]{:S(2)}) collective-permute-start(bf16[64,512]{1,0:T(8,128)(2,1)S(1)} %maximum_maximum_fusion.refs_0_), channel_id=1, source_target_pairs={{0,6},{1,7},{2,0},{3,1},{4,2},{5,3},{6,4},{7,5},{8,15},{9,14},{10,... | collective-permute-start | bytes 196616 | tf_op jit(solution)/shard_map/ppermute | solution.py:348
  14.8 16.4 %collective-permute-start.6 = (bf16[64,512]{1,0:T(8,128)(2,1)S(1)}, bf16[64,512]{1,0:T(8,128)(2,1)S(1)}, u32[]{:S(2)}, u32[]{:S(2)}) collective-permute-start(bf16[64,512]{1,0:T(8,128)(2,1)S(1)} %maximum_maximum_fusion.refs_0_), channel_id=1, source_target_pairs={{0,2},{1,3},{2,4},{3,5},{4,6},{5,7},{6,0},{7,1},{8,11},{9,10},{10,... | collective-permute-start | bytes 196616 | tf_op jit(solution)/shard_map/ppermute | solution.py:348
  15.5 17.0 %collective-permute-start.5 = (bf16[64,512]{1,0:T(8,128)(2,1)S(1)}, bf16[64,512]{1,0:T(8,128)(2,1)S(1)}, u32[]{:S(2)}, u32[]{:S(2)}) collective-permute-start(bf16[64,512]{1,0:T(8,128)(2,1)S(1)} %maximum_maximum_fusion.refs_0_), channel_id=1, source_target_pairs={{0,1},{1,0},{2,3},{3,2},{4,5},{5,4},{6,7},{7,6},{8,9},{9,8},{10,11... | collective-permute-start | bytes 196616 | tf_op jit(solution)/shard_map/ppermute | solution.py:349
  17.0 1.0 %copy-start = (bf16[16,32,256]{2,1,0:T(8,128)(2,1)S(1)}, bf16[16,32,256]{2,1,0:T(8,128)(2,1)}, u32[]{:S(2)}) copy-start(bf16[16,32,256]{2,1,0:T(8,128)(2,1)} %region.3) | copy-start | bytes 786436
  18.0 0.9 %copy-start.1 = (bf16[8,16,512]{2,1,0:T(8,128)(2,1)S(1)}, bf16[8,16,512]{2,1,0:T(8,128)(2,1)}, u32[]{:S(2)}) copy-start(bf16[8,16,512]{2,1,0:T(8,128)(2,1)} %cot.3) | copy-start | bytes 393220
  18.9 3.8 %collective-permute-start.3 = (bf16[32,256]{1,0:T(8,128)(2,1)S(1)}, bf16[32,256]{1,0:T(8,128)(2,1)S(1)}, u32[]{:S(2)}, u32[]{:S(2)}) collective-permute-start(bf16[32,256]{1,0:T(8,128)(2,1)S(1)} %get-tuple-element.29), channel_id=1, source_target_pairs={{0,1},{1,2},{2,3},{3,4},{4,5},{5,6},{6,7},{8,9},{9,10},{10,11},{11... | collective-permute-start | bytes 49160 | tf_op jit(solution)/shard_map/ppermute | solution.py:335
  22.8 11.7 %collective-permute-start.13 = (bf16[64,768]{1,0:T(8,128)(2,1)S(1)}, bf16[64,768]{1,0:T(8,128)(2,1)S(1)}, u32[]{:S(2)}, u32[]{:S(2)}) collective-permute-start(bf16[64,768]{1,0:T(8,128)(2,1)S(1)} %pad_maximum_fusion.refs_0_), channel_id=1, source_target_pairs={{0,2},{1,3},{2,4},{3,5},{4,6},{5,7},{6,0},{7,1},{8,11},{9,10},{10,... | collective-permute-start | bytes 294920 | tf_op jit(solution)/shard_map/ppermute | solution.py:348
  27.1 7.4 %collective-permute-start.4 = (bf16[96,256]{1,0:T(8,128)(2,1)S(1)}, bf16[96,256]{1,0:T(8,128)(2,1)S(1)}, u32[]{:S(2)}, u32[]{:S(2)}) collective-permute-start(bf16[96,256]{1,0:T(8,128)(2,1)S(1)} %get-tuple-element.30), channel_id=1, source_target_pairs={{1,0},{2,1},{3,2},{4,3},{5,4},{6,5},{7,6},{9,8},{10,9},{11,10},{12... | collective-permute-start | bytes 147464 | tf_op jit(solution)/shard_map/ppermute | solution.py:335
  28.4 8.6 %collective-permute-start.14 = (bf16[64,768]{1,0:T(8,128)(2,1)S(1)}, bf16[64,768]{1,0:T(8,128)(2,1)S(1)}, u32[]{:S(2)}, u32[]{:S(2)}) collective-permute-start(bf16[64,768]{1,0:T(8,128)(2,1)S(1)} %pad_maximum_fusion.refs_0_), channel_id=1, source_target_pairs={{0,4},{1,5},{2,6},{3,7},{4,0},{5,1},{6,2},{7,3},{8,13},{9,12},{10,... | collective-permute-start | bytes 294920 | tf_op jit(solution)/shard_map/ppermute | solution.py:348
  31.2 8.0 %collective-permute-start.15 = (bf16[64,768]{1,0:T(8,128)(2,1)S(1)}, bf16[64,768]{1,0:T(8,128)(2,1)S(1)}, u32[]{:S(2)}, u32[]{:S(2)}) collective-permute-start(bf16[64,768]{1,0:T(8,128)(2,1)S(1)} %pad_maximum_fusion.refs_0_), channel_id=1, source_target_pairs={{0,6},{1,7},{2,0},{3,1},{4,2},{5,3},{6,4},{7,5},{8,15},{9,14},{10,... | collective-permute-start | bytes 294920 | tf_op jit(solution)/shard_map/ppermute | solution.py:348
  32.5 6.7 %collective-permute-start.10 = (bf16[64,512]{1,0:T(8,128)(2,1)S(1)}, bf16[64,512]{1,0:T(8,128)(2,1)S(1)}, u32[]{:S(2)}, u32[]{:S(2)}) collective-permute-start(bf16[64,512]{1,0:T(8,128)(2,1)S(1)} %collective-permute-done.7.refs_3_), channel_id=1, source_target_pairs={{0,8},{8,0},{16,24},{24,16},{1,9},{9,1},{17,25},{25,17},{2,10},{10... | collective-permute-start | bytes 196616 | tf_op jit(solution)/shard_map/ppermute | solution.py:339
  34.4 5.3 %collective-permute-start.11 = (bf16[64,512]{1,0:T(8,128)(2,1)S(1)}, bf16[64,512]{1,0:T(8,128)(2,1)S(1)}, u32[]{:S(2)}, u32[]{:S(2)}) collective-permute-start(bf16[64,512]{1,0:T(8,128)(2,1)S(1)} %collective-permute-done.8.refs_4_), channel_id=1, source_target_pairs={{0,8},{8,0},{16,24},{24,16},{1,9},{9,1},{17,25},{25,17},{2,10},{10... | collective-permute-start | bytes 196616 | tf_op jit(solution)/shard_map/ppermute | solution.py:339
  34.5 5.4 %collective-permute-start.9 = (bf16[64,512]{1,0:T(8,128)(2,1)S(1)}, bf16[64,512]{1,0:T(8,128)(2,1)S(1)}, u32[]{:S(2)}, u32[]{:S(2)}) collective-permute-start(bf16[64,512]{1,0:T(8,128)(2,1)S(1)} %collective-permute-done.6.refs_2_), channel_id=1, source_target_pairs={{0,8},{8,0},{16,24},{24,16},{1,9},{9,1},{17,25},{25,17},{2,10},{10... | collective-permute-start | bytes 196616 | tf_op jit(solution)/shard_map/ppermute | solution.py:339
  37.0 6.1 %collective-permute-start.12 = (bf16[64,768]{1,0:T(8,128)(2,1)S(1)}, bf16[64,768]{1,0:T(8,128)(2,1)S(1)}, u32[]{:S(2)}, u32[]{:S(2)}) collective-permute-start(bf16[64,768]{1,0:T(8,128)(2,1)S(1)} %pad_maximum_fusion.refs_0_), channel_id=1, source_target_pairs={{0,1},{1,0},{2,3},{3,2},{4,5},{5,4},{6,7},{7,6},{8,9},{9,8},{10,11... | collective-permute-start | bytes 294920 | tf_op jit(solution)/shard_map/ppermute | solution.py:349
  39.2 3.9 %collective-permute-start.16 = (bf16[64,768]{1,0:T(8,128)(2,1)S(1)}, bf16[64,768]{1,0:T(8,128)(2,1)S(1)}, u32[]{:S(2)}, u32[]{:S(2)}) collective-permute-start(bf16[64,768]{1,0:T(8,128)(2,1)S(1)} %collective-permute-done.13.refs_2_), channel_id=1, source_target_pairs={{0,8},{8,0},{16,24},{24,16},{1,9},{9,1},{17,25},{25,17},{2,10},{10... | collective-permute-start | bytes 294920 | tf_op jit(solution)/shard_map/ppermute | solution.py:339
  39.2 3.9 %collective-permute-start.17 = (bf16[64,768]{1,0:T(8,128)(2,1)S(1)}, bf16[64,768]{1,0:T(8,128)(2,1)S(1)}, u32[]{:S(2)}, u32[]{:S(2)}) collective-permute-start(bf16[64,768]{1,0:T(8,128)(2,1)S(1)} %collective-permute-done.14.refs_3_), channel_id=1, source_target_pairs={{0,8},{8,0},{16,24},{24,16},{1,9},{9,1},{17,25},{25,17},{2,10},{10... | collective-permute-start | bytes 294920 | tf_op jit(solution)/shard_map/ppermute | solution.py:339
  39.7 3.4 %collective-permute-start.18 = (bf16[64,768]{1,0:T(8,128)(2,1)S(1)}, bf16[64,768]{1,0:T(8,128)(2,1)S(1)}, u32[]{:S(2)}, u32[]{:S(2)}) collective-permute-start(bf16[64,768]{1,0:T(8,128)(2,1)S(1)} %collective-permute-done.15.refs_4_), channel_id=1, source_target_pairs={{0,8},{8,0},{16,24},{24,16},{1,9},{9,1},{17,25},{25,17},{2,10},{10... | collective-permute-start | bytes 294920 | tf_op jit(solution)/shard_map/ppermute | solution.py:339
  47.7 1.6 %collective-permute-start.19 = (bf16[4,64,512]{2,1,0:T(8,128)(2,1)S(1)}, bf16[4,64,512]{2,1,0:T(8,128)(2,1)S(1)}, u32[]{:S(2)}, u32[]{:S(2)}) collective-permute-start(bf16[4,64,512]{2,1,0:T(8,128)(2,1)S(1)} %get-tuple-element.43), channel_id=1, source_target_pairs={{0,8},{8,0},{16,24},{24,16},{1,9},{9,1},{17,25},{25,17},{2,10},{10... | collective-permute-start | bytes 786440 | tf_op jit(solution)/shard_map/ppermute | solution.py:339
  48.1 13.2 %collective-permute-start.26 = (bf16[4,64,768]{2,1,0:T(8,128)(2,1)S(1)}, bf16[4,64,768]{2,1,0:T(8,128)(2,1)S(1)}, u32[]{:S(2)}, u32[]{:S(2)}) collective-permute-start(bf16[4,64,768]{2,1,0:T(8,128)(2,1)S(1)} %get-tuple-element.48), channel_id=1, source_target_pairs={{0,8},{8,0},{16,24},{24,16},{1,9},{9,1},{17,25},{25,17},{2,10},{10... | collective-permute-start | bytes 1179656 | tf_op jit(solution)/shard_map/ppermute | solution.py:339
  49.4 6.8 %collective-permute-start.20 = (bf16[64,512]{1,0:T(8,128)(2,1)S(1)}, bf16[64,512]{1,0:T(8,128)(2,1)S(1)}, u32[]{:S(2)}, u32[]{:S(2)}) collective-permute-start(bf16[64,512]{1,0:T(8,128)(2,1)S(1)} %get-tuple-element.56), channel_id=1, source_target_pairs={{0,6},{1,7},{2,0},{3,1},{4,2},{5,3},{6,4},{7,5},{8,15},{9,14},{10,... | collective-permute-start | bytes 196616 | tf_op jit(solution)/shard_map/ppermute | solution.py:365
  53.6 7.1 %collective-permute-start.21 = (bf16[64,512]{1,0:T(8,128)(2,1)S(1)}, bf16[64,512]{1,0:T(8,128)(2,1)S(1)}, u32[]{:S(2)}, u32[]{:S(2)}) collective-permute-start(bf16[64,512]{1,0:T(8,128)(2,1)S(1)} %get-tuple-element.59), channel_id=1, source_target_pairs={{0,4},{1,5},{2,6},{3,7},{4,0},{5,1},{6,2},{7,3},{8,13},{9,12},{10,... | collective-permute-start | bytes 196616 | tf_op jit(solution)/shard_map/ppermute | solution.py:365
  53.6 7.1 %collective-permute-start.22 = (bf16[64,512]{1,0:T(8,128)(2,1)S(1)}, bf16[64,512]{1,0:T(8,128)(2,1)S(1)}, u32[]{:S(2)}, u32[]{:S(2)}) collective-permute-start(bf16[64,512]{1,0:T(8,128)(2,1)S(1)} %get-tuple-element.58), channel_id=1, source_target_pairs={{0,2},{1,3},{2,4},{3,5},{4,6},{5,7},{6,0},{7,1},{8,11},{9,10},{10,... | collective-permute-start | bytes 196616 | tf_op jit(solution)/shard_map/ppermute | solution.py:365
  54.2 6.4 %collective-permute-start.23 = (bf16[64,512]{1,0:T(8,128)(2,1)S(1)}, bf16[64,512]{1,0:T(8,128)(2,1)S(1)}, u32[]{:S(2)}, u32[]{:S(2)}) collective-permute-start(bf16[64,512]{1,0:T(8,128)(2,1)S(1)} %get-tuple-element.57), channel_id=1, source_target_pairs={{8,9},{9,8},{10,11},{11,10},{12,13},{13,12},{14,15},{15,14},{24,25... | collective-permute-start | bytes 196616 | tf_op jit(solution)/shard_map/ppermute | solution.py:365
  60.7 5.1 %collective-permute-start.24 = (f32[64,512]{1,0:T(8,128)S(1)}, f32[64,512]{1,0:T(8,128)S(1)}, u32[]{:S(2)}, u32[]{:S(2)}) collective-permute-start(f32[64,512]{1,0:T(8,128)S(1)} %select_add_fusion.1), channel_id=1, source_target_pairs={{0,8},{8,0},{16,24},{24,16},{1,9},{9,1},{17,25},{25,17},{2,10},{10... | collective-permute-start | bytes 393224 | tf_op jit(solution)/shard_map/ppermute | solution.py:339
  61.4 5.9 %collective-permute-start.27 = (bf16[64,768]{1,0:T(8,128)(2,1)S(1)}, bf16[64,768]{1,0:T(8,128)(2,1)S(1)}, u32[]{:S(2)}, u32[]{:S(2)}) collective-permute-start(bf16[64,768]{1,0:T(8,128)(2,1)S(1)} %get-tuple-element.52), channel_id=1, source_target_pairs={{0,6},{1,7},{2,0},{3,1},{4,2},{5,3},{6,4},{7,5},{8,15},{9,14},{10,... | collective-permute-start | bytes 294920 | tf_op jit(solution)/shard_map/ppermute | solution.py:365
  63.2 10.8 %collective-permute-start.28 = (bf16[64,768]{1,0:T(8,128)(2,1)S(1)}, bf16[64,768]{1,0:T(8,128)(2,1)S(1)}, u32[]{:S(2)}, u32[]{:S(2)}) collective-permute-start(bf16[64,768]{1,0:T(8,128)(2,1)S(1)} %get-tuple-element.55), channel_id=1, source_target_pairs={{0,4},{1,5},{2,6},{3,7},{4,0},{5,1},{6,2},{7,3},{8,13},{9,12},{10,... | collective-permute-start | bytes 294920 | tf_op jit(solution)/shard_map/ppermute | solution.py:365
  64.7 9.2 %collective-permute-start.29 = (bf16[64,768]{1,0:T(8,128)(2,1)S(1)}, bf16[64,768]{1,0:T(8,128)(2,1)S(1)}, u32[]{:S(2)}, u32[]{:S(2)}) collective-permute-start(bf16[64,768]{1,0:T(8,128)(2,1)S(1)} %get-tuple-element.54), channel_id=1, source_target_pairs={{0,2},{1,3},{2,4},{3,5},{4,6},{5,7},{6,0},{7,1},{8,11},{9,10},{10,... | collective-permute-start | bytes 294920 | tf_op jit(solution)/shard_map/ppermute | solution.py:365
  65.1 8.8 %collective-permute-start.30 = (bf16[64,768]{1,0:T(8,128)(2,1)S(1)}, bf16[64,768]{1,0:T(8,128)(2,1)S(1)}, u32[]{:S(2)}, u32[]{:S(2)}) collective-permute-start(bf16[64,768]{1,0:T(8,128)(2,1)S(1)} %get-tuple-element.53), channel_id=1, source_target_pairs={{8,9},{9,8},{10,11},{11,10},{12,13},{13,12},{14,15},{15,14},{24,25... | collective-permute-start | bytes 294920 | tf_op jit(solution)/shard_map/ppermute | solution.py:365
  65.8 8.5 %collective-permute-start.25 = (bf16[64,512]{1,0:T(8,128)(2,1)S(1)}, bf16[64,512]{1,0:T(8,128)(2,1)S(1)}, u32[]{:S(2)}, u32[]{:S(2)}) collective-permute-start(bf16[64,512]{1,0:T(8,128)(2,1)S(1)} %add_convert_fusion.1), channel_id=1, source_target_pairs={{0,16},{8,24},{16,0},{24,8},{1,17},{9,25},{17,1},{25,9},{2,18},{10... | collective-permute-start | bytes 196616 | tf_op jit(solution)/shard_map/ppermute | solution.py:373
  74.0 1.5 %collective-permute-start.31 = (f32[64,768]{1,0:T(8,128)S(1)}, f32[64,768]{1,0:T(8,128)S(1)}, u32[]{:S(2)}, u32[]{:S(2)}) collective-permute-start(f32[64,768]{1,0:T(8,128)S(1)} %select_add_fusion), channel_id=1, source_target_pairs={{0,8},{8,0},{16,24},{24,16},{1,9},{9,1},{17,25},{25,17},{2,10},{10... | collective-permute-start | bytes 589832 | tf_op jit(solution)/shard_map/ppermute | solution.py:339
  75.5 5.0 %collective-permute-start.32 = (bf16[64,768]{1,0:T(8,128)(2,1)S(1)}, bf16[64,768]{1,0:T(8,128)(2,1)S(1)}, u32[]{:S(2)}, u32[]{:S(2)}) collective-permute-start(bf16[64,768]{1,0:T(8,128)(2,1)S(1)} %add_convert_fusion), channel_id=1, source_target_pairs={{0,16},{8,24},{16,0},{24,8},{1,17},{9,25},{17,1},{25,9},{2,18},{10... | collective-permute-start | bytes 294920 | tf_op jit(solution)/shard_map/ppermute | solution.py:373

commit v2 on v1

v2 whole, which is shorter than its diff:
```python
import functools

import jax
import jax.numpy as jnp
from jax import lax
from jax.experimental import pallas as pl
from jax.experimental.pallas import tpu as pltpu
from jax.sharding import PartitionSpec as P

GW = 16
TAPS = 9
HALF = 256
BACK = (4, 5, 3, 7, 1, 8, 2, 6, 0)
F32 = jnp.float32
BF16 = jnp.bfloat16
VMEM_LIMIT = 40 * 1024 * 1024


class Sizes:
    def __init__(self, tile_rows, tile_cols):
        self.tr, self.tc = tile_rows, tile_cols
        self.hr, self.hc = tile_rows // 2, tile_cols // 2
        self.odd = (self.hr + 2) * self.hc
        self.even = (self.hr + 1) * self.hc
        self.band = self.odd + self.even
        self.side = 3 * self.band
        self.pixels = self.side + TAPS * 16
        self.main = self.hr * self.hc
        self.wide = self.main + self.hc
        self.out = self.wide + 16

    def tap(self, tap):
        a, b = divmod(tap, 3)
        return b * self.band + (0, self.odd, self.hc)[a]

    def tap_side(self, tap):
        return self.side + tap * 16

    def planes(self):
        return (
            self.band + self.odd,
            2 * self.band + self.odd,
            self.band + self.hc,
            2 * self.band + self.hc,
        )


def dot(a, b, dims=((1,), (0,))):
    return lax.dot_general(a, b, (dims, ((), ())), preferred_element_type=F32)


def sigmoid(value):
    return 1.0 / (1.0 + jnp.exp(-value))


def place():
    col = lax.axis_index("col")
    return col // 2, lax.rem(col, 2), lax.rem(lax.axis_index("row"), 2)


def pieces(halves, own, passed, swapped):
    h, low, core = place()
    shard = own.shape[0]
    flips = (low + core - 2 * low * core, 1 - low - core + 2 * low * core)
    found = [(own, (2 * h + low) * shard)]
    for ref, flip in zip((passed, swapped), flips, strict=True):
        for j in range(1, halves):
            spot = 2 * lax.rem(h - j + halves, halves) + flip
            found.append((ref.at[(j - 1) * shard : j * shard], spot * shard))
    share = passed.shape[0] - (halves - 1) * shard
    beside = (2 * h + 1 - low) * shard
    if share == shard:
        return found + [(passed.at[(halves - 1) * shard :], beside)]
    for ref, part in ((passed, core), (swapped, 1 - core)):
        found.append((ref.at[(halves - 1) * shard :], beside + part * share))
    return found


def send_kernel(sizes, *refs):
    given, (weights, outer, draft, cols) = refs[:6], refs[6:10]
    local, arrived = refs[10:16], refs[16]
    copies = [
        pltpu.make_async_copy(given[i], local[i], arrived.at[i]) for i in range(len(given))
    ]
    for copy in copies:
        copy.start()
    for copy in copies:
        copy.wait()
    region, cot, reduce_t, group_t, expand_t, short_t = local
    shard, taps = group_t.shape
    cin, mid = reduce_t.shape[1], expand_t.shape[1]
    last = cin + 256 + mid
    pad = jnp.zeros((shard, 256 - taps), BF16)
    weights[:, :cin] = reduce_t[...]
    weights[:, cin : cin + 256] = jnp.concatenate([group_t[...], pad], axis=1)
    weights[:, cin + 256 : last] = expand_t[...]
    weights[:, last:] = short_t[...]
    tc, half = sizes.tc, cot.shape[2] // 2
    for i, r in enumerate((sizes.tr - 1, 0, 1)):
        outer[i * tc : (i + 1) * tc] = region[r]
    outer[3 * tc : 3 * tc + sizes.hc] = cot[0, :, :half]
    outer[3 * tc + sizes.hc :] = cot[0, :, half:]
    cols[...] = jnp.zeros_like(cols)
    for r in range(sizes.tr):
        head, tail = region[r, :16].astype(F32), region[r, tc - 16 :].astype(F32)
        cols[r + 1 : r + 2, :cin] = head[0:1]
        cols[r + 1 : r + 2, cin : 2 * cin] = head[1:2]
        cols[r + 1 : r + 2, 2 * cin : 3 * cin] = tail[15:16]
    for i in range(sizes.hr):
        cols[i : i + 1, 3 * cin :] = cot[i, :16].astype(F32)[0:1]
    share = draft.shape[0] - 32
    if share == shard:
        draft[:share] = weights[...]
    else:
        core = lax.rem(lax.axis_index("row"), 2)
        draft[:share] = weights[pl.ds(pl.multiple_of(core * share, share), share), :]
    draft[share:] = cols[...].astype(BF16)


def choose(first, one, other, to_one, to_other):
    @pl.when(first)
    def _():
        to_one[...] = one[...]
        to_other[...] = other[...]

    @pl.when(jnp.logical_not(first))
    def _():
        to_one[...] = other[...]
        to_other[...] = one[...]


def columns_kernel(sizes, core_rows, far_rows, draft, beside, edge, north, south, cols):
    choose(lax.rem(lax.axis_index("row"), 2) == 0, core_rows, far_rows, south, north)
    cin, tc, tr = core_rows.shape[1], sizes.tc, sizes.tr
    share = draft.shape[0] - 32
    beside[:share] = draft[:share]
    cols[...] = draft[share:].astype(F32)
    for to, rows, at in ((0, north, 0), (tr + 1, south, tc), (tr + 2, south, 2 * tc)):
        head = rows[at : at + 16].astype(F32)
        tail = rows[at + tc - 16 : at + tc].astype(F32)
        cols[to : to + 1, :cin] = head[0:1]
        cols[to : to + 1, cin : 2 * cin] = head[1:2]
        cols[to : to + 1, 2 * cin : 3 * cin] = tail[15:16]
    for i in range(2):
        at, lanes = 3 * tc + i * sizes.hc, slice((3 + i) * cin, (4 + i) * cin)
        cols[sizes.hr : sizes.hr + 1, lanes] = south[at : at + 16].astype(F32)[0:1]
    beside[share:] = cols[...].astype(BF16)
    edge[...] = cols[...].astype(BF16)


def pass_kernel(beside, _, *refs):
    far, passed = refs[:-1], refs[-1]
    shard, share = far[0].shape[0], beside.shape[0] - 32
    for j, block in enumerate(far):
        passed[j * shard : (j + 1) * shard] = block[...]
    passed[len(far) * shard :] = beside[:share]


def spread_kernel(sizes, region, cot, core_rows, far_rows, beside, edge, *refs):
    x, cot_all, north, south, west, east, left, right, ext, cols = refs
    choose(lax.rem(lax.axis_index("row"), 2) == 0, core_rows, far_rows, south, north)
    choose(lax.rem(lax.axis_index("col"), 2) == 0, beside.at[beside.shape[0] - 32 :], edge, east, west)
    cin, tc, tr, hc = region.shape[2], sizes.tc, sizes.tr, sizes.hc
    left[...] = west[:, 2 * cin : 3 * cin].astype(F32)
    right[...] = east[:, : 2 * cin].astype(F32)
    cols[...] = jnp.zeros_like(cols)
    for v in range(cin // 128):
        lanes = slice(v * 128, (v + 1) * 128)
        for r in range(tr + 3):
            if r == 0:
                row = north[:tc, lanes]
            elif r <= tr:
                row = region[r - 1, :, lanes]
            else:
                row = south[(r - tr) * tc : (1 + r - tr) * tc, lanes]
            ext[v, r, 8 : 8 + tc] = row.astype(F32)
            ext[v, r, 7:8] = left[r : r + 1, lanes]
            cols[0, v, r : r + 1] = ext[v, r, 7 + tc : 8 + tc]
        for b in (1, 2):
            cols[b, v, :32] = right[:, (b - 1) * cin + v * 128 : (b - 1) * cin + (v + 1) * 128]
        for b in range(3):
            base = b * sizes.band
            for r in list(range(0, tr + 3, 2)) + list(range(1, tr + 3, 2)):
                picked = ext[v, r, pl.ds(7 + b, hc, stride=2)]
                x[base : base + hc, lanes] = picked.astype(BF16)
                base += hc
            for a in range(3):
                at = sizes.tap_side(3 * a + b)
                x[at : at + 16, lanes] = cols[b, v, pl.ds(a, 16, stride=2)].astype(BF16)
    half = cot_all.shape[1] // 2
    cot_all[: sizes.main] = cot[...].reshape(sizes.main, 2 * half)
    cot_all[sizes.main : sizes.wide, :half] = south[3 * tc : 3 * tc + hc]
    cot_all[sizes.main : sizes.wide, half:] = south[3 * tc + hc :]
    cot_all[sizes.wide :] = east[:16, 3 * cin :]


def first_kernel(sizes, halves, x, *refs):
    hidden, slope_one, hidden_two, slope_two, back, reduce_t = refs[3:9]
    pre, group_t, group, front, pre_two = refs[9:]
    cin = reduce_t.shape[1]
    mid = reduce_t.shape[0]
    for block, first in pieces(halves, *refs[:3]):
        rows = pl.ds(pl.multiple_of(first, 16), block.shape[0])
        reduce_t[rows, :] = block[:, :cin]
        group_t[rows, :] = block[:, cin : cin + 256]
    pre[...] = dot(x[...], reduce_t[...], ((1,), (1,)))
    group[...] = group_t[...].astype(F32).T.astype(BF16)
    row_group = lax.broadcasted_iota(jnp.int32, (HALF, HALF), 0) // GW
    lane_group = lax.broadcasted_iota(jnp.int32, (HALF, HALF), 1) // GW
    mask = jnp.where(row_group == lane_group, 1.0, 0.0).astype(BF16)
    for n in range(mid // HALF):
        for tap in range(TAPS):
            rows = group[tap * GW : (tap + 1) * GW, n * HALF : (n + 1) * HALF]
            dense = jnp.concatenate([rows] * (HALF // GW), axis=0) * mask
            front[n, tap * HALF : (tap + 1) * HALF] = dense
            spot = BACK.index(tap)
            back[n, :, spot * HALF : (spot + 1) * HALF] = dense

    def silu_rows(at, _):
        rows = pl.ds(pl.multiple_of(at * 16, 16), 16)
        value = pre[rows, :]
        hidden[rows, :] = (value * sigmoid(value)).astype(BF16)
        return 0

    def plane_rows(at, start, to):
        source = pl.ds(pl.multiple_of(start + at * 16, 16), 16)
        target = pl.ds(pl.multiple_of(to + at * 16, 16), 16)
        value = pre[source, :]
        sigma = sigmoid(value)
        active = value * sigma
        hidden[source, :] = active.astype(BF16)
        slope_one[target, :] = sigma + active * (1.0 - sigma)

    lax.fori_loop(0, sizes.pixels // 16, silu_rows, 0, unroll=2)
    for i, start in enumerate(sizes.planes()):

        def body(at, _, start=start, to=i * sizes.main):
            plane_rows(at, start, to)
            return 0

        lax.fori_loop(0, sizes.main // 16, body, 0, unroll=2)

    for n in range(mid // HALF):
        lanes = slice(n * HALF, (n + 1) * HALF)
        patches = []
        for tap in range(TAPS):
            at, side = sizes.tap(tap), sizes.tap_side(tap)
            patches.append(
                jnp.concatenate(
                    [hidden[at : at + sizes.wide, lanes], hidden[side : side + 16, lanes]], axis=0
                )
            )
        pre_two[:, lanes] = dot(jnp.concatenate(patches, axis=1), front[n])
    value = pre_two[...]
    sigma = sigmoid(value)
    active = value * sigma
    hidden_two[...] = active.astype(BF16)
    slope_two[...] = sigma + active * (1.0 - sigma)


def split_out(halves, total, shard, keeps, give):
    h, low, core = place()
    keep = low + core - 2 * low * core
    for j in range(halves):
        base = 2 * lax.rem(h + j, halves)
        mine = pl.ds(pl.multiple_of((base + keep) * shard, shard), shard)
        theirs = pl.ds(pl.multiple_of((base + 1 - keep) * shard, shard), shard)
        keeps[j][...] = total[mine, :]
        give[j] = total[theirs, :].astype(BF16)


def second_kernel(sizes, halves, x, hidden_two, slope_two, cot, *refs):
    block_out, grad_two, grad_side, short_back, total, expand_t, short_t, shift = refs[3:]
    skip = refs[0].shape[1] - total.shape[1]
    mid = expand_t.shape[1]
    width = expand_t.shape[0]
    for block, first in pieces(halves, *refs[:3]):
        rows = pl.ds(pl.multiple_of(first, 16), block.shape[0])
        expand_t[rows, :] = block[:, skip : skip + mid]
        short_t[rows, :] = block[:, skip + mid :]
    at, side = sizes.tap(4), sizes.tap_side(4)
    strided = jnp.concatenate([x[at : at + sizes.wide], x[side : side + 16]], axis=0)
    summed = dot(hidden_two[...], expand_t[...], ((1,), (1,))) + dot(
        strided, short_t[...], ((1,), (1,))
    )
    sigma = sigmoid(summed)
    active = summed * sigma
    block_out[...] = (
        active[: sizes.main].astype(BF16).reshape(sizes.hr, sizes.hc, width)
    )
    grad_sum = (cot[...].astype(F32) * (sigma + active * (1.0 - sigma))).astype(BF16)
    own = grad_sum[: sizes.main]
    flipped = own.astype(F32).T.astype(BF16)
    total[:, :mid] = dot(flipped, hidden_two[: sizes.main])
    total[:, mid:] = dot(flipped, strided[: sizes.main])
    short_back[...] = dot(own, short_t[...])
    back = dot(grad_sum, expand_t[...]) * slope_two[...]
    grad_two[...] = back[: sizes.wide].astype(BF16)
    for i in range(sizes.hr + 1):
        shift[i, : sizes.hc] = back[i * sizes.hc : (i + 1) * sizes.hc]
        shift[i, sizes.hc : sizes.hc + 1] = back[sizes.wide + i : sizes.wide + i + 1]
    for i in range(sizes.hr + 1):
        grad_side[i * sizes.hc : (i + 1) * sizes.hc] = shift[i, 1 : sizes.hc + 1].astype(BF16)


def third_kernel(
    sizes, halves, x, hidden, slope_one, back, reduce_t, grad_two, grad_side, short_back, late, *refs
):
    region_grad, give = refs[:2]
    keeps = refs[2 : 2 + halves]
    total, grad_one, planes, spread_out = refs[2 + halves :]
    mid, cin = reduce_t.shape
    main, hc = sizes.main, sizes.hc
    shard = keeps[0].shape[0]
    down = slice(hc, hc + main)
    own = slice(0, main)
    for n in range(mid // HALF):
        lanes = slice(n * HALF, (n + 1) * HALF)
        two, low = grad_two[own, lanes], grad_two[down, lanes]
        side, corner = grad_side[own, lanes], grad_side[down, lanes]
        first = 0
        for i, parts in enumerate(((two,), (two, side), (two, low), (two, low, side, corner))):
            left = jnp.concatenate(parts, axis=1)
            last = first + len(parts) * HALF
            spread = dot(left, back[n, :, first:last], ((1,), (1,)))
            first = last
            rows = slice(i * main, (i + 1) * main)
            grad_one[rows, lanes] = (spread * slope_one[rows, lanes]).astype(BF16)
    flat = jnp.concatenate([x[at : at + main] for at in sizes.planes()], axis=0)
    total[:, :cin] = dot(grad_one[...].astype(F32).T.astype(BF16), flat)
    flipped = grad_two[own, :].astype(F32).T.astype(BF16)
    lane = lax.broadcasted_iota(jnp.int32, (GW, 128), 1) // GW
    for n in range(mid // HALF):
        lanes = slice(n * HALF, (n + 1) * HALF)
        sums = [jnp.zeros((GW, 128), F32)] * (HALF // GW)
        for tap in range(TAPS):
            at = sizes.tap(tap)
            piece = dot(flipped[n * HALF : (n + 1) * HALF], hidden[at : at + main, lanes])
            for q in range(HALF // GW):
                tile = q // 8
                block = piece[q * GW : (q + 1) * GW, tile * 128 : (tile + 1) * 128]
                block = pltpu.roll(block, (GW * (tap - q)) % 128, 1)
                if tap < 8:
                    sums[q] = jnp.where(lane == tap, block, sums[q])
                else:
                    rows = slice(n * HALF + q * GW, n * HALF + (q + 1) * GW)
                    total[rows, cin : cin + 128] = sums[q]
                    total[rows, cin + 128 : cin + 256] = jnp.where(lane == 0, block, 0.0)
    total[:, cin + 256 :] = late[...]
    split_out(halves, total, shard, keeps, give)
    planes[...] = dot(grad_one[...], reduce_t[...])
    planes[:main] += short_back[...]
    for i in range(4):
        for r in range(sizes.hr):
            at = i * main + r * hc
            for v in range(cin // 128):
                lanes = slice(v * 128, (v + 1) * 128)
                spread_out[v, 2 * r + i // 2, pl.ds(i % 2, hc, stride=2)] = planes[at : at + hc, lanes]
    for v in range(cin // 128):
        region_grad[:, :, v * 128 : (v + 1) * 128] = spread_out[v].astype(BF16)


def call(kernel, out_shape, scratch, *operands, flops=0, space=pltpu.VMEM, limit=VMEM_LIMIT):
    sizes = sum(o.size * o.dtype.itemsize for o in operands)
    sizes += sum(o.size * o.dtype.itemsize for o in jax.tree.leaves(out_shape))
    return pl.pallas_call(
        kernel,
        out_shape=out_shape,
        in_specs=[pl.BlockSpec(memory_space=space)] * len(operands),
        out_specs=jax.tree.map(lambda _: pl.BlockSpec(memory_space=pltpu.VMEM), out_shape),
        scratch_shapes=scratch,
        compiler_params=pltpu.CompilerParams(vmem_limit_bytes=limit),
        cost_estimate=pl.CostEstimate(flops=flops, bytes_accessed=sizes, transcendentals=0),
    )(*operands)


def finish_kernel(total, across, *outs):
    value = total[...].astype(F32) + across[...].astype(F32)
    at = 0
    for out, skip in zip(outs, (0, 256 - outs[1].shape[1], 0, 0), strict=True):
        out[...] = value[:, at : at + out.shape[1]]
        at += out.shape[1] + skip


def both(rows, cols, target):
    pairs = []
    for r in range(rows):
        for c in range(cols):
            to = target(r % 2, c // 2, c % 2)
            if to is not None:
                pairs.append((r * cols + c, r * cols + 2 * to[0] + to[1]))
    return pairs


def swap_odd(x, axis):
    pairs = []
    for i in range(1, lax.axis_size(axis) - 1, 2):
        pairs += [(i, i + 1), (i + 1, i)]
    return lax.ppermute(x, axis, pairs)


def swap_even(x, axis):
    return lax.ppermute(x, axis, [(i, i ^ 1) for i in range(lax.axis_size(axis))])


def cross(x, j):
    rows, cols = lax.axis_size("row"), lax.axis_size("col")
    halves = cols // 2

    def target(k, h, low):
        return None if j == k == 0 else ((h + j) % halves, low ^ k)

    return lax.ppermute(x, ("row", "col"), both(rows, cols, target))


def reduce(keeps, give):
    rows, halves = lax.axis_size("row"), lax.axis_size("col") // 2
    core = lax.axis_index("row") % 2
    other = swap_even(give, "row")
    sums = [keeps[j] + other[j].astype(F32) for j in range(halves)]
    total = None
    for j in range(halves - 1, -1, -1):
        came = cross(sums[j].astype(BF16), j).astype(F32)
        if j == 0:
            came = jnp.where(core == 0, sums[0], came)
        total = came if total is None else total + came
    if rows != 4:
        return lax.psum(total, "row"), jnp.zeros_like(total)
    total = (total + swap_even(total, "row")).astype(BF16)
    return total, lax.ppermute(total, "row", [(r, r ^ 2) for r in range(4)])


def per_device(region, reduce_weight, group_weight, expand_weight, shortcut_weight, cotangent):
    tile_rows, tile_cols, cin = region.shape
    sizes = Sizes(tile_rows, tile_cols)
    halves = lax.axis_size("col") // 2
    mid, shard = expand_weight.shape
    width = shard * lax.axis_size("col")
    taps = group_weight.shape[0]
    early, late = cin + 256, mid + cin
    halo = 3 * cin + width
    share = shard // 2 if shard % 32 == 0 else shard

    def shape(dims, dtype=BF16):
        return jax.ShapeDtypeStruct(dims, dtype)

    def scratch(*dims, dtype=F32):
        return pltpu.VMEM(dims, dtype)

    inputs = (
        region, cotangent, reduce_weight.T, group_weight.T, expand_weight.T, shortcut_weight.T,
    )
    weights, outer, draft = call(
        functools.partial(send_kernel, sizes),
        (
            shape((shard, early + late)),
            shape((4 * tile_cols, cin)),
            shape((share + 32, halo)),
        ),
        [scratch(32, halo)]
        + [scratch(*given.shape, dtype=BF16) for given in inputs]
        + [pltpu.SemaphoreType.DMA((len(inputs),))],
        *inputs,
        space=pltpu.HBM,
        limit=62 * 1024 * 1024,
    )
    far = [cross(weights, j) for j in range(1, halves)]
    core_rows = swap_even(outer, "row")
    far_rows = swap_odd(outer, "row")
    rows_scratch = [scratch(4 * tile_cols, cin, dtype=BF16)] * 2
    beside, edge = call(
        functools.partial(columns_kernel, sizes),
        (shape(draft.shape), shape((32, halo))),
        rows_scratch + [scratch(32, halo)],
        core_rows, far_rows, draft,
    )
    beside, edge = swap_even(beside, "col"), swap_odd(edge, "col")
    x, cot_all = call(
        functools.partial(spread_kernel, sizes),
        (shape((sizes.pixels, cin)), shape((sizes.out, width))),
        rows_scratch
        + [
            scratch(32, halo, dtype=BF16),
            scratch(32, halo, dtype=BF16),
            scratch(32, cin),
            scratch(32, 2 * cin),
            scratch(cin // 128, tile_rows + 3, 8 + tile_cols, 128),
            scratch(3, cin // 128, 40, 128),
        ],
        region, cotangent, core_rows, far_rows, beside, edge,
    )
    passed = call(
        pass_kernel,
        shape(((halves - 1) * shard + share, early + late)),
        [],
        beside, edge, *far,
    )
    blocks = [weights, passed, swap_even(passed, "row")]
    hidden, slope_one, hidden_two, slope_two, back, reduce_t = call(
        functools.partial(first_kernel, sizes, halves),
        (
            shape((sizes.pixels, mid)),
            shape((4 * sizes.main, mid), F32),
            shape((sizes.out, mid)),
            shape((sizes.out, mid), F32),
            shape((mid // HALF, HALF, TAPS * HALF)),
            shape((mid, cin)),
        ),
        [
            scratch(sizes.pixels, mid),
            scratch(mid, 256, dtype=BF16),
            scratch(256, mid, dtype=BF16),
            scratch(mid // HALF, TAPS * HALF, HALF, dtype=BF16),
            scratch(sizes.out, mid),
        ],
        x, *blocks,
        flops=2 * sizes.pixels * cin * mid + 2 * sizes.out * TAPS * HALF * mid,
    )
    block_out, grad_two, grad_side, short_back, late_total = call(
        functools.partial(second_kernel, sizes, halves),
        (
            shape((sizes.hr, sizes.hc, width)),
            shape((sizes.wide, mid)),
            shape((sizes.wide, mid)),
            shape((sizes.main, cin), F32),
            shape((width, late), F32),
        ),
        [
            scratch(width, mid, dtype=BF16),
            scratch(width, cin, dtype=BF16),
            scratch(sizes.hr + 1, 24, mid),
        ],
        x, hidden_two, slope_two, cot_all, *blocks,
        flops=6 * sizes.out * width * (mid + cin),
    )
    region_grad, give, *keeps = call(
        functools.partial(third_kernel, sizes, halves),
        (shape(region.shape), shape((halves, shard, early + late)))
        + (shape((shard, early + late), F32),) * halves,
        [
            scratch(mid, early + late),
            scratch(4 * sizes.main, mid, dtype=BF16),
            scratch(4 * sizes.main, cin),
            scratch(cin // 128, tile_rows, tile_cols, 128),
        ],
        x, hidden, slope_one, back, reduce_t, grad_two, grad_side, short_back, late_total,
        flops=4 * 4 * sizes.main * cin * mid + 4 * sizes.main * TAPS * HALF * mid,
    )
    total, across = reduce(keeps, give)
    grads = call(
        finish_kernel,
        tuple(shape((shard, lanes), F32) for lanes in (cin, taps, mid, cin)),
        [],
        total, across,
    )
    return (block_out, region_grad, *(grad.T for grad in grads))


def solution(mesh):
    tiles, split = P("row", "col", None), P(None, "col")
    return jax.shard_map(
        per_device,
        mesh=mesh,
        in_specs=(tiles, split, split, split, split, tiles),
        out_specs=(tiles, tiles, split, split, split, split),
        check_vma=False,
    )
```

time: 82.4 us -> 63 us (0.76)
  starting transfers between devices: 44.9 us -> 21.2 us
  waiting for transfers between devices: 19.5 us -> 28.4 us
  local copies, waits for them, and re-layouts: 6.75 us -> 0.93 us
  Pallas kernels: 7.88 us -> 10.2 us
  other arithmetic: 2 us -> 0.27 us
    ppermute x33 -> x15, starting transfers between devices: 44.9 us -> 21.2 us  [the longest x7 14.3 us: cross(): return lax.ppermute(x, ('row', 'col'), both(rows, cols, target))]
    ppermute x33 -> x15, waiting for transfers between devices: 19.5 us -> 28.4 us  [the longest x7 16 us: cross(): return lax.ppermute(x, ('row', 'col'), both(rows, cols, target))]
    transpose x4 -> x0, local copies, waits for them, and re-layouts: 2.57 us -> none  [the longest x1 0.66 us: per_device(): late_sum[:, :mid]]
    pallas_call x5 -> x8, Pallas kernels: 7.88 us -> 10.2 us  [call(): pl.pallas_call(kernel, out_shape=out_shape, in_specs=[pl.BlockSpec(memory...]
    slice x3 -> x0, local copies, waits for them, and re-layouts: 2.24 us -> none  [the longest x1 0.8 us: per_device(): south = shifted(region[:2], 'row', -1)]
    concatenate x2 -> x0, other arithmetic: 1.66 us -> none  [the longest x1 0.87 us: per_device(): late = jnp.concatenate([expand_weight.T, shortcut_weight.T], axis=1)]
    unnamed x6 -> x8, local copies, waits for them, and re-layouts: 1.86 us -> 0.93 us
  transfers between devices with their start and end apart: 33 -> 15, of which waited for: 8 -> 8; matrix products, arithmetic and copies ran while one was open for 6% -> 0% of each run, Pallas kernels for 4% -> 0%
where the time goes in v2:
time: 63 us; the launch traced here: 61.8 us
  waiting for transfers between devices  28.4 us (45%)
  starting transfers between devices  21.2 us (34%)
  Pallas kernels  10.2 us (16%)
  local copies, waits for them, and re-layouts  0.93 us (1%)
  between operations  0.75 us (1%)
    ppermute x7, waiting for transfers between devices, cross(): return lax.ppermute(x, ('row', 'col'), both(rows, cols, target))  16 us
    ppermute x7, starting transfers between devices, cross(): return lax.ppermute(x, ('row', 'col'), both(rows, cols, target))  14.3 us
    pallas_call x8, Pallas kernels, call(): pl.pallas_call(kernel, out_shape=out_shape, in_specs=[pl.BlockSpec(memory...  10.2 us
    ppermute x5, waiting for transfers between devices, swap_even(): lax.ppermute(x, axis, [(i, i ^ 1) for i in range(lax.axis_size(axis))])  6.79 us
    ppermute x1, waiting for transfers between devices, reduce(): return (total, lax.ppermute(total, 'row', [(r, r ^ 2) for r in range(4)]))  5.67 us
    ppermute x5, starting transfers between devices, swap_even(): lax.ppermute(x, axis, [(i, i ^ 1) for i in range(lax.axis_size(axis))])  4.73 us
    ppermute x2, starting transfers between devices, swap_odd(): return lax.ppermute(x, axis, pairs)  1.31 us
  transfers between devices with their start and end apart: 15, of which 8 were waited for; matrix products, arithmetic and copies ran while one was open for 0% of the time, Pallas kernels for 0%

profile of v2, /device:TPU:0, one launch (start us, length us, event | category | flops | bytes accessed | tf_op | source)
XLA Modules:
  0.0 61.8 jit_solution(8002756937060600350)
XLA Ops:
  0.6 0.0 copy-start
  0.6 0.0 copy-start.1
  0.7 1.9 %shard_map.109 = (bf16[64,1280]{1,0:T(8,128)(2,1)}, bf16[128,256]{1,0:T(8,128)(2,1)}, bf16[64,1280]{1,0:T(8,128)(2,1)}) custom-call(bf16[16,32,256]{2,1,0:T(8,128)(2,1)} %region.1, bf16[8,16,512]{2,1,0:T(8,128)(2,1)} %cot.1, bf16[64,256]{1,0:T(8,128)(2,1)} %bitcast.31, bf16[64,144]{1,0:T(8,128)(2,1)} %bitcast.32, bf16[64,512]{1,0:T(8,128)(2,1)} %bitcast.30, ...), custom_call_target="tpu_custom_call" | custom-call | bytes 935936 | tf_op jit(solution)/shard_map/pallas_call | solution.py:366
  2.5 0.0 copy-start.2
  2.5 0.5 collective-permute-start
  3.1 0.7 %collective-permute-start.1 = (bf16[128,256]{1,0:T(8,128)(2,1)}, bf16[128,256]{1,0:T(8,128)(2,1)S(1)}, u32[]{:S(2)}, u32[]{:S(2)}) collective-permute-start(bf16[128,256]{1,0:T(8,128)(2,1)} %get-tuple-element.34), channel_id=1, source_target_pairs={{8,16},{16,8},{9,17},{17,9},{10,18},{18,10},{11,19},{19,11},{12,20... | collective-permute-start | bytes 196616 | tf_op jit(solution)/shard_map/ppermute | solution.py:399
  3.7 2.6 %collective-permute-start.4 = (bf16[64,1280]{1,0:T(8,128)(2,1)}, bf16[64,1280]{1,0:T(8,128)(2,1)S(1)}, u32[]{:S(2)}, u32[]{:S(2)}) collective-permute-start(bf16[64,1280]{1,0:T(8,128)(2,1)} %get-tuple-element.39.refs_0_), channel_id=1, source_target_pairs={{0,2},{1,3},{2,4},{3,5},{4,6},{5,7},{6,0},{7,1},{8,11},{9,10},{10,... | collective-permute-start | bytes 491528 | tf_op jit(solution)/shard_map/ppermute | solution.py:413
  6.4 2.6 %collective-permute-start.5 = (bf16[64,1280]{1,0:T(8,128)(2,1)}, bf16[64,1280]{1,0:T(8,128)(2,1)S(1)}, u32[]{:S(2)}, u32[]{:S(2)}) collective-permute-start(bf16[64,1280]{1,0:T(8,128)(2,1)} %get-tuple-element.39.refs_0_), channel_id=1, source_target_pairs={{0,4},{1,5},{2,6},{3,7},{4,0},{5,1},{6,2},{7,3},{8,13},{9,12},{10,... | collective-permute-start | bytes 491528 | tf_op jit(solution)/shard_map/ppermute | solution.py:413
  9.0 1.3 %collective-permute-start.6 = (bf16[64,1280]{1,0:T(8,128)(2,1)}, bf16[64,1280]{1,0:T(8,128)(2,1)S(1)}, u32[]{:S(2)}, u32[]{:S(2)}) collective-permute-start(bf16[64,1280]{1,0:T(8,128)(2,1)} %get-tuple-element.39.refs_0_), channel_id=1, source_target_pairs={{0,6},{1,7},{2,0},{3,1},{4,2},{5,3},{6,4},{7,5},{8,15},{9,14},{10,... | collective-permute-start | bytes 491528 | tf_op jit(solution)/shard_map/ppermute | solution.py:413
  10.3 0.0 collective-permute-done.core_rows
  10.3 0.0 collective-permute-done.1.far_rows
  10.3 0.0 copy-start.3
  10.3 0.9 %copy-done.3 = bf16[64,1280]{1,0:T(8,128)(2,1)S(1)} copy-done((bf16[64,1280]{1,0:T(8,128)(2,1)S(1)}, bf16[64,1280]{1,0:T(8,128)(2,1)}, u32[]{:S(2)}) %copy-start.3) | copy-done | bytes 163864
  11.3 1.6 %collective-permute-start.2 = (bf16[64,1280]{1,0:T(8,128)(2,1)S(1)}, bf16[64,1280]{1,0:T(8,128)(2,1)S(1)}, u32[]{:S(2)}, u32[]{:S(2)}) collective-permute-start(bf16[64,1280]{1,0:T(8,128)(2,1)S(1)} %get-tuple-element.36), channel_id=1, source_target_pairs={{0,1},{1,0},{2,3},{3,2},{4,5},{5,4},{6,7},{7,6},{8,9},{9,8},{10,11... | collective-permute-start | bytes 491528 | tf_op jit(solution)/shard_map/ppermute | solution.py:403
  12.9 0.7 %collective-permute-start.3 = (bf16[32,1280]{1,0:T(8,128)(2,1)S(1)}, bf16[32,1280]{1,0:T(8,128)(2,1)S(1)}, u32[]{:S(2)}, u32[]{:S(2)}) collective-permute-start(bf16[32,1280]{1,0:T(8,128)(2,1)S(1)} %get-tuple-element.37), channel_id=1, source_target_pairs={{1,2},{2,1},{3,4},{4,3},{5,6},{6,5},{9,10},{10,9},{11,12},{12,11},... | collective-permute-start | bytes 245768 | tf_op jit(solution)/shard_map/ppermute | solution.py:399
  13.5 0.0 collective-permute-done.3.edge._
  13.5 0.0 collective-permute-done.4.refs_0_
  13.5 7.0 %collective-permute-done.5.refs_1_ = bf16[64,1280]{1,0:T(8,128)(2,1)S(1)} collective-permute-done((bf16[64,1280]{1,0:T(8,128)(2,1)}, bf16[64,1280]{1,0:T(8,128)(2,1)S(1)}, u32[]{:S(2)}, u32[]{:S(2)}) %collective-permute-start.5) | collective-permute-done | bytes 163872 | tf_op jit(solution)/shard_map/ppermute | solution.py:413
  20.6 0.0 collective-permute-done.6.refs_2_
  20.6 2.4 %collective-permute-done.2.beside = bf16[64,1280]{1,0:T(8,128)(2,1)S(1)} collective-permute-done((bf16[64,1280]{1,0:T(8,128)(2,1)S(1)}, bf16[64,1280]{1,0:T(8,128)(2,1)S(1)}, u32[]{:S(2)}, u32[]{:S(2)}) %collective-permute-start.2) | collective-permute-done | bytes 163872 | tf_op jit(solution)/shard_map/ppermute | solution.py:403
  23.0 0.7 %collective-permute-start.7 = (bf16[224,1280]{1,0:T(8,128)(2,1)S(1)}, bf16[224,1280]{1,0:T(8,128)(2,1)S(1)}, u32[]{:S(2)}, u32[]{:S(2)}) collective-permute-start(bf16[224,1280]{1,0:T(8,128)(2,1)S(1)} %shard_map.112.refs_1_), channel_id=1, source_target_pairs={{0,8},{8,0},{16,24},{24,16},{1,9},{9,1},{17,25},{25,17},{2,10},{10... | collective-permute-start | bytes 1720328 | tf_op jit(solution)/shard_map/ppermute | solution.py:403
  23.8 0.0 copy-done
  23.8 0.0 copy-done.1
  23.8 0.2 shard_map.111
  24.0 1.4 %collective-permute-done.7.refs_2_ = bf16[224,1280]{1,0:T(8,128)(2,1)S(1)} collective-permute-done((bf16[224,1280]{1,0:T(8,128)(2,1)S(1)}, bf16[224,1280]{1,0:T(8,128)(2,1)S(1)}, u32[]{:S(2)}, u32[]{:S(2)}) %collective-permute-start.7) | collective-permute-done | bytes 573472 | tf_op jit(solution)/shard_map/ppermute | solution.py:403
  25.4 0.0 copy-done.2
  25.4 3.1 %shard_map.113 = (bf16[1056,512]{1,0:T(8,128)(2,1)S(1)}, f32[512,512]{1,0:T(8,128)S(1)}, bf16[160,512]{1,0:T(8,128)(2,1)S(1)}, f32[160,512]{1,0:T(8,128)S(1)}, b...) custom-call(bf16[1056,256]{1,0:T(8,128)(2,1)S(1)} %get-tuple-element.38.x, bf16[64,1280]{1,0:T(8,128)(2,1)S(1)} %copy-done.2, ...), custom_call_target="tpu_custom_call" | custom-call | flops 654311424 | bytes 7094272 | tf_op jit(solution)/shard_map/pallas_call | solution.py:366
  28.5 1.2 %shard_map.114 = (bf16[8,16,512]{2,1,0:T(8,128)(2,1)}, bf16[144,512]{1,0:T(8,128)(2,1)S(1)}, bf16[144,512]{1,0:T(8,128)(2,1)S(1)}, f32[128,256]{1,0:T(8,128)S(1)}, f32[512,768]{1,0:T(8,128)S(1)}) custom-call(bf16[1056,256]{1,0:T(8,128)(2,1)S(1)} %get-tuple-element.38.x, bf16[160,512]{1,0:T(8,128)(2,1)S(1)} %get-tuple-element.40.hidden_two, ...), custom_call_target="tpu_custom_call" | custom-call | flops 377487360 | bytes 4636672 | tf_op jit(solution)/shard_map/pallas_call | solution.py:366
  29.7 3.0 %shard_map.115 = (bf16[16,32,256]{2,1,0:T(8,128)(2,1)}, bf16[4,64,1280]{2,1,0:T(8,128)(2,1)S(1)}, f32[64,1280]{1,0:T(8,128)S(1)}, f32[64,1280]{1,0:T(8,128)S(1)}...) custom-call(bf16[1056,256]{1,0:T(8,128)(2,1)S(1)} %get-tuple-element.38.x, ...), custom_call_target="tpu_custom_call" | custom-call | flops 872415232 | bytes 9519104 | tf_op jit(solution)/shard_map/pallas_call | solution.py:366
  32.7 0.4 collective-permute-start.8
  33.0 1.7 %collective-permute-done.8 = bf16[4,64,1280]{2,1,0:T(8,128)(2,1)S(1)} collective-permute-done((bf16[4,64,1280]{2,1,0:T(8,128)(2,1)S(1)}, bf16[4,64,1280]{2,1,0:T(8,128)(2,1)S(1)}, u32[]{:S(2)}, u32[]{:S(2)}) %collective-permute-start.8) | collective-permute-done | bytes 655392 | tf_op jit(solution)/shard_map/ppermute | solution.py:403
  34.8 0.1 fusion.2
  34.9 0.7 %collective-permute-start.12 = (bf16[64,1280]{1,0:T(8,128)(2,1)S(1)}, bf16[64,1280]{1,0:T(8,128)(2,1)S(1)}, u32[]{:S(2)}, u32[]{:S(2)}) collective-permute-start(bf16[64,1280]{1,0:T(8,128)(2,1)S(1)} %get-tuple-element.63), channel_id=1, source_target_pairs={{8,9},{9,8},{10,11},{11,10},{12,13},{13,12},{14,15},{15,14},{24,25... | collective-permute-start | bytes 491528 | tf_op jit(solution)/shard_map/ppermute | solution.py:413
  35.6 2.2 %collective-permute-start.11 = (bf16[64,1280]{1,0:T(8,128)(2,1)S(1)}, bf16[64,1280]{1,0:T(8,128)(2,1)S(1)}, u32[]{:S(2)}, u32[]{:S(2)}) collective-permute-start(bf16[64,1280]{1,0:T(8,128)(2,1)S(1)} %get-tuple-element.64), channel_id=1, source_target_pairs={{0,2},{1,3},{2,4},{3,5},{4,6},{5,7},{6,0},{7,1},{8,11},{9,10},{10,... | collective-permute-start | bytes 491528 | tf_op jit(solution)/shard_map/ppermute | solution.py:413
  37.7 2.6 %collective-permute-start.10 = (bf16[64,1280]{1,0:T(8,128)(2,1)S(1)}, bf16[64,1280]{1,0:T(8,128)(2,1)S(1)}, u32[]{:S(2)}, u32[]{:S(2)}) collective-permute-start(bf16[64,1280]{1,0:T(8,128)(2,1)S(1)} %get-tuple-element.65), channel_id=1, source_target_pairs={{0,4},{1,5},{2,6},{3,7},{4,0},{5,1},{6,2},{7,3},{8,13},{9,12},{10,... | collective-permute-start | bytes 491528 | tf_op jit(solution)/shard_map/ppermute | solution.py:413
  40.3 2.4 %collective-permute-start.9 = (bf16[64,1280]{1,0:T(8,128)(2,1)S(1)}, bf16[64,1280]{1,0:T(8,128)(2,1)S(1)}, u32[]{:S(2)}, u32[]{:S(2)}) collective-permute-start(bf16[64,1280]{1,0:T(8,128)(2,1)S(1)} %get-tuple-element.62), channel_id=1, source_target_pairs={{0,6},{1,7},{2,0},{3,1},{4,2},{5,3},{6,4},{7,5},{8,15},{9,14},{10,... | collective-permute-start | bytes 491528 | tf_op jit(solution)/shard_map/ppermute | solution.py:413
  42.6 0.0 collective-permute-done.12
  42.6 0.5 collective-permute-done.11
  43.1 8.5 %collective-permute-done.10 = bf16[64,1280]{1,0:T(8,128)(2,1)S(1)} collective-permute-done((bf16[64,1280]{1,0:T(8,128)(2,1)S(1)}, bf16[64,1280]{1,0:T(8,128)(2,1)S(1)}, u32[]{:S(2)}, u32[]{:S(2)}) %collective-permute-start.10) | collective-permute-done | bytes 163872 | tf_op jit(solution)/shard_map/ppermute | solution.py:413
  51.6 0.0 collective-permute-done.9
  51.6 0.1 select_add_fusion
  51.7 1.5 %collective-permute-start.13 = (f32[64,1280]{1,0:T(8,128)S(1)}, f32[64,1280]{1,0:T(8,128)S(1)}, u32[]{:S(2)}, u32[]{:S(2)}) collective-permute-start(f32[64,1280]{1,0:T(8,128)S(1)} %select_add_fusion), channel_id=1, source_target_pairs={{0,8},{8,0},{16,24},{24,16},{1,9},{9,1},{17,25},{25,17},{2,10},{10... | collective-permute-start | bytes 983048 | tf_op jit(solution)/shard_map/ppermute | solution.py:403
  53.2 1.3 %collective-permute-done.13 = f32[64,1280]{1,0:T(8,128)S(1)} collective-permute-done((f32[64,1280]{1,0:T(8,128)S(1)}, f32[64,1280]{1,0:T(8,128)S(1)}, u32[]{:S(2)}, u32[]{:S(2)}) %collective-permute-start.13) | collective-permute-done | bytes 327712 | tf_op jit(solution)/shard_map/ppermute | solution.py:403
  54.5 0.9 %collective-permute-start.14 = (bf16[64,1280]{1,0:T(8,128)(2,1)S(1)}, bf16[64,1280]{1,0:T(8,128)(2,1)S(1)}, u32[]{:S(2)}, u32[]{:S(2)}) collective-permute-start(bf16[64,1280]{1,0:T(8,128)(2,1)S(1)} %add_convert_fusion.total), channel_id=1, source_target_pairs={{0,16},{8,24},{16,0},{24,8},{1,17},{9,25},{17,1},{25,9},{2,18},{10... | collective-permute-start | bytes 491528 | tf_op jit(solution)/shard_map/ppermute | solution.py:430
  55.4 5.7 %collective-permute-done.14.across = bf16[64,1280]{1,0:T(8,128)(2,1)S(1)} collective-permute-done((bf16[64,1280]{1,0:T(8,128)(2,1)S(1)}, bf16[64,1280]{1,0:T(8,128)(2,1)S(1)}, u32[]{:S(2)}, u32[]{:S(2)}) %collective-permute-start.14) | collective-permute-done | bytes 163872 | tf_op jit(solution)/shard_map/ppermute | solution.py:430
  61.1 0.7 %shard_map.116 = (f32[64,256]{1,0:T(8,128)}, f32[64,144]{1,0:T(8,128)}, f32[64,512]{1,0:T(8,128)}, f32[64,256]{1,0:T(8,128)}) custom-call(bf16[64,1280]{1,0:T(8,128)(2,1)S(1)} %add_convert_fusion.total, bf16[64,1280]{1,0:T(8,128)(2,1)S(1)} %collective-permute-done.14.across), custom_call_target="tpu_custom_call" | custom-call | bytes 626688 | tf_op jit(solution)/shard_map/pallas_call | solution.py:366
  (3 shorter events, 0.1 us)
Async XLA Ops:
  0.6 23.1 %copy-start = (bf16[16,32,256]{2,1,0:T(8,128)(2,1)S(1)}, bf16[16,32,256]{2,1,0:T(8,128)(2,1)}, u32[]{:S(2)}) copy-start(bf16[16,32,256]{2,1,0:T(8,128)(2,1)} %region.1) | copy-start | bytes 786436
  0.6 23.1 %copy-start.1 = (bf16[8,16,512]{2,1,0:T(8,128)(2,1)S(1)}, bf16[8,16,512]{2,1,0:T(8,128)(2,1)}, u32[]{:S(2)}) copy-start(bf16[8,16,512]{2,1,0:T(8,128)(2,1)} %cot.1) | copy-start | bytes 393220
  2.5 22.8 %copy-start.2 = (bf16[64,1280]{1,0:T(8,128)(2,1)S(1)}, bf16[64,1280]{1,0:T(8,128)(2,1)}, u32[]{:S(2)}) copy-start(bf16[64,1280]{1,0:T(8,128)(2,1)} %get-tuple-element.39.refs_0_) | copy-start | bytes 491524
  2.5 7.8 %collective-permute-start = (bf16[128,256]{1,0:T(8,128)(2,1)}, bf16[128,256]{1,0:T(8,128)(2,1)S(1)}, u32[]{:S(2)}, u32[]{:S(2)}) collective-permute-start(bf16[128,256]{1,0:T(8,128)(2,1)} %get-tuple-element.34), channel_id=1, source_target_pairs={{0,8},{8,0},{16,24},{24,16},{1,9},{9,1},{17,25},{25,17},{2,10},{10... | collective-permute-start | bytes 196616 | tf_op jit(solution)/shard_map/ppermute | solution.py:403
  3.1 7.3 %collective-permute-start.1 = (bf16[128,256]{1,0:T(8,128)(2,1)}, bf16[128,256]{1,0:T(8,128)(2,1)S(1)}, u32[]{:S(2)}, u32[]{:S(2)}) collective-permute-start(bf16[128,256]{1,0:T(8,128)(2,1)} %get-tuple-element.34), channel_id=1, source_target_pairs={{8,16},{16,8},{9,17},{17,9},{10,18},{18,10},{11,19},{19,11},{12,20... | collective-permute-start | bytes 196616 | tf_op jit(solution)/shard_map/ppermute | solution.py:399
  3.7 9.8 %collective-permute-start.4 = (bf16[64,1280]{1,0:T(8,128)(2,1)}, bf16[64,1280]{1,0:T(8,128)(2,1)S(1)}, u32[]{:S(2)}, u32[]{:S(2)}) collective-permute-start(bf16[64,1280]{1,0:T(8,128)(2,1)} %get-tuple-element.39.refs_0_), channel_id=1, source_target_pairs={{0,2},{1,3},{2,4},{3,5},{4,6},{5,7},{6,0},{7,1},{8,11},{9,10},{10,... | collective-permute-start | bytes 491528 | tf_op jit(solution)/shard_map/ppermute | solution.py:413
  6.4 14.2 %collective-permute-start.5 = (bf16[64,1280]{1,0:T(8,128)(2,1)}, bf16[64,1280]{1,0:T(8,128)(2,1)S(1)}, u32[]{:S(2)}, u32[]{:S(2)}) collective-permute-start(bf16[64,1280]{1,0:T(8,128)(2,1)} %get-tuple-element.39.refs_0_), channel_id=1, source_target_pairs={{0,4},{1,5},{2,6},{3,7},{4,0},{5,1},{6,2},{7,3},{8,13},{9,12},{10,... | collective-permute-start | bytes 491528 | tf_op jit(solution)/shard_map/ppermute | solution.py:413
  9.0 11.6 %collective-permute-start.6 = (bf16[64,1280]{1,0:T(8,128)(2,1)}, bf16[64,1280]{1,0:T(8,128)(2,1)S(1)}, u32[]{:S(2)}, u32[]{:S(2)}) collective-permute-start(bf16[64,1280]{1,0:T(8,128)(2,1)} %get-tuple-element.39.refs_0_), channel_id=1, source_target_pairs={{0,6},{1,7},{2,0},{3,1},{4,2},{5,3},{6,4},{7,5},{8,15},{9,14},{10,... | collective-permute-start | bytes 491528 | tf_op jit(solution)/shard_map/ppermute | solution.py:413
  10.3 0.9 %copy-start.3 = (bf16[64,1280]{1,0:T(8,128)(2,1)S(1)}, bf16[64,1280]{1,0:T(8,128)(2,1)}, u32[]{:S(2)}) copy-start(bf16[64,1280]{1,0:T(8,128)(2,1)} %get-tuple-element.35.draft) | copy-start | bytes 491524
  11.3 11.7 %collective-permute-start.2 = (bf16[64,1280]{1,0:T(8,128)(2,1)S(1)}, bf16[64,1280]{1,0:T(8,128)(2,1)S(1)}, u32[]{:S(2)}, u32[]{:S(2)}) collective-permute-start(bf16[64,1280]{1,0:T(8,128)(2,1)S(1)} %get-tuple-element.36), channel_id=1, source_target_pairs={{0,1},{1,0},{2,3},{3,2},{4,5},{5,4},{6,7},{7,6},{8,9},{9,8},{10,11... | collective-permute-start | bytes 491528 | tf_op jit(solution)/shard_map/ppermute | solution.py:403
  12.9 0.7 %collective-permute-start.3 = (bf16[32,1280]{1,0:T(8,128)(2,1)S(1)}, bf16[32,1280]{1,0:T(8,128)(2,1)S(1)}, u32[]{:S(2)}, u32[]{:S(2)}) collective-permute-start(bf16[32,1280]{1,0:T(8,128)(2,1)S(1)} %get-tuple-element.37), channel_id=1, source_target_pairs={{1,2},{2,1},{3,4},{4,3},{5,6},{6,5},{9,10},{10,9},{11,12},{12,11},... | collective-permute-start | bytes 245768 | tf_op jit(solution)/shard_map/ppermute | solution.py:399
  23.0 2.3 %collective-permute-start.7 = (bf16[224,1280]{1,0:T(8,128)(2,1)S(1)}, bf16[224,1280]{1,0:T(8,128)(2,1)S(1)}, u32[]{:S(2)}, u32[]{:S(2)}) collective-permute-start(bf16[224,1280]{1,0:T(8,128)(2,1)S(1)} %shard_map.112.refs_1_), channel_id=1, source_target_pairs={{0,8},{8,0},{16,24},{24,16},{1,9},{9,1},{17,25},{25,17},{2,10},{10... | collective-permute-start | bytes 1720328 | tf_op jit(solution)/shard_map/ppermute | solution.py:403
  32.7 2.1 %collective-permute-start.8 = (bf16[4,64,1280]{2,1,0:T(8,128)(2,1)S(1)}, bf16[4,64,1280]{2,1,0:T(8,128)(2,1)S(1)}, u32[]{:S(2)}, u32[]{:S(2)}) collective-permute-start(bf16[4,64,1280]{2,1,0:T(8,128)(2,1)S(1)} %get-tuple-element.54), channel_id=1, source_target_pairs={{0,8},{8,0},{16,24},{24,16},{1,9},{9,1},{17,25},{25,17},{2,10},{10... | collective-permute-start | bytes 1966088 | tf_op jit(solution)/shard_map/ppermute | solution.py:403
  34.9 7.8 %collective-permute-start.12 = (bf16[64,1280]{1,0:T(8,128)(2,1)S(1)}, bf16[64,1280]{1,0:T(8,128)(2,1)S(1)}, u32[]{:S(2)}, u32[]{:S(2)}) collective-permute-start(bf16[64,1280]{1,0:T(8,128)(2,1)S(1)} %get-tuple-element.63), channel_id=1, source_target_pairs={{8,9},{9,8},{10,11},{11,10},{12,13},{13,12},{14,15},{15,14},{24,25... | collective-permute-start | bytes 491528 | tf_op jit(solution)/shard_map/ppermute | solution.py:413
  35.6 7.5 %collective-permute-start.11 = (bf16[64,1280]{1,0:T(8,128)(2,1)S(1)}, bf16[64,1280]{1,0:T(8,128)(2,1)S(1)}, u32[]{:S(2)}, u32[]{:S(2)}) collective-permute-start(bf16[64,1280]{1,0:T(8,128)(2,1)S(1)} %get-tuple-element.64), channel_id=1, source_target_pairs={{0,2},{1,3},{2,4},{3,5},{4,6},{5,7},{6,0},{7,1},{8,11},{9,10},{10,... | collective-permute-start | bytes 491528 | tf_op jit(solution)/shard_map/ppermute | solution.py:413
  37.7 13.9 %collective-permute-start.10 = (bf16[64,1280]{1,0:T(8,128)(2,1)S(1)}, bf16[64,1280]{1,0:T(8,128)(2,1)S(1)}, u32[]{:S(2)}, u32[]{:S(2)}) collective-permute-start(bf16[64,1280]{1,0:T(8,128)(2,1)S(1)} %get-tuple-element.65), channel_id=1, source_target_pairs={{0,4},{1,5},{2,6},{3,7},{4,0},{5,1},{6,2},{7,3},{8,13},{9,12},{10,... | collective-permute-start | bytes 491528 | tf_op jit(solution)/shard_map/ppermute | solution.py:413
  40.3 11.3 %collective-permute-start.9 = (bf16[64,1280]{1,0:T(8,128)(2,1)S(1)}, bf16[64,1280]{1,0:T(8,128)(2,1)S(1)}, u32[]{:S(2)}, u32[]{:S(2)}) collective-permute-start(bf16[64,1280]{1,0:T(8,128)(2,1)S(1)} %get-tuple-element.62), channel_id=1, source_target_pairs={{0,6},{1,7},{2,0},{3,1},{4,2},{5,3},{6,4},{7,5},{8,15},{9,14},{10,... | collective-permute-start | bytes 491528 | tf_op jit(solution)/shard_map/ppermute | solution.py:413
  51.7 2.8 %collective-permute-start.13 = (f32[64,1280]{1,0:T(8,128)S(1)}, f32[64,1280]{1,0:T(8,128)S(1)}, u32[]{:S(2)}, u32[]{:S(2)}) collective-permute-start(f32[64,1280]{1,0:T(8,128)S(1)} %select_add_fusion), channel_id=1, source_target_pairs={{0,8},{8,0},{16,24},{24,16},{1,9},{9,1},{17,25},{25,17},{2,10},{10... | collective-permute-start | bytes 983048 | tf_op jit(solution)/shard_map/ppermute | solution.py:403
  54.5 6.5 %collective-permute-start.14 = (bf16[64,1280]{1,0:T(8,128)(2,1)S(1)}, bf16[64,1280]{1,0:T(8,128)(2,1)S(1)}, u32[]{:S(2)}, u32[]{:S(2)}) collective-permute-start(bf16[64,1280]{1,0:T(8,128)(2,1)S(1)} %add_convert_fusion.total), channel_id=1, source_target_pairs={{0,16},{8,24},{16,0},{24,8},{1,17},{9,25},{17,1},{25,9},{2,18},{10... | collective-permute-start | bytes 491528 | tf_op jit(solution)/shard_map/ppermute | solution.py:430

commit v3 on v2

--- a/solution.py
+++ b/solution.py
@@ -50,7 +50,9 @@
 
 
 def sigmoid(value):
-    return 1.0 / (1.0 + jnp.exp(-value))
+    below = 1.0 + jnp.exp(jnp.minimum(-value, 80.0))
+    guess = pl.reciprocal(below, approx=True)
+    return guess * (2.0 - below * guess)
 
 
 def place():
@@ -216,30 +218,23 @@
             spot = BACK.index(tap)
             back[n, :, spot * HALF : (spot + 1) * HALF] = dense
 
-    def silu_rows(at, _):
-        rows = pl.ds(pl.multiple_of(at * 16, 16), 16)
-        value = pre[rows, :]
-        hidden[rows, :] = (value * sigmoid(value)).astype(BF16)
-        return 0
-
-    def plane_rows(at, start, to):
-        source = pl.ds(pl.multiple_of(start + at * 16, 16), 16)
-        target = pl.ds(pl.multiple_of(to + at * 16, 16), 16)
-        value = pre[source, :]
-        sigma = sigmoid(value)
-        active = value * sigma
-        hidden[source, :] = active.astype(BF16)
-        slope_one[target, :] = sigma + active * (1.0 - sigma)
-
-    lax.fori_loop(0, sizes.pixels // 16, silu_rows, 0, unroll=2)
-    for i, start in enumerate(sizes.planes()):
-
-        def body(at, _, start=start, to=i * sizes.main):
-            plane_rows(at, start, to)
-            return 0
-
-        lax.fori_loop(0, sizes.main // 16, body, 0, unroll=2)
-
+    planes = sizes.planes()
+    first = 0
+    for start in sorted(planes) + [sizes.pixels]:
+        for at in range(first, start, 32):
+            rows = slice(at, min(at + 32, start))
+            value = pre[rows, :]
+            hidden[rows, :] = (value * sigmoid(value)).astype(BF16)
+        first = start + sizes.main
+    for i, start in enumerate(planes):
+        for at in range(0, sizes.main, 32):
+            rows = slice(start + at, start + at + 32)
+            value = pre[rows, :]
+            sigma = sigmoid(value)
+            active = value * sigma
+            hidden[rows, :] = active.astype(BF16)
+            rows = slice(i * sizes.main + at, i * sizes.main + at + 32)
+            slope_one[rows, :] = sigma + active * (1.0 - sigma)
     for n in range(mid // HALF):
         lanes = slice(n * HALF, (n + 1) * HALF)
         patches = []
@@ -419,7 +414,7 @@
     other = swap_even(give, "row")
     sums = [keeps[j] + other[j].astype(F32) for j in range(halves)]
     total = None
-    for j in range(halves - 1, -1, -1):
+    for j in sorted(range(halves), key=lambda j: min(j, halves - j)):
         came = cross(sums[j].astype(BF16), j).astype(F32)
         if j == 0:
             came = jnp.where(core == 0, sums[0], came)

time: 63 us -> 60.3 us (0.957); the launches traced: 61.8 us -> 60.1 us
  starting transfers between devices: 21.2 us -> 19.1 us
  waiting for transfers between devices: 28.4 us -> 30.2 us
  Pallas kernels: 10.2 us -> 8.9 us
    ppermute x7, waiting for transfers between devices: 16 us -> 17.8 us  [cross(): return lax.ppermute(x, ('row', 'col'), both(rows, cols, target))]
    ppermute x5, starting transfers between devices: 4.73 us -> 3.27 us  [swap_even(): lax.ppermute(x, axis, [(i, i ^ 1) for i in range(lax.axis_size(axis))])]
    pallas_call x8, Pallas kernels: 10.2 us -> 8.9 us  [call(): pl.pallas_call(kernel, out_shape=out_shape, in_specs=[pl.BlockSpec(memory...]
    ppermute x7, starting transfers between devices: 14.3 us -> 13.4 us  [cross(): return lax.ppermute(x, ('row', 'col'), both(rows, cols, target))]
where the time goes in v3:
time: 60.3 us; the launch traced here: 60.1 us
  waiting for transfers between devices  30.2 us (50%)
  starting transfers between devices  19.1 us (32%)
  Pallas kernels  8.9 us (15%)
  local copies, waits for them, and re-layouts  0.93 us (2%)
  between operations  0.77 us (1%)
    ppermute x7, waiting for transfers between devices, cross(): return lax.ppermute(x, ('row', 'col'), both(rows, cols, target))  17.8 us
    ppermute x7, starting transfers between devices, cross(): return lax.ppermute(x, ('row', 'col'), both(rows, cols, target))  13.4 us
    pallas_call x8, Pallas kernels, call(): pl.pallas_call(kernel, out_shape=out_shape, in_specs=[pl.BlockSpec(memory...  8.9 us
    ppermute x5, waiting for transfers between devices, swap_even(): lax.ppermute(x, axis, [(i, i ^ 1) for i in range(lax.axis_size(axis))])  7.15 us
    ppermute x1, waiting for transfers between devices, reduce(): return (total, lax.ppermute(total, 'row', [(r, r ^ 2) for r in range(4)]))  5.2 us
    ppermute x5, starting transfers between devices, swap_even(): lax.ppermute(x, axis, [(i, i ^ 1) for i in range(lax.axis_size(axis))])  3.27 us
    ppermute x2, starting transfers between devices, swap_odd(): return lax.ppermute(x, axis, pairs)  1.31 us
  transfers between devices with their start and end apart: 15, of which 8 were waited for; matrix products, arithmetic and copies ran while one was open for 0% of the time, Pallas kernels for 0%

profile of v3, /device:TPU:0, one launch (start us, length us, event | category | flops | bytes accessed | tf_op | source)
XLA Modules:
  0.0 60.1 jit_solution(445492988185909449)
XLA Ops:
  0.6 0.0 copy-start
  0.6 0.0 copy-start.1
  0.7 1.9 %shard_map.109 = (bf16[64,1280]{1,0:T(8,128)(2,1)}, bf16[128,256]{1,0:T(8,128)(2,1)}, bf16[64,1280]{1,0:T(8,128)(2,1)}) custom-call(bf16[16,32,256]{2,1,0:T(8,128)(2,1)} %region.1, bf16[8,16,512]{2,1,0:T(8,128)(2,1)} %cot.1, bf16[64,256]{1,0:T(8,128)(2,1)} %bitcast.31, bf16[64,144]{1,0:T(8,128)(2,1)} %bitcast.32, bf16[64,512]{1,0:T(8,128)(2,1)} %bitcast.30, ...), custom_call_target="tpu_custom_call" | custom-call | bytes 935936 | tf_op jit(solution)/shard_map/pallas_call | solution.py:361
  2.5 0.0 copy-start.2
  2.5 0.5 collective-permute-start
  3.1 0.7 %collective-permute-start.1 = (bf16[128,256]{1,0:T(8,128)(2,1)}, bf16[128,256]{1,0:T(8,128)(2,1)S(1)}, u32[]{:S(2)}, u32[]{:S(2)}) collective-permute-start(bf16[128,256]{1,0:T(8,128)(2,1)} %get-tuple-element.34), channel_id=1, source_target_pairs={{8,16},{16,8},{9,17},{17,9},{10,18},{18,10},{11,19},{19,11},{12,20... | collective-permute-start | bytes 196616 | tf_op jit(solution)/shard_map/ppermute | solution.py:394
  3.7 2.6 %collective-permute-start.4 = (bf16[64,1280]{1,0:T(8,128)(2,1)}, bf16[64,1280]{1,0:T(8,128)(2,1)S(1)}, u32[]{:S(2)}, u32[]{:S(2)}) collective-permute-start(bf16[64,1280]{1,0:T(8,128)(2,1)} %get-tuple-element.39.refs_0_), channel_id=1, source_target_pairs={{0,2},{1,3},{2,4},{3,5},{4,6},{5,7},{6,0},{7,1},{8,11},{9,10},{10,... | collective-permute-start | bytes 491528 | tf_op jit(solution)/shard_map/ppermute | solution.py:408
  6.4 2.6 %collective-permute-start.5 = (bf16[64,1280]{1,0:T(8,128)(2,1)}, bf16[64,1280]{1,0:T(8,128)(2,1)S(1)}, u32[]{:S(2)}, u32[]{:S(2)}) collective-permute-start(bf16[64,1280]{1,0:T(8,128)(2,1)} %get-tuple-element.39.refs_0_), channel_id=1, source_target_pairs={{0,4},{1,5},{2,6},{3,7},{4,0},{5,1},{6,2},{7,3},{8,13},{9,12},{10,... | collective-permute-start | bytes 491528 | tf_op jit(solution)/shard_map/ppermute | solution.py:408
  9.0 1.3 %collective-permute-start.6 = (bf16[64,1280]{1,0:T(8,128)(2,1)}, bf16[64,1280]{1,0:T(8,128)(2,1)S(1)}, u32[]{:S(2)}, u32[]{:S(2)}) collective-permute-start(bf16[64,1280]{1,0:T(8,128)(2,1)} %get-tuple-element.39.refs_0_), channel_id=1, source_target_pairs={{0,6},{1,7},{2,0},{3,1},{4,2},{5,3},{6,4},{7,5},{8,15},{9,14},{10,... | collective-permute-start | bytes 491528 | tf_op jit(solution)/shard_map/ppermute | solution.py:408
  10.3 0.0 collective-permute-done.core_rows
  10.3 0.0 collective-permute-done.1.far_rows
  10.3 0.0 copy-start.3
  10.3 0.9 %copy-done.3 = bf16[64,1280]{1,0:T(8,128)(2,1)S(1)} copy-done((bf16[64,1280]{1,0:T(8,128)(2,1)S(1)}, bf16[64,1280]{1,0:T(8,128)(2,1)}, u32[]{:S(2)}) %copy-start.3) | copy-done | bytes 163864
  11.3 1.6 %collective-permute-start.2 = (bf16[64,1280]{1,0:T(8,128)(2,1)S(1)}, bf16[64,1280]{1,0:T(8,128)(2,1)S(1)}, u32[]{:S(2)}, u32[]{:S(2)}) collective-permute-start(bf16[64,1280]{1,0:T(8,128)(2,1)S(1)} %get-tuple-element.36), channel_id=1, source_target_pairs={{0,1},{1,0},{2,3},{3,2},{4,5},{5,4},{6,7},{7,6},{8,9},{9,8},{10,11... | collective-permute-start | bytes 491528 | tf_op jit(solution)/shard_map/ppermute | solution.py:398
  12.9 0.7 %collective-permute-start.3 = (bf16[32,1280]{1,0:T(8,128)(2,1)S(1)}, bf16[32,1280]{1,0:T(8,128)(2,1)S(1)}, u32[]{:S(2)}, u32[]{:S(2)}) collective-permute-start(bf16[32,1280]{1,0:T(8,128)(2,1)S(1)} %get-tuple-element.37), channel_id=1, source_target_pairs={{1,2},{2,1},{3,4},{4,3},{5,6},{6,5},{9,10},{10,9},{11,12},{12,11},... | collective-permute-start | bytes 245768 | tf_op jit(solution)/shard_map/ppermute | solution.py:394
  13.5 0.0 collective-permute-done.3.edge._
  13.5 0.0 collective-permute-done.4.refs_0_
  13.5 7.0 %collective-permute-done.5.refs_1_ = bf16[64,1280]{1,0:T(8,128)(2,1)S(1)} collective-permute-done((bf16[64,1280]{1,0:T(8,128)(2,1)}, bf16[64,1280]{1,0:T(8,128)(2,1)S(1)}, u32[]{:S(2)}, u32[]{:S(2)}) %collective-permute-start.5) | collective-permute-done | bytes 163872 | tf_op jit(solution)/shard_map/ppermute | solution.py:408
  20.6 0.0 collective-permute-done.6.refs_2_
  20.6 2.4 %collective-permute-done.2.beside = bf16[64,1280]{1,0:T(8,128)(2,1)S(1)} collective-permute-done((bf16[64,1280]{1,0:T(8,128)(2,1)S(1)}, bf16[64,1280]{1,0:T(8,128)(2,1)S(1)}, u32[]{:S(2)}, u32[]{:S(2)}) %collective-permute-start.2) | collective-permute-done | bytes 163872 | tf_op jit(solution)/shard_map/ppermute | solution.py:398
  23.0 0.7 %collective-permute-start.7 = (bf16[224,1280]{1,0:T(8,128)(2,1)S(1)}, bf16[224,1280]{1,0:T(8,128)(2,1)S(1)}, u32[]{:S(2)}, u32[]{:S(2)}) collective-permute-start(bf16[224,1280]{1,0:T(8,128)(2,1)S(1)} %shard_map.112.refs_1_), channel_id=1, source_target_pairs={{0,8},{8,0},{16,24},{24,16},{1,9},{9,1},{17,25},{25,17},{2,10},{10... | collective-permute-start | bytes 1720328 | tf_op jit(solution)/shard_map/ppermute | solution.py:398
  23.8 0.0 copy-done
  23.8 0.0 copy-done.1
  23.8 0.2 shard_map.111
  24.0 1.4 %collective-permute-done.7.refs_2_ = bf16[224,1280]{1,0:T(8,128)(2,1)S(1)} collective-permute-done((bf16[224,1280]{1,0:T(8,128)(2,1)S(1)}, bf16[224,1280]{1,0:T(8,128)(2,1)S(1)}, u32[]{:S(2)}, u32[]{:S(2)}) %collective-permute-start.7) | collective-permute-done | bytes 573472 | tf_op jit(solution)/shard_map/ppermute | solution.py:398
  25.4 0.0 copy-done.2
  25.4 1.8 %shard_map.113 = (bf16[1056,512]{1,0:T(8,128)(2,1)S(1)}, f32[512,512]{1,0:T(8,128)S(1)}, bf16[160,512]{1,0:T(8,128)(2,1)S(1)}, f32[160,512]{1,0:T(8,128)S(1)}, b...) custom-call(bf16[1056,256]{1,0:T(8,128)(2,1)S(1)} %get-tuple-element.38.x, bf16[64,1280]{1,0:T(8,128)(2,1)S(1)} %copy-done.2, ...), custom_call_target="tpu_custom_call" | custom-call | flops 654311424 | bytes 7094272 | tf_op jit(solution)/shard_map/pallas_call | solution.py:361
  27.2 1.2 %shard_map.114 = (bf16[8,16,512]{2,1,0:T(8,128)(2,1)}, bf16[144,512]{1,0:T(8,128)(2,1)S(1)}, bf16[144,512]{1,0:T(8,128)(2,1)S(1)}, f32[128,256]{1,0:T(8,128)S(1)}, f32[512,768]{1,0:T(8,128)S(1)}) custom-call(bf16[1056,256]{1,0:T(8,128)(2,1)S(1)} %get-tuple-element.38.x, bf16[160,512]{1,0:T(8,128)(2,1)S(1)} %get-tuple-element.40.hidden_two, ...), custom_call_target="tpu_custom_call" | custom-call | flops 377487360 | bytes 4636672 | tf_op jit(solution)/shard_map/pallas_call | solution.py:361
  28.4 3.0 %shard_map.115 = (bf16[16,32,256]{2,1,0:T(8,128)(2,1)}, bf16[4,64,1280]{2,1,0:T(8,128)(2,1)S(1)}, f32[64,1280]{1,0:T(8,128)S(1)}, f32[64,1280]{1,0:T(8,128)S(1)}...) custom-call(bf16[1056,256]{1,0:T(8,128)(2,1)S(1)} %get-tuple-element.38.x, ...), custom_call_target="tpu_custom_call" | custom-call | flops 872415232 | bytes 9519104 | tf_op jit(solution)/shard_map/pallas_call | solution.py:361
  31.4 0.4 collective-permute-start.8
  31.8 1.7 %collective-permute-done.8 = bf16[4,64,1280]{2,1,0:T(8,128)(2,1)S(1)} collective-permute-done((bf16[4,64,1280]{2,1,0:T(8,128)(2,1)S(1)}, bf16[4,64,1280]{2,1,0:T(8,128)(2,1)S(1)}, u32[]{:S(2)}, u32[]{:S(2)}) %collective-permute-start.8) | collective-permute-done | bytes 655392 | tf_op jit(solution)/shard_map/ppermute | solution.py:398
  33.5 0.1 fusion.3
  33.6 4.2 %collective-permute-start.12 = (bf16[64,1280]{1,0:T(8,128)(2,1)S(1)}, bf16[64,1280]{1,0:T(8,128)(2,1)S(1)}, u32[]{:S(2)}, u32[]{:S(2)}) collective-permute-start(bf16[64,1280]{1,0:T(8,128)(2,1)S(1)} %get-tuple-element.63), channel_id=1, source_target_pairs={{0,4},{1,5},{2,6},{3,7},{4,0},{5,1},{6,2},{7,3},{8,13},{9,12},{10,... | collective-permute-start | bytes 491528 | tf_op jit(solution)/shard_map/ppermute | solution.py:408
  37.8 0.4 collective-permute-start.11
  38.1 1.7 %collective-permute-start.10 = (bf16[64,1280]{1,0:T(8,128)(2,1)S(1)}, bf16[64,1280]{1,0:T(8,128)(2,1)S(1)}, u32[]{:S(2)}, u32[]{:S(2)}) collective-permute-start(bf16[64,1280]{1,0:T(8,128)(2,1)S(1)} %get-tuple-element.65), channel_id=1, source_target_pairs={{0,2},{1,3},{2,4},{3,5},{4,6},{5,7},{6,0},{7,1},{8,11},{9,10},{10,... | collective-permute-start | bytes 491528 | tf_op jit(solution)/shard_map/ppermute | solution.py:408
  39.8 0.7 %collective-permute-start.9 = (bf16[64,1280]{1,0:T(8,128)(2,1)S(1)}, bf16[64,1280]{1,0:T(8,128)(2,1)S(1)}, u32[]{:S(2)}, u32[]{:S(2)}) collective-permute-start(bf16[64,1280]{1,0:T(8,128)(2,1)S(1)} %get-tuple-element.62), channel_id=1, source_target_pairs={{8,9},{9,8},{10,11},{11,10},{12,13},{13,12},{14,15},{15,14},{24,25... | collective-permute-start | bytes 491528 | tf_op jit(solution)/shard_map/ppermute | solution.py:408
  40.5 6.6 %collective-permute-done.12 = bf16[64,1280]{1,0:T(8,128)(2,1)S(1)} collective-permute-done((bf16[64,1280]{1,0:T(8,128)(2,1)S(1)}, bf16[64,1280]{1,0:T(8,128)(2,1)S(1)}, u32[]{:S(2)}, u32[]{:S(2)}) %collective-permute-start.12) | collective-permute-done | bytes 163872 | tf_op jit(solution)/shard_map/ppermute | solution.py:408
  47.1 4.1 %collective-permute-done.11 = bf16[64,1280]{1,0:T(8,128)(2,1)S(1)} collective-permute-done((bf16[64,1280]{1,0:T(8,128)(2,1)S(1)}, bf16[64,1280]{1,0:T(8,128)(2,1)S(1)}, u32[]{:S(2)}, u32[]{:S(2)}) %collective-permute-start.11) | collective-permute-done | bytes 163872 | tf_op jit(solution)/shard_map/ppermute | solution.py:408
  51.2 0.0 collective-permute-done.10
  51.2 0.0 collective-permute-done.9
  51.2 0.1 convert_add_fusion.4
  51.4 0.1 collective-permute-start.13
  51.4 1.6 %collective-permute-done.13 = f32[64,1280]{1,0:T(8,128)S(1)} collective-permute-done((f32[64,1280]{1,0:T(8,128)S(1)}, f32[64,1280]{1,0:T(8,128)S(1)}, u32[]{:S(2)}, u32[]{:S(2)}) %collective-permute-start.13) | collective-permute-done | bytes 327712 | tf_op jit(solution)/shard_map/ppermute | solution.py:398
  53.1 1.1 %collective-permute-start.14 = (bf16[64,1280]{1,0:T(8,128)(2,1)S(1)}, bf16[64,1280]{1,0:T(8,128)(2,1)S(1)}, u32[]{:S(2)}, u32[]{:S(2)}) collective-permute-start(bf16[64,1280]{1,0:T(8,128)(2,1)S(1)} %add_convert_fusion.total), channel_id=1, source_target_pairs={{0,16},{8,24},{16,0},{24,8},{1,17},{9,25},{17,1},{25,9},{2,18},{10... | collective-permute-start | bytes 491528 | tf_op jit(solution)/shard_map/ppermute | solution.py:425
  54.2 5.2 %collective-permute-done.14.across = bf16[64,1280]{1,0:T(8,128)(2,1)S(1)} collective-permute-done((bf16[64,1280]{1,0:T(8,128)(2,1)S(1)}, bf16[64,1280]{1,0:T(8,128)(2,1)S(1)}, u32[]{:S(2)}, u32[]{:S(2)}) %collective-permute-start.14) | collective-permute-done | bytes 163872 | tf_op jit(solution)/shard_map/ppermute | solution.py:425
  59.4 0.7 %shard_map.116 = (f32[64,256]{1,0:T(8,128)}, f32[64,144]{1,0:T(8,128)}, f32[64,512]{1,0:T(8,128)}, f32[64,256]{1,0:T(8,128)}) custom-call(bf16[64,1280]{1,0:T(8,128)(2,1)S(1)} %add_convert_fusion.total, bf16[64,1280]{1,0:T(8,128)(2,1)S(1)} %collective-permute-done.14.across), custom_call_target="tpu_custom_call" | custom-call | bytes 626688 | tf_op jit(solution)/shard_map/pallas_call | solution.py:361
  (3 shorter events, 0.1 us)
Async XLA Ops:
  0.6 23.1 %copy-start = (bf16[16,32,256]{2,1,0:T(8,128)(2,1)S(1)}, bf16[16,32,256]{2,1,0:T(8,128)(2,1)}, u32[]{:S(2)}) copy-start(bf16[16,32,256]{2,1,0:T(8,128)(2,1)} %region.1) | copy-start | bytes 786436
  0.6 23.1 %copy-start.1 = (bf16[8,16,512]{2,1,0:T(8,128)(2,1)S(1)}, bf16[8,16,512]{2,1,0:T(8,128)(2,1)}, u32[]{:S(2)}) copy-start(bf16[8,16,512]{2,1,0:T(8,128)(2,1)} %cot.1) | copy-start | bytes 393220
  2.5 22.8 %copy-start.2 = (bf16[64,1280]{1,0:T(8,128)(2,1)S(1)}, bf16[64,1280]{1,0:T(8,128)(2,1)}, u32[]{:S(2)}) copy-start(bf16[64,1280]{1,0:T(8,128)(2,1)} %get-tuple-element.39.refs_0_) | copy-start | bytes 491524
  2.5 7.8 %collective-permute-start = (bf16[128,256]{1,0:T(8,128)(2,1)}, bf16[128,256]{1,0:T(8,128)(2,1)S(1)}, u32[]{:S(2)}, u32[]{:S(2)}) collective-permute-start(bf16[128,256]{1,0:T(8,128)(2,1)} %get-tuple-element.34), channel_id=1, source_target_pairs={{0,8},{8,0},{16,24},{24,16},{1,9},{9,1},{17,25},{25,17},{2,10},{10... | collective-permute-start | bytes 196616 | tf_op jit(solution)/shard_map/ppermute | solution.py:398
  3.1 7.3 %collective-permute-start.1 = (bf16[128,256]{1,0:T(8,128)(2,1)}, bf16[128,256]{1,0:T(8,128)(2,1)S(1)}, u32[]{:S(2)}, u32[]{:S(2)}) collective-permute-start(bf16[128,256]{1,0:T(8,128)(2,1)} %get-tuple-element.34), channel_id=1, source_target_pairs={{8,16},{16,8},{9,17},{17,9},{10,18},{18,10},{11,19},{19,11},{12,20... | collective-permute-start | bytes 196616 | tf_op jit(solution)/shard_map/ppermute | solution.py:394
  3.7 9.8 %collective-permute-start.4 = (bf16[64,1280]{1,0:T(8,128)(2,1)}, bf16[64,1280]{1,0:T(8,128)(2,1)S(1)}, u32[]{:S(2)}, u32[]{:S(2)}) collective-permute-start(bf16[64,1280]{1,0:T(8,128)(2,1)} %get-tuple-element.39.refs_0_), channel_id=1, source_target_pairs={{0,2},{1,3},{2,4},{3,5},{4,6},{5,7},{6,0},{7,1},{8,11},{9,10},{10,... | collective-permute-start | bytes 491528 | tf_op jit(solution)/shard_map/ppermute | solution.py:408
  6.4 14.2 %collective-permute-start.5 = (bf16[64,1280]{1,0:T(8,128)(2,1)}, bf16[64,1280]{1,0:T(8,128)(2,1)S(1)}, u32[]{:S(2)}, u32[]{:S(2)}) collective-permute-start(bf16[64,1280]{1,0:T(8,128)(2,1)} %get-tuple-element.39.refs_0_), channel_id=1, source_target_pairs={{0,4},{1,5},{2,6},{3,7},{4,0},{5,1},{6,2},{7,3},{8,13},{9,12},{10,... | collective-permute-start | bytes 491528 | tf_op jit(solution)/shard_map/ppermute | solution.py:408
  9.0 11.6 %collective-permute-start.6 = (bf16[64,1280]{1,0:T(8,128)(2,1)}, bf16[64,1280]{1,0:T(8,128)(2,1)S(1)}, u32[]{:S(2)}, u32[]{:S(2)}) collective-permute-start(bf16[64,1280]{1,0:T(8,128)(2,1)} %get-tuple-element.39.refs_0_), channel_id=1, source_target_pairs={{0,6},{1,7},{2,0},{3,1},{4,2},{5,3},{6,4},{7,5},{8,15},{9,14},{10,... | collective-permute-start | bytes 491528 | tf_op jit(solution)/shard_map/ppermute | solution.py:408
  10.3 0.9 %copy-start.3 = (bf16[64,1280]{1,0:T(8,128)(2,1)S(1)}, bf16[64,1280]{1,0:T(8,128)(2,1)}, u32[]{:S(2)}) copy-start(bf16[64,1280]{1,0:T(8,128)(2,1)} %get-tuple-element.35.draft) | copy-start | bytes 491524
  11.3 11.7 %collective-permute-start.2 = (bf16[64,1280]{1,0:T(8,128)(2,1)S(1)}, bf16[64,1280]{1,0:T(8,128)(2,1)S(1)}, u32[]{:S(2)}, u32[]{:S(2)}) collective-permute-start(bf16[64,1280]{1,0:T(8,128)(2,1)S(1)} %get-tuple-element.36), channel_id=1, source_target_pairs={{0,1},{1,0},{2,3},{3,2},{4,5},{5,4},{6,7},{7,6},{8,9},{9,8},{10,11... | collective-permute-start | bytes 491528 | tf_op jit(solution)/shard_map/ppermute | solution.py:398
  12.9 0.7 %collective-permute-start.3 = (bf16[32,1280]{1,0:T(8,128)(2,1)S(1)}, bf16[32,1280]{1,0:T(8,128)(2,1)S(1)}, u32[]{:S(2)}, u32[]{:S(2)}) collective-permute-start(bf16[32,1280]{1,0:T(8,128)(2,1)S(1)} %get-tuple-element.37), channel_id=1, source_target_pairs={{1,2},{2,1},{3,4},{4,3},{5,6},{6,5},{9,10},{10,9},{11,12},{12,11},... | collective-permute-start | bytes 245768 | tf_op jit(solution)/shard_map/ppermute | solution.py:394
  23.0 2.3 %collective-permute-start.7 = (bf16[224,1280]{1,0:T(8,128)(2,1)S(1)}, bf16[224,1280]{1,0:T(8,128)(2,1)S(1)}, u32[]{:S(2)}, u32[]{:S(2)}) collective-permute-start(bf16[224,1280]{1,0:T(8,128)(2,1)S(1)} %shard_map.112.refs_1_), channel_id=1, source_target_pairs={{0,8},{8,0},{16,24},{24,16},{1,9},{9,1},{17,25},{25,17},{2,10},{10... | collective-permute-start | bytes 1720328 | tf_op jit(solution)/shard_map/ppermute | solution.py:398
  31.4 2.1 %collective-permute-start.8 = (bf16[4,64,1280]{2,1,0:T(8,128)(2,1)S(1)}, bf16[4,64,1280]{2,1,0:T(8,128)(2,1)S(1)}, u32[]{:S(2)}, u32[]{:S(2)}) collective-permute-start(bf16[4,64,1280]{2,1,0:T(8,128)(2,1)S(1)} %get-tuple-element.54), channel_id=1, source_target_pairs={{0,8},{8,0},{16,24},{24,16},{1,9},{9,1},{17,25},{25,17},{2,10},{10... | collective-permute-start | bytes 1966088 | tf_op jit(solution)/shard_map/ppermute | solution.py:398
  33.6 13.5 %collective-permute-start.12 = (bf16[64,1280]{1,0:T(8,128)(2,1)S(1)}, bf16[64,1280]{1,0:T(8,128)(2,1)S(1)}, u32[]{:S(2)}, u32[]{:S(2)}) collective-permute-start(bf16[64,1280]{1,0:T(8,128)(2,1)S(1)} %get-tuple-element.63), channel_id=1, source_target_pairs={{0,4},{1,5},{2,6},{3,7},{4,0},{5,1},{6,2},{7,3},{8,13},{9,12},{10,... | collective-permute-start | bytes 491528 | tf_op jit(solution)/shard_map/ppermute | solution.py:408
  37.8 13.5 %collective-permute-start.11 = (bf16[64,1280]{1,0:T(8,128)(2,1)S(1)}, bf16[64,1280]{1,0:T(8,128)(2,1)S(1)}, u32[]{:S(2)}, u32[]{:S(2)}) collective-permute-start(bf16[64,1280]{1,0:T(8,128)(2,1)S(1)} %get-tuple-element.64), channel_id=1, source_target_pairs={{0,6},{1,7},{2,0},{3,1},{4,2},{5,3},{6,4},{7,5},{8,15},{9,14},{10,... | collective-permute-start | bytes 491528 | tf_op jit(solution)/shard_map/ppermute | solution.py:408
  38.1 13.1 %collective-permute-start.10 = (bf16[64,1280]{1,0:T(8,128)(2,1)S(1)}, bf16[64,1280]{1,0:T(8,128)(2,1)S(1)}, u32[]{:S(2)}, u32[]{:S(2)}) collective-permute-start(bf16[64,1280]{1,0:T(8,128)(2,1)S(1)} %get-tuple-element.65), channel_id=1, source_target_pairs={{0,2},{1,3},{2,4},{3,5},{4,6},{5,7},{6,0},{7,1},{8,11},{9,10},{10,... | collective-permute-start | bytes 491528 | tf_op jit(solution)/shard_map/ppermute | solution.py:408
  39.8 11.4 %collective-permute-start.9 = (bf16[64,1280]{1,0:T(8,128)(2,1)S(1)}, bf16[64,1280]{1,0:T(8,128)(2,1)S(1)}, u32[]{:S(2)}, u32[]{:S(2)}) collective-permute-start(bf16[64,1280]{1,0:T(8,128)(2,1)S(1)} %get-tuple-element.62), channel_id=1, source_target_pairs={{8,9},{9,8},{10,11},{11,10},{12,13},{13,12},{14,15},{15,14},{24,25... | collective-permute-start | bytes 491528 | tf_op jit(solution)/shard_map/ppermute | solution.py:408
  51.4 1.7 %collective-permute-start.13 = (f32[64,1280]{1,0:T(8,128)S(1)}, f32[64,1280]{1,0:T(8,128)S(1)}, u32[]{:S(2)}, u32[]{:S(2)}) collective-permute-start(f32[64,1280]{1,0:T(8,128)S(1)} %convert_add_fusion.4), channel_id=1, source_target_pairs={{0,8},{8,0},{16,24},{24,16},{1,9},{9,1},{17,25},{25,17},{2,10},{10... | collective-permute-start | bytes 983048 | tf_op jit(solution)/shard_map/ppermute | solution.py:398
  53.1 6.3 %collective-permute-start.14 = (bf16[64,1280]{1,0:T(8,128)(2,1)S(1)}, bf16[64,1280]{1,0:T(8,128)(2,1)S(1)}, u32[]{:S(2)}, u32[]{:S(2)}) collective-permute-start(bf16[64,1280]{1,0:T(8,128)(2,1)S(1)} %add_convert_fusion.total), channel_id=1, source_target_pairs={{0,16},{8,24},{16,0},{24,8},{1,17},{9,25},{17,1},{25,9},{2,18},{10... | collective-permute-start | bytes 491528 | tf_op jit(solution)/shard_map/ppermute | solution.py:425

commit v4 on v3

--- a/solution.py
+++ b/solution.py
@@ -60,22 +60,33 @@
     return col // 2, lax.rem(col, 2), lax.rem(lax.axis_index("row"), 2)
 
 
-def pieces(halves, own, passed, swapped):
+def fold(block):
+    parts = [
+        pltpu.roll(block[at : at + GW], at, 1) if at else block[:GW]
+        for at in range(0, block.shape[0], GW)
+    ]
+    return sum(parts[1:], parts[0])
+
+
+def unfold(tail, rows):
+    return [pltpu.roll(tail, (128 - at) % 128, 1) if at else tail for at in range(0, rows, GW)]
+
+
+def pieces(halves, shard, own, passed, swapped, beside):
     h, low, core = place()
-    shard = own.shape[0]
+    length = own.shape[0]
     flips = (low + core - 2 * low * core, 1 - low - core + 2 * low * core)
     found = [(own, (2 * h + low) * shard)]
     for ref, flip in zip((passed, swapped), flips, strict=True):
         for j in range(1, halves):
             spot = 2 * lax.rem(h - j + halves, halves) + flip
-            found.append((ref.at[(j - 1) * shard : j * shard], spot * shard))
-    share = passed.shape[0] - (halves - 1) * shard
-    beside = (2 * h + 1 - low) * shard
-    if share == shard:
-        return found + [(passed.at[(halves - 1) * shard :], beside)]
+            found.append((ref.at[(j - 1) * length : j * length], spot * shard))
+    first = (halves - 1) * length
+    share = passed.shape[0] - first
     for ref, part in ((passed, core), (swapped, 1 - core)):
-        found.append((ref.at[(halves - 1) * shard :], beside + part * share))
-    return found
+        rows = pl.ds(pl.multiple_of(part * (length - share), 16), share)
+        beside[rows, :] = ref[first : first + share]
+    return found + [(beside, (2 * h + 1 - low) * shard)]
 
 
 def send_kernel(sizes, *refs):
@@ -91,12 +102,15 @@
     region, cot, reduce_t, group_t, expand_t, short_t = local
     shard, taps = group_t.shape
     cin, mid = reduce_t.shape[1], expand_t.shape[1]
-    last = cin + 256 + mid
+    tiles = [reduce_t[:, at : at + 128] for at in range(0, cin, 128)]
+    tiles.append(group_t[:, :128])
+    tiles += [expand_t[:, at : at + 128] for at in range(0, mid, 128)]
+    tiles += [short_t[:, at : at + 128] for at in range(0, cin, 128)]
+    for i, tile in enumerate(tiles):
+        weights[i * shard : (i + 1) * shard] = tile
     pad = jnp.zeros((shard, 256 - taps), BF16)
-    weights[:, :cin] = reduce_t[...]
-    weights[:, cin : cin + 256] = jnp.concatenate([group_t[...], pad], axis=1)
-    weights[:, cin + 256 : last] = expand_t[...]
-    weights[:, last:] = short_t[...]
+    rest = jnp.concatenate([group_t[...], pad], axis=1)[:, 128:].astype(F32)
+    weights[len(tiles) * shard :] = fold(rest).astype(BF16)
     tc, half = sizes.tc, cot.shape[2] // 2
     for i, r in enumerate((sizes.tr - 1, 0, 1)):
         outer[i * tc : (i + 1) * tc] = region[r]
@@ -104,19 +118,31 @@
     outer[3 * tc + sizes.hc :] = cot[0, :, half:]
     cols[...] = jnp.zeros_like(cols)
     for r in range(sizes.tr):
-        head, tail = region[r, :16].astype(F32), region[r, tc - 16 :].astype(F32)
-        cols[r + 1 : r + 2, :cin] = head[0:1]
-        cols[r + 1 : r + 2, cin : 2 * cin] = head[1:2]
-        cols[r + 1 : r + 2, 2 * cin : 3 * cin] = tail[15:16]
+        put_columns(cols, r + 1, region[r, :16], region[r, tc - 16 :])
     for i in range(sizes.hr):
-        cols[i : i + 1, 3 * cin :] = cot[i, :16].astype(F32)[0:1]
-    share = draft.shape[0] - 32
-    if share == shard:
-        draft[:share] = weights[...]
-    else:
-        core = lax.rem(lax.axis_index("row"), 2)
-        draft[:share] = weights[pl.ds(pl.multiple_of(core * share, share), share), :]
+        put_cotangent(cols, i, cot[i, :16])
+    share = draft.shape[0] - cols.shape[0]
+    core = lax.rem(lax.axis_index("row"), 2)
+    first = pl.multiple_of(core * (weights.shape[0] - share), 16)
+    draft[:share] = weights[pl.ds(first, share), :]
     draft[share:] = cols[...].astype(BF16)
+
+
+def put_columns(cols, row, head, tail):
+    head, tail = head.astype(F32), tail.astype(F32)
+    tiles = head.shape[1] // 128
+    for i, pixel in enumerate((head[0:1], head[1:2], tail[15:16])):
+        for v in range(tiles):
+            at = (i * tiles + v) * 32 + row
+            cols[at : at + 1] = pixel[:, v * 128 : (v + 1) * 128]
+
+
+def put_cotangent(cols, row, head):
+    pixel = head.astype(F32)[0:1]
+    tiles = pixel.shape[1] // 128
+    for v in range(tiles):
+        at = cols.shape[0] - (tiles - v) * 16 + row
+        cols[at : at + 1] = pixel[:, v * 128 : (v + 1) * 128]
 
 
 def choose(first, one, other, to_one, to_other):
@@ -133,38 +159,35 @@
 
 def columns_kernel(sizes, core_rows, far_rows, draft, beside, edge, north, south, cols):
     choose(lax.rem(lax.axis_index("row"), 2) == 0, core_rows, far_rows, south, north)
-    cin, tc, tr = core_rows.shape[1], sizes.tc, sizes.tr
-    share = draft.shape[0] - 32
+    tc, tr, hc = sizes.tc, sizes.tr, sizes.hc
+    share = draft.shape[0] - cols.shape[0]
     beside[:share] = draft[:share]
     cols[...] = draft[share:].astype(F32)
     for to, rows, at in ((0, north, 0), (tr + 1, south, tc), (tr + 2, south, 2 * tc)):
-        head = rows[at : at + 16].astype(F32)
-        tail = rows[at + tc - 16 : at + tc].astype(F32)
-        cols[to : to + 1, :cin] = head[0:1]
-        cols[to : to + 1, cin : 2 * cin] = head[1:2]
-        cols[to : to + 1, 2 * cin : 3 * cin] = tail[15:16]
-    for i in range(2):
-        at, lanes = 3 * tc + i * sizes.hc, slice((3 + i) * cin, (4 + i) * cin)
-        cols[sizes.hr : sizes.hr + 1, lanes] = south[at : at + 16].astype(F32)[0:1]
+        put_columns(cols, to, rows[at : at + 16], rows[at + tc - 16 : at + tc])
+    ends = [south[at : at + 16] for at in (3 * tc, 3 * tc + hc)]
+    put_cotangent(cols, sizes.hr, jnp.concatenate(ends, axis=1))
     beside[share:] = cols[...].astype(BF16)
     edge[...] = cols[...].astype(BF16)
 
 
-def pass_kernel(beside, _, *refs):
+def pass_kernel(beside, edge, *refs):
     far, passed = refs[:-1], refs[-1]
-    shard, share = far[0].shape[0], beside.shape[0] - 32
+    length, share = far[0].shape[0], beside.shape[0] - edge.shape[0]
     for j, block in enumerate(far):
-        passed[j * shard : (j + 1) * shard] = block[...]
-    passed[len(far) * shard :] = beside[:share]
+        passed[j * length : (j + 1) * length] = block[...]
+    passed[len(far) * length :] = beside[:share]
 
 
 def spread_kernel(sizes, region, cot, core_rows, far_rows, beside, edge, *refs):
-    x, cot_all, north, south, west, east, left, right, ext, cols = refs
+    x, cot_all, north, south, west, east, left, ext, cols = refs
     choose(lax.rem(lax.axis_index("row"), 2) == 0, core_rows, far_rows, south, north)
-    choose(lax.rem(lax.axis_index("col"), 2) == 0, beside.at[beside.shape[0] - 32 :], edge, east, west)
+    choose(lax.rem(lax.axis_index("col"), 2) == 0, beside.at[beside.shape[0] - edge.shape[0] :], edge, east, west)
     cin, tc, tr, hc = region.shape[2], sizes.tc, sizes.tr, sizes.hc
-    left[...] = west[:, 2 * cin : 3 * cin].astype(F32)
-    right[...] = east[:, : 2 * cin].astype(F32)
+    tiles = cin // 128
+    for v in range(tiles):
+        at = (2 * tiles + v) * 32
+        left[:, v * 128 : (v + 1) * 128] = west[at : at + 32].astype(F32)
     cols[...] = jnp.zeros_like(cols)
     for v in range(cin // 128):
         lanes = slice(v * 128, (v + 1) * 128)
@@ -179,7 +202,8 @@
             ext[v, r, 7:8] = left[r : r + 1, lanes]
             cols[0, v, r : r + 1] = ext[v, r, 7 + tc : 8 + tc]
         for b in (1, 2):
-            cols[b, v, :32] = right[:, (b - 1) * cin + v * 128 : (b - 1) * cin + (v + 1) * 128]
+            at = ((b - 1) * tiles + v) * 32
+            cols[b, v, :32] = east[at : at + 32].astype(F32)
         for b in range(3):
             base = b * sizes.band
             for r in list(range(0, tr + 3, 2)) + list(range(1, tr + 3, 2)):
@@ -193,18 +217,28 @@
     cot_all[: sizes.main] = cot[...].reshape(sizes.main, 2 * half)
     cot_all[sizes.main : sizes.wide, :half] = south[3 * tc : 3 * tc + hc]
     cot_all[sizes.main : sizes.wide, half:] = south[3 * tc + hc :]
-    cot_all[sizes.wide :] = east[:16, 3 * cin :]
+    for v in range(2 * half // 128):
+        at = 3 * tiles * 32 + v * 16
+        cot_all[sizes.wide :, v * 128 : (v + 1) * 128] = east[at : at + 16]
 
 
 def first_kernel(sizes, halves, x, *refs):
     hidden, slope_one, hidden_two, slope_two, back, reduce_t = refs[3:9]
-    pre, group_t, group, front, pre_two = refs[9:]
+    pre, group_t, group, front, pre_two, beside = refs[9:]
     cin = reduce_t.shape[1]
     mid = reduce_t.shape[0]
-    for block, first in pieces(halves, *refs[:3]):
-        rows = pl.ds(pl.multiple_of(first, 16), block.shape[0])
-        reduce_t[rows, :] = block[:, :cin]
-        group_t[rows, :] = block[:, cin : cin + 256]
+    shard = mid // (2 * halves)
+    lane = lax.broadcasted_iota(jnp.int32, (GW, 128), 1)
+    for block, first in pieces(halves, shard, *refs[:3], beside):
+        rows = pl.ds(pl.multiple_of(first, 16), shard)
+        for v in range(cin // 128):
+            reduce_t[rows, v * 128 : (v + 1) * 128] = block[v * shard : (v + 1) * shard]
+        at = cin // 128 * shard
+        group_t[rows, :128] = block[at : at + shard]
+        tail = block[block.shape[0] - GW :].astype(F32)
+        for i, part in enumerate(unfold(tail, shard)):
+            rows = pl.ds(pl.multiple_of(first + i * GW, 16), GW)
+            group_t[rows, 128:] = jnp.where(lane < GW, part, 0.0).astype(BF16)
     pre[...] = dot(x[...], reduce_t[...], ((1,), (1,)))
     group[...] = group_t[...].astype(F32).T.astype(BF16)
     row_group = lax.broadcasted_iota(jnp.int32, (HALF, HALF), 0) // GW
@@ -253,26 +287,35 @@
     slope_two[...] = sigma + active * (1.0 - sigma)
 
 
-def split_out(halves, total, shard, keeps, give):
+def split_out(halves, total, shard, rest, keeps, give):
+    tiles = [at for at in range(0, total.shape[1], 128) if at != rest]
     h, low, core = place()
     keep = low + core - 2 * low * core
     for j in range(halves):
         base = 2 * lax.rem(h + j, halves)
         mine = pl.ds(pl.multiple_of((base + keep) * shard, shard), shard)
         theirs = pl.ds(pl.multiple_of((base + 1 - keep) * shard, shard), shard)
-        keeps[j][...] = total[mine, :]
-        give[j] = total[theirs, :].astype(BF16)
+        for i, at in enumerate(tiles):
+            slab = slice(i * shard, (i + 1) * shard)
+            keeps[j][slab] = total[mine, at : at + 128]
+            give[j, slab] = total[theirs, at : at + 128].astype(BF16)
+        keeps[j][len(tiles) * shard :] = fold(total[mine, rest : rest + 128])
+        give[j, len(tiles) * shard :] = fold(total[theirs, rest : rest + 128]).astype(BF16)
 
 
 def second_kernel(sizes, halves, x, hidden_two, slope_two, cot, *refs):
-    block_out, grad_two, grad_side, short_back, total, expand_t, short_t, shift = refs[3:]
-    skip = refs[0].shape[1] - total.shape[1]
+    block_out, grad_two, grad_side, short_back, total, expand_t, short_t, shift, beside = refs[3:]
     mid = expand_t.shape[1]
     width = expand_t.shape[0]
-    for block, first in pieces(halves, *refs[:3]):
-        rows = pl.ds(pl.multiple_of(first, 16), block.shape[0])
-        expand_t[rows, :] = block[:, skip : skip + mid]
-        short_t[rows, :] = block[:, skip + mid :]
+    shard = width // (2 * halves)
+    cin = short_t.shape[1]
+    for block, first in pieces(halves, shard, *refs[:3], beside):
+        rows = pl.ds(pl.multiple_of(first, 16), shard)
+        at = (cin // 128 + 1) * shard
+        for ref in (expand_t, short_t):
+            for v in range(ref.shape[1] // 128):
+                ref[rows, v * 128 : (v + 1) * 128] = block[at : at + shard]
+                at += shard
     at, side = sizes.tap(4), sizes.tap_side(4)
     strided = jnp.concatenate([x[at : at + sizes.wide], x[side : side + 16]], axis=0)
     summed = dot(hidden_two[...], expand_t[...], ((1,), (1,))) + dot(
@@ -306,7 +349,7 @@
     total, grad_one, planes, spread_out = refs[2 + halves :]
     mid, cin = reduce_t.shape
     main, hc = sizes.main, sizes.hc
-    shard = keeps[0].shape[0]
+    shard = mid // (2 * halves)
     down = slice(hc, hc + main)
     own = slice(0, main)
     for n in range(mid // HALF):
@@ -342,7 +385,7 @@
                     total[rows, cin : cin + 128] = sums[q]
                     total[rows, cin + 128 : cin + 256] = jnp.where(lane == 0, block, 0.0)
     total[:, cin + 256 :] = late[...]
-    split_out(halves, total, shard, keeps, give)
+    split_out(halves, total, shard, cin + 128, keeps, give)
     planes[...] = dot(grad_one[...], reduce_t[...])
     planes[:main] += short_back[...]
     for i in range(4):
@@ -371,10 +414,15 @@
 
 def finish_kernel(total, across, *outs):
     value = total[...].astype(F32) + across[...].astype(F32)
+    shard = outs[0].shape[0]
     at = 0
-    for out, skip in zip(outs, (0, 256 - outs[1].shape[1], 0, 0), strict=True):
-        out[...] = value[:, at : at + out.shape[1]]
-        at += out.shape[1] + skip
+    for out in outs:
+        for v in range(out.shape[1] // 128):
+            out[:, v * 128 : (v + 1) * 128] = value[at : at + shard]
+            at += shard
+    rest = outs[1].shape[1] - 128
+    for i, part in enumerate(unfold(value[at:], shard)):
+        outs[1][i * GW : (i + 1) * GW, 128:] = part[:, :rest]
 
 
 def both(rows, cols, target):
@@ -433,8 +481,9 @@
     width = shard * lax.axis_size("col")
     taps = group_weight.shape[0]
     early, late = cin + 256, mid + cin
-    halo = 3 * cin + width
-    share = shard // 2 if shard % 32 == 0 else shard
+    length = (early + late) // 128 * shard - shard + GW
+    share = (length + 31) // 32 * 16
+    halo = 3 * cin // 128 * 32 + width // 128 * 16
 
     def shape(dims, dtype=BF16):
         return jax.ShapeDtypeStruct(dims, dtype)
@@ -448,11 +497,11 @@
     weights, outer, draft = call(
         functools.partial(send_kernel, sizes),
         (
-            shape((shard, early + late)),
+            shape((length, 128)),
             shape((4 * tile_cols, cin)),
-            shape((share + 32, halo)),
+            shape((share + halo, 128)),
         ),
-        [scratch(32, halo)]
+        [scratch(halo, 128)]
         + [scratch(*given.shape, dtype=BF16) for given in inputs]
         + [pltpu.SemaphoreType.DMA((len(inputs),))],
         *inputs,
@@ -465,8 +514,8 @@
     rows_scratch = [scratch(4 * tile_cols, cin, dtype=BF16)] * 2
     beside, edge = call(
         functools.partial(columns_kernel, sizes),
-        (shape(draft.shape), shape((32, halo))),
-        rows_scratch + [scratch(32, halo)],
+        (shape(draft.shape), shape((halo, 128))),
+        rows_scratch + [scratch(halo, 128)],
         core_rows, far_rows, draft,
     )
     beside, edge = swap_even(beside, "col"), swap_odd(edge, "col")
@@ -475,10 +524,9 @@
         (shape((sizes.pixels, cin)), shape((sizes.out, width))),
         rows_scratch
         + [
-            scratch(32, halo, dtype=BF16),
-            scratch(32, halo, dtype=BF16),
+            scratch(halo, 128, dtype=BF16),
+            scratch(halo, 128, dtype=BF16),
             scratch(32, cin),
-            scratch(32, 2 * cin),
             scratch(cin // 128, tile_rows + 3, 8 + tile_cols, 128),
             scratch(3, cin // 128, 40, 128),
         ],
@@ -486,7 +534,7 @@
     )
     passed = call(
         pass_kernel,
-        shape(((halves - 1) * shard + share, early + late)),
+        shape(((halves - 1) * length + share, 128)),
         [],
         beside, edge, *far,
     )
@@ -507,6 +555,7 @@
             scratch(256, mid, dtype=BF16),
             scratch(mid // HALF, TAPS * HALF, HALF, dtype=BF16),
             scratch(sizes.out, mid),
+            scratch(length, 128, dtype=BF16),
         ],
         x, *blocks,
         flops=2 * sizes.pixels * cin * mid + 2 * sizes.out * TAPS * HALF * mid,
@@ -524,14 +573,15 @@
             scratch(width, mid, dtype=BF16),
             scratch(width, cin, dtype=BF16),
             scratch(sizes.hr + 1, 24, mid),
+            scratch(length, 128, dtype=BF16),
         ],
         x, hidden_two, slope_two, cot_all, *blocks,
         flops=6 * sizes.out * width * (mid + cin),
     )
     region_grad, give, *keeps = call(
         functools.partial(third_kernel, sizes, halves),
-        (shape(region.shape), shape((halves, shard, early + late)))
-        + (shape((shard, early + late), F32),) * halves,
+        (shape(region.shape), shape((halves, length, 128)))
+        + (shape((length, 128), F32),) * halves,
         [
             scratch(mid, early + late),
             scratch(4 * sizes.main, mid, dtype=BF16),

time: 60.3 us -> 57.8 us (0.959)
  waiting for transfers between devices: 30.2 us -> 28.3 us
  starting transfers between devices: 19.1 us -> 18.2 us
    ppermute x7, waiting for transfers between devices: 17.8 us -> 16 us  [cross(): return lax.ppermute(x, ('row', 'col'), both(rows, cols, target))]
    ppermute x1, starting transfers between devices: 1.11 us -> 0.07 us  [reduce(): return (total, lax.ppermute(total, 'row', [(r, r ^ 2) for r in range(4)]))]
    ppermute x5, waiting for transfers between devices: 7.15 us -> 6.33 us  [swap_even(): lax.ppermute(x, axis, [(i, i ^ 1) for i in range(lax.axis_size(axis))])]
    ppermute x1, waiting for transfers between devices: 5.2 us -> 5.96 us  [reduce(): return (total, lax.ppermute(total, 'row', [(r, r ^ 2) for r in range(4)]))]
where the time goes in v4:
time: 57.8 us; the launch traced here: 57.6 us
  waiting for transfers between devices  28.3 us (49%)
  starting transfers between devices  18.2 us (31%)
  Pallas kernels  9.11 us (16%)
  local copies, waits for them, and re-layouts  0.92 us (2%)
  between operations  0.78 us (1%)
    ppermute x7, waiting for transfers between devices, cross(): return lax.ppermute(x, ('row', 'col'), both(rows, cols, target))  16 us
    ppermute x7, starting transfers between devices, cross(): return lax.ppermute(x, ('row', 'col'), both(rows, cols, target))  13.3 us
    pallas_call x8, Pallas kernels, call(): pl.pallas_call(kernel, out_shape=out_shape, in_specs=[pl.BlockSpec(memory...  9.11 us
    ppermute x5, waiting for transfers between devices, swap_even(): lax.ppermute(x, axis, [(i, i ^ 1) for i in range(lax.axis_size(axis))])  6.33 us
    ppermute x1, waiting for transfers between devices, reduce(): return (total, lax.ppermute(total, 'row', [(r, r ^ 2) for r in range(4)]))  5.96 us
    ppermute x5, starting transfers between devices, swap_even(): lax.ppermute(x, axis, [(i, i ^ 1) for i in range(lax.axis_size(axis))])  3.5 us
    ppermute x2, starting transfers between devices, swap_odd(): return lax.ppermute(x, axis, pairs)  1.31 us
  transfers between devices with their start and end apart: 15, of which 8 were waited for; matrix products, arithmetic and copies ran while one was open for 0% of the time, Pallas kernels for 0%

profile of v4, /device:TPU:0, one launch (start us, length us, event | category | flops | bytes accessed | tf_op | source)
XLA Modules:
  0.0 57.6 jit_solution(11043309475678601841)
XLA Ops:
  0.6 0.0 copy-start
  0.6 0.0 copy-start.1
  0.7 1.9 %shard_map.109 = (bf16[592,128]{1,0:T(8,128)(2,1)}, bf16[128,256]{1,0:T(8,128)(2,1)}, bf16[560,128]{1,0:T(8,128)(2,1)}) custom-call(bf16[16,32,256]{2,1,0:T(8,128)(2,1)} %region.1, bf16[8,16,512]{2,1,0:T(8,128)(2,1)} %cot.1, bf16[64,256]{1,0:T(8,128)(2,1)} %bitcast.31, bf16[64,144]{1,0:T(8,128)(2,1)} %bitcast.32, bf16[64,512]{1,0:T(8,128)(2,1)} %bitcast.30, ...), custom_call_target="tpu_custom_call" | custom-call | bytes 903168 | tf_op jit(solution)/shard_map/pallas_call | solution.py:404
  2.6 0.0 copy-start.2
  2.6 0.5 collective-permute-start
  3.1 0.7 %collective-permute-start.1 = (bf16[128,256]{1,0:T(8,128)(2,1)}, bf16[128,256]{1,0:T(8,128)(2,1)S(1)}, u32[]{:S(2)}, u32[]{:S(2)}) collective-permute-start(bf16[128,256]{1,0:T(8,128)(2,1)} %get-tuple-element.34), channel_id=1, source_target_pairs={{8,16},{16,8},{9,17},{17,9},{10,18},{18,10},{11,19},{19,11},{12,20... | collective-permute-start | bytes 196616 | tf_op jit(solution)/shard_map/ppermute | solution.py:442
  3.8 2.6 %collective-permute-start.4 = (bf16[592,128]{1,0:T(8,128)(2,1)}, bf16[592,128]{1,0:T(8,128)(2,1)S(1)}, u32[]{:S(2)}, u32[]{:S(2)}) collective-permute-start(bf16[592,128]{1,0:T(8,128)(2,1)} %get-tuple-element.39.refs_0_), channel_id=1, source_target_pairs={{0,2},{1,3},{2,4},{3,5},{4,6},{5,7},{6,0},{7,1},{8,11},{9,10},{10,... | collective-permute-start | bytes 454664 | tf_op jit(solution)/shard_map/ppermute | solution.py:456
  6.4 2.6 %collective-permute-start.5 = (bf16[592,128]{1,0:T(8,128)(2,1)}, bf16[592,128]{1,0:T(8,128)(2,1)S(1)}, u32[]{:S(2)}, u32[]{:S(2)}) collective-permute-start(bf16[592,128]{1,0:T(8,128)(2,1)} %get-tuple-element.39.refs_0_), channel_id=1, source_target_pairs={{0,4},{1,5},{2,6},{3,7},{4,0},{5,1},{6,2},{7,3},{8,13},{9,12},{10,... | collective-permute-start | bytes 454664 | tf_op jit(solution)/shard_map/ppermute | solution.py:456
  9.0 1.3 %collective-permute-start.6 = (bf16[592,128]{1,0:T(8,128)(2,1)}, bf16[592,128]{1,0:T(8,128)(2,1)S(1)}, u32[]{:S(2)}, u32[]{:S(2)}) collective-permute-start(bf16[592,128]{1,0:T(8,128)(2,1)} %get-tuple-element.39.refs_0_), channel_id=1, source_target_pairs={{0,6},{1,7},{2,0},{3,1},{4,2},{5,3},{6,4},{7,5},{8,15},{9,14},{10,... | collective-permute-start | bytes 454664 | tf_op jit(solution)/shard_map/ppermute | solution.py:456
  10.3 0.0 collective-permute-done.core_rows
  10.3 0.0 collective-permute-done.1.far_rows
  10.3 0.0 copy-start.3
  10.4 0.9 %copy-done.3 = bf16[560,128]{1,0:T(8,128)(2,1)S(1)} copy-done((bf16[560,128]{1,0:T(8,128)(2,1)S(1)}, bf16[560,128]{1,0:T(8,128)(2,1)}, u32[]{:S(2)}) %copy-start.3) | copy-done | bytes 143384
  11.3 1.6 %collective-permute-start.2 = (bf16[560,128]{1,0:T(8,128)(2,1)S(1)}, bf16[560,128]{1,0:T(8,128)(2,1)S(1)}, u32[]{:S(2)}, u32[]{:S(2)}) collective-permute-start(bf16[560,128]{1,0:T(8,128)(2,1)S(1)} %get-tuple-element.36), channel_id=1, source_target_pairs={{0,1},{1,0},{2,3},{3,2},{4,5},{5,4},{6,7},{7,6},{8,9},{9,8},{10,11... | collective-permute-start | bytes 430088 | tf_op jit(solution)/shard_map/ppermute | solution.py:446
  12.9 0.7 %collective-permute-start.3 = (bf16[256,128]{1,0:T(8,128)(2,1)S(1)}, bf16[256,128]{1,0:T(8,128)(2,1)S(1)}, u32[]{:S(2)}, u32[]{:S(2)}) collective-permute-start(bf16[256,128]{1,0:T(8,128)(2,1)S(1)} %get-tuple-element.37), channel_id=1, source_target_pairs={{1,2},{2,1},{3,4},{4,3},{5,6},{6,5},{9,10},{10,9},{11,12},{12,11},... | collective-permute-start | bytes 196616 | tf_op jit(solution)/shard_map/ppermute | solution.py:442
  13.5 0.0 collective-permute-done.3.edge
  13.5 0.0 collective-permute-done.4.refs_0_
  13.6 6.2 %collective-permute-done.5.refs_1_ = bf16[592,128]{1,0:T(8,128)(2,1)S(1)} collective-permute-done((bf16[592,128]{1,0:T(8,128)(2,1)}, bf16[592,128]{1,0:T(8,128)(2,1)S(1)}, u32[]{:S(2)}, u32[]{:S(2)}) %collective-permute-start.5) | collective-permute-done | bytes 151584 | tf_op jit(solution)/shard_map/ppermute | solution.py:456
  19.8 0.0 collective-permute-done.6.refs_2_
  19.8 1.8 %collective-permute-done.2.beside = bf16[560,128]{1,0:T(8,128)(2,1)S(1)} collective-permute-done((bf16[560,128]{1,0:T(8,128)(2,1)S(1)}, bf16[560,128]{1,0:T(8,128)(2,1)S(1)}, u32[]{:S(2)}, u32[]{:S(2)}) %collective-permute-start.2) | collective-permute-done | bytes 143392 | tf_op jit(solution)/shard_map/ppermute | solution.py:446
  21.6 1.0 %collective-permute-start.7 = (bf16[2080,128]{1,0:T(8,128)(2,1)S(1)}, bf16[2080,128]{1,0:T(8,128)(2,1)S(1)}, u32[]{:S(2)}, u32[]{:S(2)}) collective-permute-start(bf16[2080,128]{1,0:T(8,128)(2,1)S(1)} %shard_map.112.refs_1_), channel_id=1, source_target_pairs={{0,8},{8,0},{16,24},{24,16},{1,9},{9,1},{17,25},{25,17},{2,10},{10... | collective-permute-start | bytes 1597448 | tf_op jit(solution)/shard_map/ppermute | solution.py:446
  22.5 0.0 copy-done
  22.5 0.0 copy-done.1
  22.5 0.2 shard_map.111
  22.8 1.3 %collective-permute-done.7.refs_2_ = bf16[2080,128]{1,0:T(8,128)(2,1)S(1)} collective-permute-done((bf16[2080,128]{1,0:T(8,128)(2,1)S(1)}, bf16[2080,128]{1,0:T(8,128)(2,1)S(1)}, u32[]{:S(2)}, u32[]{:S(2)}) %collective-permute-start.7) | collective-permute-done | bytes 532512 | tf_op jit(solution)/shard_map/ppermute | solution.py:446
  24.1 0.0 copy-done.2
  24.1 1.9 %shard_map.113 = (bf16[1056,512]{1,0:T(8,128)(2,1)S(1)}, f32[512,512]{1,0:T(8,128)S(1)}, bf16[160,512]{1,0:T(8,128)(2,1)S(1)}, f32[160,512]{1,0:T(8,128)S(1)}, b...) custom-call(bf16[1056,256]{1,0:T(8,128)(2,1)S(1)} %get-tuple-element.38.x, bf16[592,128]{1,0:T(8,128)(2,1)S(1)} %copy-done.2, ...), custom_call_target="tpu_custom_call" | custom-call | flops 654311424 | bytes 7000064 | tf_op jit(solution)/shard_map/pallas_call | solution.py:404
  26.0 1.3 %shard_map.114 = (bf16[8,16,512]{2,1,0:T(8,128)(2,1)}, bf16[144,512]{1,0:T(8,128)(2,1)S(1)}, bf16[144,512]{1,0:T(8,128)(2,1)S(1)}, f32[128,256]{1,0:T(8,128)S(1)}, f32[512,768]{1,0:T(8,128)S(1)}) custom-call(bf16[1056,256]{1,0:T(8,128)(2,1)S(1)} %get-tuple-element.38.x, bf16[160,512]{1,0:T(8,128)(2,1)S(1)} %get-tuple-element.40.hidden_two, ...), custom_call_target="tpu_custom_call" | custom-call | flops 377487360 | bytes 4542464 | tf_op jit(solution)/shard_map/pallas_call | solution.py:404
  27.3 3.0 %shard_map.115 = (bf16[16,32,256]{2,1,0:T(8,128)(2,1)}, bf16[4,592,128]{2,1,0:T(8,128)(2,1)S(1)}, f32[592,128]{1,0:T(8,128)S(1)}, f32[592,128]{1,0:T(8,128)S(1)}...) custom-call(bf16[1056,256]{1,0:T(8,128)(2,1)S(1)} %get-tuple-element.38.x, ...), custom_call_target="tpu_custom_call" | custom-call | flops 872415232 | bytes 9371648 | tf_op jit(solution)/shard_map/pallas_call | solution.py:404
  30.3 0.4 collective-permute-start.8
  30.6 1.7 %collective-permute-done.8 = bf16[4,592,128]{2,1,0:T(8,128)(2,1)S(1)} collective-permute-done((bf16[4,592,128]{2,1,0:T(8,128)(2,1)S(1)}, bf16[4,592,128]{2,1,0:T(8,128)(2,1)S(1)}, u32[]{:S(2)}, u32[]{:S(2)}) %collective-permute-start.8) | collective-permute-done | bytes 606240 | tf_op jit(solution)/shard_map/ppermute | solution.py:446
  32.3 0.1 fusion.3
  32.4 4.0 %collective-permute-start.12 = (bf16[592,128]{1,0:T(8,128)(2,1)S(1)}, bf16[592,128]{1,0:T(8,128)(2,1)S(1)}, u32[]{:S(2)}, u32[]{:S(2)}) collective-permute-start(bf16[592,128]{1,0:T(8,128)(2,1)S(1)} %get-tuple-element.63), channel_id=1, source_target_pairs={{0,4},{1,5},{2,6},{3,7},{4,0},{5,1},{6,2},{7,3},{8,13},{9,12},{10,... | collective-permute-start | bytes 454664 | tf_op jit(solution)/shard_map/ppermute | solution.py:456
  36.5 0.7 %collective-permute-start.11 = (bf16[592,128]{1,0:T(8,128)(2,1)S(1)}, bf16[592,128]{1,0:T(8,128)(2,1)S(1)}, u32[]{:S(2)}, u32[]{:S(2)}) collective-permute-start(bf16[592,128]{1,0:T(8,128)(2,1)S(1)} %get-tuple-element.64), channel_id=1, source_target_pairs={{0,6},{1,7},{2,0},{3,1},{4,2},{5,3},{6,4},{7,5},{8,15},{9,14},{10,... | collective-permute-start | bytes 454664 | tf_op jit(solution)/shard_map/ppermute | solution.py:456
  37.2 1.3 %collective-permute-start.10 = (bf16[592,128]{1,0:T(8,128)(2,1)S(1)}, bf16[592,128]{1,0:T(8,128)(2,1)S(1)}, u32[]{:S(2)}, u32[]{:S(2)}) collective-permute-start(bf16[592,128]{1,0:T(8,128)(2,1)S(1)} %get-tuple-element.65), channel_id=1, source_target_pairs={{0,2},{1,3},{2,4},{3,5},{4,6},{5,7},{6,0},{7,1},{8,11},{9,10},{10,... | collective-permute-start | bytes 454664 | tf_op jit(solution)/shard_map/ppermute | solution.py:456
  38.5 0.7 %collective-permute-start.9 = (bf16[592,128]{1,0:T(8,128)(2,1)S(1)}, bf16[592,128]{1,0:T(8,128)(2,1)S(1)}, u32[]{:S(2)}, u32[]{:S(2)}) collective-permute-start(bf16[592,128]{1,0:T(8,128)(2,1)S(1)} %get-tuple-element.62), channel_id=1, source_target_pairs={{8,9},{9,8},{10,11},{11,10},{12,13},{13,12},{14,15},{15,14},{24,25... | collective-permute-start | bytes 454664 | tf_op jit(solution)/shard_map/ppermute | solution.py:456
  39.2 5.4 %collective-permute-done.12 = bf16[592,128]{1,0:T(8,128)(2,1)S(1)} collective-permute-done((bf16[592,128]{1,0:T(8,128)(2,1)S(1)}, bf16[592,128]{1,0:T(8,128)(2,1)S(1)}, u32[]{:S(2)}, u32[]{:S(2)}) %collective-permute-start.12) | collective-permute-done | bytes 151584 | tf_op jit(solution)/shard_map/ppermute | solution.py:456
  44.6 4.4 %collective-permute-done.11 = bf16[592,128]{1,0:T(8,128)(2,1)S(1)} collective-permute-done((bf16[592,128]{1,0:T(8,128)(2,1)S(1)}, bf16[592,128]{1,0:T(8,128)(2,1)S(1)}, u32[]{:S(2)}, u32[]{:S(2)}) %collective-permute-start.11) | collective-permute-done | bytes 151584 | tf_op jit(solution)/shard_map/ppermute | solution.py:456
  48.9 0.0 collective-permute-done.10
  48.9 0.0 collective-permute-done.9
  49.0 0.1 convert_add_fusion.4
  49.1 0.1 collective-permute-start.13
  49.1 1.6 %collective-permute-done.13 = f32[592,128]{1,0:T(8,128)S(1)} collective-permute-done((f32[592,128]{1,0:T(8,128)S(1)}, f32[592,128]{1,0:T(8,128)S(1)}, u32[]{:S(2)}, u32[]{:S(2)}) %collective-permute-start.13) | collective-permute-done | bytes 303136 | tf_op jit(solution)/shard_map/ppermute | solution.py:446
  50.8 0.1 collective-permute-start.14
  50.9 6.0 %collective-permute-done.14.across = bf16[592,128]{1,0:T(8,128)(2,1)S(1)} collective-permute-done((bf16[592,128]{1,0:T(8,128)(2,1)S(1)}, bf16[592,128]{1,0:T(8,128)(2,1)S(1)}, u32[]{:S(2)}, u32[]{:S(2)}) %collective-permute-start.14) | collective-permute-done | bytes 151584 | tf_op jit(solution)/shard_map/ppermute | solution.py:473
  56.8 0.8 %shard_map.116 = (f32[64,256]{1,0:T(8,128)}, f32[64,144]{1,0:T(8,128)}, f32[64,512]{1,0:T(8,128)}, f32[64,256]{1,0:T(8,128)}) custom-call(bf16[592,128]{1,0:T(8,128)(2,1)S(1)} %add_convert_fusion.total, bf16[592,128]{1,0:T(8,128)(2,1)S(1)} %collective-permute-done.14.across), custom_call_target="tpu_custom_call" | custom-call | bytes 602112 | tf_op jit(solution)/shard_map/pallas_call | solution.py:404
  (3 shorter events, 0.1 us)
Async XLA Ops:
  0.6 21.9 %copy-start = (bf16[16,32,256]{2,1,0:T(8,128)(2,1)S(1)}, bf16[16,32,256]{2,1,0:T(8,128)(2,1)}, u32[]{:S(2)}) copy-start(bf16[16,32,256]{2,1,0:T(8,128)(2,1)} %region.1) | copy-start | bytes 786436
  0.6 21.9 %copy-start.1 = (bf16[8,16,512]{2,1,0:T(8,128)(2,1)S(1)}, bf16[8,16,512]{2,1,0:T(8,128)(2,1)}, u32[]{:S(2)}) copy-start(bf16[8,16,512]{2,1,0:T(8,128)(2,1)} %cot.1) | copy-start | bytes 393220
  2.6 21.5 %copy-start.2 = (bf16[592,128]{1,0:T(8,128)(2,1)S(1)}, bf16[592,128]{1,0:T(8,128)(2,1)}, u32[]{:S(2)}) copy-start(bf16[592,128]{1,0:T(8,128)(2,1)} %get-tuple-element.39.refs_0_) | copy-start | bytes 454660
  2.6 7.8 %collective-permute-start = (bf16[128,256]{1,0:T(8,128)(2,1)}, bf16[128,256]{1,0:T(8,128)(2,1)S(1)}, u32[]{:S(2)}, u32[]{:S(2)}) collective-permute-start(bf16[128,256]{1,0:T(8,128)(2,1)} %get-tuple-element.34), channel_id=1, source_target_pairs={{0,8},{8,0},{16,24},{24,16},{1,9},{9,1},{17,25},{25,17},{2,10},{10... | collective-permute-start | bytes 196616 | tf_op jit(solution)/shard_map/ppermute | solution.py:446
  3.1 7.3 %collective-permute-start.1 = (bf16[128,256]{1,0:T(8,128)(2,1)}, bf16[128,256]{1,0:T(8,128)(2,1)S(1)}, u32[]{:S(2)}, u32[]{:S(2)}) collective-permute-start(bf16[128,256]{1,0:T(8,128)(2,1)} %get-tuple-element.34), channel_id=1, source_target_pairs={{8,16},{16,8},{9,17},{17,9},{10,18},{18,10},{11,19},{19,11},{12,20... | collective-permute-start | bytes 196616 | tf_op jit(solution)/shard_map/ppermute | solution.py:442
  3.8 9.8 %collective-permute-start.4 = (bf16[592,128]{1,0:T(8,128)(2,1)}, bf16[592,128]{1,0:T(8,128)(2,1)S(1)}, u32[]{:S(2)}, u32[]{:S(2)}) collective-permute-start(bf16[592,128]{1,0:T(8,128)(2,1)} %get-tuple-element.39.refs_0_), channel_id=1, source_target_pairs={{0,2},{1,3},{2,4},{3,5},{4,6},{5,7},{6,0},{7,1},{8,11},{9,10},{10,... | collective-permute-start | bytes 454664 | tf_op jit(solution)/shard_map/ppermute | solution.py:456
  6.4 13.4 %collective-permute-start.5 = (bf16[592,128]{1,0:T(8,128)(2,1)}, bf16[592,128]{1,0:T(8,128)(2,1)S(1)}, u32[]{:S(2)}, u32[]{:S(2)}) collective-permute-start(bf16[592,128]{1,0:T(8,128)(2,1)} %get-tuple-element.39.refs_0_), channel_id=1, source_target_pairs={{0,4},{1,5},{2,6},{3,7},{4,0},{5,1},{6,2},{7,3},{8,13},{9,12},{10,... | collective-permute-start | bytes 454664 | tf_op jit(solution)/shard_map/ppermute | solution.py:456
  9.0 10.8 %collective-permute-start.6 = (bf16[592,128]{1,0:T(8,128)(2,1)}, bf16[592,128]{1,0:T(8,128)(2,1)S(1)}, u32[]{:S(2)}, u32[]{:S(2)}) collective-permute-start(bf16[592,128]{1,0:T(8,128)(2,1)} %get-tuple-element.39.refs_0_), channel_id=1, source_target_pairs={{0,6},{1,7},{2,0},{3,1},{4,2},{5,3},{6,4},{7,5},{8,15},{9,14},{10,... | collective-permute-start | bytes 454664 | tf_op jit(solution)/shard_map/ppermute | solution.py:456
  10.3 0.9 %copy-start.3 = (bf16[560,128]{1,0:T(8,128)(2,1)S(1)}, bf16[560,128]{1,0:T(8,128)(2,1)}, u32[]{:S(2)}) copy-start(bf16[560,128]{1,0:T(8,128)(2,1)} %get-tuple-element.35.draft) | copy-start | bytes 430084
  11.3 10.3 %collective-permute-start.2 = (bf16[560,128]{1,0:T(8,128)(2,1)S(1)}, bf16[560,128]{1,0:T(8,128)(2,1)S(1)}, u32[]{:S(2)}, u32[]{:S(2)}) collective-permute-start(bf16[560,128]{1,0:T(8,128)(2,1)S(1)} %get-tuple-element.36), channel_id=1, source_target_pairs={{0,1},{1,0},{2,3},{3,2},{4,5},{5,4},{6,7},{7,6},{8,9},{9,8},{10,11... | collective-permute-start | bytes 430088 | tf_op jit(solution)/shard_map/ppermute | solution.py:446
  12.9 0.7 %collective-permute-start.3 = (bf16[256,128]{1,0:T(8,128)(2,1)S(1)}, bf16[256,128]{1,0:T(8,128)(2,1)S(1)}, u32[]{:S(2)}, u32[]{:S(2)}) collective-permute-start(bf16[256,128]{1,0:T(8,128)(2,1)S(1)} %get-tuple-element.37), channel_id=1, source_target_pairs={{1,2},{2,1},{3,4},{4,3},{5,6},{6,5},{9,10},{10,9},{11,12},{12,11},... | collective-permute-start | bytes 196616 | tf_op jit(solution)/shard_map/ppermute | solution.py:442
  21.6 2.5 %collective-permute-start.7 = (bf16[2080,128]{1,0:T(8,128)(2,1)S(1)}, bf16[2080,128]{1,0:T(8,128)(2,1)S(1)}, u32[]{:S(2)}, u32[]{:S(2)}) collective-permute-start(bf16[2080,128]{1,0:T(8,128)(2,1)S(1)} %shard_map.112.refs_1_), channel_id=1, source_target_pairs={{0,8},{8,0},{16,24},{24,16},{1,9},{9,1},{17,25},{25,17},{2,10},{10... | collective-permute-start | bytes 1597448 | tf_op jit(solution)/shard_map/ppermute | solution.py:446
  30.3 2.0 %collective-permute-start.8 = (bf16[4,592,128]{2,1,0:T(8,128)(2,1)S(1)}, bf16[4,592,128]{2,1,0:T(8,128)(2,1)S(1)}, u32[]{:S(2)}, u32[]{:S(2)}) collective-permute-start(bf16[4,592,128]{2,1,0:T(8,128)(2,1)S(1)} %get-tuple-element.54), channel_id=1, source_target_pairs={{0,8},{8,0},{16,24},{24,16},{1,9},{9,1},{17,25},{25,17},{2,10},{10... | collective-permute-start | bytes 1818632 | tf_op jit(solution)/shard_map/ppermute | solution.py:446
  32.4 12.1 %collective-permute-start.12 = (bf16[592,128]{1,0:T(8,128)(2,1)S(1)}, bf16[592,128]{1,0:T(8,128)(2,1)S(1)}, u32[]{:S(2)}, u32[]{:S(2)}) collective-permute-start(bf16[592,128]{1,0:T(8,128)(2,1)S(1)} %get-tuple-element.63), channel_id=1, source_target_pairs={{0,4},{1,5},{2,6},{3,7},{4,0},{5,1},{6,2},{7,3},{8,13},{9,12},{10,... | collective-permute-start | bytes 454664 | tf_op jit(solution)/shard_map/ppermute | solution.py:456
  36.5 12.5 %collective-permute-start.11 = (bf16[592,128]{1,0:T(8,128)(2,1)S(1)}, bf16[592,128]{1,0:T(8,128)(2,1)S(1)}, u32[]{:S(2)}, u32[]{:S(2)}) collective-permute-start(bf16[592,128]{1,0:T(8,128)(2,1)S(1)} %get-tuple-element.64), channel_id=1, source_target_pairs={{0,6},{1,7},{2,0},{3,1},{4,2},{5,3},{6,4},{7,5},{8,15},{9,14},{10,... | collective-permute-start | bytes 454664 | tf_op jit(solution)/shard_map/ppermute | solution.py:456
  37.2 11.8 %collective-permute-start.10 = (bf16[592,128]{1,0:T(8,128)(2,1)S(1)}, bf16[592,128]{1,0:T(8,128)(2,1)S(1)}, u32[]{:S(2)}, u32[]{:S(2)}) collective-permute-start(bf16[592,128]{1,0:T(8,128)(2,1)S(1)} %get-tuple-element.65), channel_id=1, source_target_pairs={{0,2},{1,3},{2,4},{3,5},{4,6},{5,7},{6,0},{7,1},{8,11},{9,10},{10,... | collective-permute-start | bytes 454664 | tf_op jit(solution)/shard_map/ppermute | solution.py:456
  38.5 10.5 %collective-permute-start.9 = (bf16[592,128]{1,0:T(8,128)(2,1)S(1)}, bf16[592,128]{1,0:T(8,128)(2,1)S(1)}, u32[]{:S(2)}, u32[]{:S(2)}) collective-permute-start(bf16[592,128]{1,0:T(8,128)(2,1)S(1)} %get-tuple-element.62), channel_id=1, source_target_pairs={{8,9},{9,8},{10,11},{11,10},{12,13},{13,12},{14,15},{15,14},{24,25... | collective-permute-start | bytes 454664 | tf_op jit(solution)/shard_map/ppermute | solution.py:456
  49.1 1.7 %collective-permute-start.13 = (f32[592,128]{1,0:T(8,128)S(1)}, f32[592,128]{1,0:T(8,128)S(1)}, u32[]{:S(2)}, u32[]{:S(2)}) collective-permute-start(f32[592,128]{1,0:T(8,128)S(1)} %convert_add_fusion.4), channel_id=1, source_target_pairs={{0,8},{8,0},{16,24},{24,16},{1,9},{9,1},{17,25},{25,17},{2,10},{10... | collective-permute-start | bytes 909320 | tf_op jit(solution)/shard_map/ppermute | solution.py:446
  50.8 6.0 %collective-permute-start.14 = (bf16[592,128]{1,0:T(8,128)(2,1)S(1)}, bf16[592,128]{1,0:T(8,128)(2,1)S(1)}, u32[]{:S(2)}, u32[]{:S(2)}) collective-permute-start(bf16[592,128]{1,0:T(8,128)(2,1)S(1)} %add_convert_fusion.total), channel_id=1, source_target_pairs={{0,16},{8,24},{16,0},{24,8},{1,17},{9,25},{17,1},{25,9},{2,18},{10... | collective-permute-start | bytes 454664 | tf_op jit(solution)/shard_map/ppermute | solution.py:473

commit v5 on v4

--- a/solution.py
+++ b/solution.py
@@ -304,7 +304,7 @@
 
 
 def second_kernel(sizes, halves, x, hidden_two, slope_two, cot, *refs):
-    block_out, grad_two, grad_side, short_back, total, expand_t, short_t, shift, beside = refs[3:]
+    active_three, grad_two, grad_side, own, short_t, total, expand_t, shift, beside = refs[3:]
     mid = expand_t.shape[1]
     width = expand_t.shape[0]
     shard = width // (2 * halves)
@@ -323,15 +323,12 @@
     )
     sigma = sigmoid(summed)
     active = summed * sigma
-    block_out[...] = (
-        active[: sizes.main].astype(BF16).reshape(sizes.hr, sizes.hc, width)
-    )
+    active_three[...] = active[: sizes.main].astype(BF16)
     grad_sum = (cot[...].astype(F32) * (sigma + active * (1.0 - sigma))).astype(BF16)
-    own = grad_sum[: sizes.main]
-    flipped = own.astype(F32).T.astype(BF16)
+    own[...] = grad_sum[: sizes.main]
+    flipped = grad_sum[: sizes.main].astype(F32).T.astype(BF16)
     total[:, :mid] = dot(flipped, hidden_two[: sizes.main])
     total[:, mid:] = dot(flipped, strided[: sizes.main])
-    short_back[...] = dot(own, short_t[...])
     back = dot(grad_sum, expand_t[...]) * slope_two[...]
     grad_two[...] = back[: sizes.wide].astype(BF16)
     for i in range(sizes.hr + 1):
@@ -342,12 +339,12 @@
 
 
 def third_kernel(
-    sizes, halves, x, hidden, slope_one, back, reduce_t, grad_two, grad_side, short_back, late, *refs
+    sizes, halves, cin, x, hidden, slope_one, back, grad_two, grad_side, late, *refs
 ):
-    region_grad, give = refs[:2]
+    grad_one, give = refs[:2]
     keeps = refs[2 : 2 + halves]
-    total, grad_one, planes, spread_out = refs[2 + halves :]
-    mid, cin = reduce_t.shape
+    total = refs[2 + halves]
+    mid = hidden.shape[1]
     main, hc = sizes.main, sizes.hc
     shard = mid // (2 * halves)
     down = slice(hc, hc + main)
@@ -386,8 +383,13 @@
                     total[rows, cin + 128 : cin + 256] = jnp.where(lane == 0, block, 0.0)
     total[:, cin + 256 :] = late[...]
     split_out(halves, total, shard, cin + 128, keeps, give)
+
+
+def outputs_kernel(sizes, grad_one, reduce_t, grad_sum, short_t, active, block_out, region_grad, planes, spread_out):
+    main, hc, cin = sizes.main, sizes.hc, reduce_t.shape[1]
+    block_out[...] = active[...].reshape(block_out.shape)
     planes[...] = dot(grad_one[...], reduce_t[...])
-    planes[:main] += short_back[...]
+    planes[:main] += dot(grad_sum[...], short_t[...])
     for i in range(4):
         for r in range(sizes.hr):
             at = i * main + r * hc
@@ -462,7 +464,7 @@
     other = swap_even(give, "row")
     sums = [keeps[j] + other[j].astype(F32) for j in range(halves)]
     total = None
-    for j in sorted(range(halves), key=lambda j: min(j, halves - j)):
+    for j in sorted(range(halves), key=lambda j: (j > 0, -min(j, halves - j), -j)):
         came = cross(sums[j].astype(BF16), j).astype(F32)
         if j == 0:
             came = jnp.where(core == 0, sums[0], came)
@@ -560,36 +562,43 @@
         x, *blocks,
         flops=2 * sizes.pixels * cin * mid + 2 * sizes.out * TAPS * HALF * mid,
     )
-    block_out, grad_two, grad_side, short_back, late_total = call(
+    active_three, grad_two, grad_side, grad_sum, short_t, late_total = call(
         functools.partial(second_kernel, sizes, halves),
         (
-            shape((sizes.hr, sizes.hc, width)),
+            shape((sizes.main, width)),
             shape((sizes.wide, mid)),
             shape((sizes.wide, mid)),
-            shape((sizes.main, cin), F32),
+            shape((sizes.main, width)),
+            shape((width, cin)),
             shape((width, late), F32),
         ),
         [
             scratch(width, mid, dtype=BF16),
-            scratch(width, cin, dtype=BF16),
             scratch(sizes.hr + 1, 24, mid),
             scratch(length, 128, dtype=BF16),
         ],
         x, hidden_two, slope_two, cot_all, *blocks,
         flops=6 * sizes.out * width * (mid + cin),
     )
-    region_grad, give, *keeps = call(
-        functools.partial(third_kernel, sizes, halves),
-        (shape(region.shape), shape((halves, length, 128)))
+    grad_one, give, *keeps = call(
+        functools.partial(third_kernel, sizes, halves, cin),
+        (shape((4 * sizes.main, mid)), shape((halves, length, 128)))
         + (shape((length, 128), F32),) * halves,
         [
             scratch(mid, early + late),
-            scratch(4 * sizes.main, mid, dtype=BF16),
+        ],
+        x, hidden, slope_one, back, grad_two, grad_side, late_total,
+        flops=2 * 4 * sizes.main * cin * mid + 4 * sizes.main * TAPS * HALF * mid,
+    )
+    block_out, region_grad = call(
+        functools.partial(outputs_kernel, sizes),
+        (shape((sizes.hr, sizes.hc, width)), shape(region.shape)),
+        [
             scratch(4 * sizes.main, cin),
             scratch(cin // 128, tile_rows, tile_cols, 128),
         ],
-        x, hidden, slope_one, back, reduce_t, grad_two, grad_side, short_back, late_total,
-        flops=4 * 4 * sizes.main * cin * mid + 4 * sizes.main * TAPS * HALF * mid,
+        grad_one, reduce_t, grad_sum, short_t, active_three,
+        flops=2 * 4 * sizes.main * cin * mid,
     )
     total, across = reduce(keeps, give)
     grads = call(

time: 57.8 us -> 56.8 us (0.983)
  waiting for transfers between devices: 28.3 us -> 27.2 us
    ppermute x1, waiting for transfers between devices: 5.96 us -> 4.87 us  [reduce(): return (total, lax.ppermute(total, 'row', [(r, r ^ 2) for r in range(4)]))]
    pallas_call x8 -> x9, Pallas kernels: 9.11 us -> 9.15 us  [call(): pl.pallas_call(kernel, out_shape=out_shape, in_specs=[pl.BlockSpec(memory...]
  transfers between devices with their start and end apart: 15 -> 15, of which waited for: 8 -> 8; matrix products, arithmetic and copies ran while one was open for 0% -> 0% of each run, Pallas kernels for 0% -> 2%
where the time goes in v5:
time: 56.8 us; the launch traced here: 56.6 us
  waiting for transfers between devices  27.2 us (48%)
  starting transfers between devices  18.2 us (32%)
  Pallas kernels  9.15 us (16%)
  local copies, waits for them, and re-layouts  0.92 us (2%)
  between operations  0.8 us (1%)
    ppermute x7, waiting for transfers between devices, cross(): return lax.ppermute(x, ('row', 'col'), both(rows, cols, target))  16 us
    ppermute x7, starting transfers between devices, cross(): return lax.ppermute(x, ('row', 'col'), both(rows, cols, target))  13.3 us
    pallas_call x9, Pallas kernels, call(): pl.pallas_call(kernel, out_shape=out_shape, in_specs=[pl.BlockSpec(memory...  9.15 us
    ppermute x5, waiting for transfers between devices, swap_even(): lax.ppermute(x, axis, [(i, i ^ 1) for i in range(lax.axis_size(axis))])  6.33 us
    ppermute x1, waiting for transfers between devices, reduce(): return (total, lax.ppermute(total, 'row', [(r, r ^ 2) for r in range(4)]))  4.87 us
    ppermute x5, starting transfers between devices, swap_even(): lax.ppermute(x, axis, [(i, i ^ 1) for i in range(lax.axis_size(axis))])  3.56 us
    ppermute x2, starting transfers between devices, swap_odd(): return lax.ppermute(x, axis, pairs)  1.31 us
  transfers between devices with their start and end apart: 15, of which 8 were waited for; matrix products, arithmetic and copies ran while one was open for 0% of the time, Pallas kernels for 2%

profile of v5, /device:TPU:0, one launch (start us, length us, event | category | flops | bytes accessed | tf_op | source)
XLA Modules:
  0.0 56.6 jit_solution(7978848224485005560)
XLA Ops:
  0.6 0.0 copy-start.1
  0.6 0.0 copy-start
  0.7 1.9 %shard_map.109 = (bf16[592,128]{1,0:T(8,128)(2,1)}, bf16[128,256]{1,0:T(8,128)(2,1)}, bf16[560,128]{1,0:T(8,128)(2,1)}) custom-call(bf16[16,32,256]{2,1,0:T(8,128)(2,1)} %region.1, bf16[8,16,512]{2,1,0:T(8,128)(2,1)} %cot.1, bf16[64,256]{1,0:T(8,128)(2,1)} %bitcast.31, bf16[64,144]{1,0:T(8,128)(2,1)} %bitcast.32, bf16[64,512]{1,0:T(8,128)(2,1)} %bitcast.30, ...), custom_call_target="tpu_custom_call" | custom-call | bytes 903168 | tf_op jit(solution)/shard_map/pallas_call | solution.py:406
  2.6 0.0 copy-start.2
  2.6 0.5 collective-permute-start
  3.1 0.7 %collective-permute-start.1 = (bf16[128,256]{1,0:T(8,128)(2,1)}, bf16[128,256]{1,0:T(8,128)(2,1)S(1)}, u32[]{:S(2)}, u32[]{:S(2)}) collective-permute-start(bf16[128,256]{1,0:T(8,128)(2,1)} %get-tuple-element.37), channel_id=1, source_target_pairs={{8,16},{16,8},{9,17},{17,9},{10,18},{18,10},{11,19},{19,11},{12,20... | collective-permute-start | bytes 196616 | tf_op jit(solution)/shard_map/ppermute | solution.py:444
  3.8 2.6 %collective-permute-start.4 = (bf16[592,128]{1,0:T(8,128)(2,1)}, bf16[592,128]{1,0:T(8,128)(2,1)S(1)}, u32[]{:S(2)}, u32[]{:S(2)}) collective-permute-start(bf16[592,128]{1,0:T(8,128)(2,1)} %get-tuple-element.42.refs_0_), channel_id=1, source_target_pairs={{0,2},{1,3},{2,4},{3,5},{4,6},{5,7},{6,0},{7,1},{8,11},{9,10},{10,... | collective-permute-start | bytes 454664 | tf_op jit(solution)/shard_map/ppermute | solution.py:458
  6.4 2.6 %collective-permute-start.5 = (bf16[592,128]{1,0:T(8,128)(2,1)}, bf16[592,128]{1,0:T(8,128)(2,1)S(1)}, u32[]{:S(2)}, u32[]{:S(2)}) collective-permute-start(bf16[592,128]{1,0:T(8,128)(2,1)} %get-tuple-element.42.refs_0_), channel_id=1, source_target_pairs={{0,4},{1,5},{2,6},{3,7},{4,0},{5,1},{6,2},{7,3},{8,13},{9,12},{10,... | collective-permute-start | bytes 454664 | tf_op jit(solution)/shard_map/ppermute | solution.py:458
  9.0 1.3 %collective-permute-start.6 = (bf16[592,128]{1,0:T(8,128)(2,1)}, bf16[592,128]{1,0:T(8,128)(2,1)S(1)}, u32[]{:S(2)}, u32[]{:S(2)}) collective-permute-start(bf16[592,128]{1,0:T(8,128)(2,1)} %get-tuple-element.42.refs_0_), channel_id=1, source_target_pairs={{0,6},{1,7},{2,0},{3,1},{4,2},{5,3},{6,4},{7,5},{8,15},{9,14},{10,... | collective-permute-start | bytes 454664 | tf_op jit(solution)/shard_map/ppermute | solution.py:458
  10.4 0.0 collective-permute-done.core_rows
  10.4 0.0 collective-permute-done.1.far_rows
  10.4 0.0 copy-start.3
  10.4 0.9 %copy-done.3 = bf16[560,128]{1,0:T(8,128)(2,1)S(1)} copy-done((bf16[560,128]{1,0:T(8,128)(2,1)S(1)}, bf16[560,128]{1,0:T(8,128)(2,1)}, u32[]{:S(2)}) %copy-start.3) | copy-done | bytes 143384
  11.3 1.6 %collective-permute-start.2 = (bf16[560,128]{1,0:T(8,128)(2,1)S(1)}, bf16[560,128]{1,0:T(8,128)(2,1)S(1)}, u32[]{:S(2)}, u32[]{:S(2)}) collective-permute-start(bf16[560,128]{1,0:T(8,128)(2,1)S(1)} %get-tuple-element.39), channel_id=1, source_target_pairs={{0,1},{1,0},{2,3},{3,2},{4,5},{5,4},{6,7},{7,6},{8,9},{9,8},{10,11... | collective-permute-start | bytes 430088 | tf_op jit(solution)/shard_map/ppermute | solution.py:448
  12.9 0.7 %collective-permute-start.3 = (bf16[256,128]{1,0:T(8,128)(2,1)S(1)}, bf16[256,128]{1,0:T(8,128)(2,1)S(1)}, u32[]{:S(2)}, u32[]{:S(2)}) collective-permute-start(bf16[256,128]{1,0:T(8,128)(2,1)S(1)} %get-tuple-element.40), channel_id=1, source_target_pairs={{1,2},{2,1},{3,4},{4,3},{5,6},{6,5},{9,10},{10,9},{11,12},{12,11},... | collective-permute-start | bytes 196616 | tf_op jit(solution)/shard_map/ppermute | solution.py:444
  13.6 0.0 collective-permute-done.3.edge
  13.6 0.0 collective-permute-done.4.refs_0_
  13.6 6.2 %collective-permute-done.5.refs_1_ = bf16[592,128]{1,0:T(8,128)(2,1)S(1)} collective-permute-done((bf16[592,128]{1,0:T(8,128)(2,1)}, bf16[592,128]{1,0:T(8,128)(2,1)S(1)}, u32[]{:S(2)}, u32[]{:S(2)}) %collective-permute-start.5) | collective-permute-done | bytes 151584 | tf_op jit(solution)/shard_map/ppermute | solution.py:458
  19.8 0.0 collective-permute-done.6.refs_2_
  19.8 1.8 %collective-permute-done.2.beside = bf16[560,128]{1,0:T(8,128)(2,1)S(1)} collective-permute-done((bf16[560,128]{1,0:T(8,128)(2,1)S(1)}, bf16[560,128]{1,0:T(8,128)(2,1)S(1)}, u32[]{:S(2)}, u32[]{:S(2)}) %collective-permute-start.2) | collective-permute-done | bytes 143392 | tf_op jit(solution)/shard_map/ppermute | solution.py:448
  21.6 1.0 %collective-permute-start.7 = (bf16[2080,128]{1,0:T(8,128)(2,1)S(1)}, bf16[2080,128]{1,0:T(8,128)(2,1)S(1)}, u32[]{:S(2)}, u32[]{:S(2)}) collective-permute-start(bf16[2080,128]{1,0:T(8,128)(2,1)S(1)} %shard_map.112.refs_1_), channel_id=1, source_target_pairs={{0,8},{8,0},{16,24},{24,16},{1,9},{9,1},{17,25},{25,17},{2,10},{10... | collective-permute-start | bytes 1597448 | tf_op jit(solution)/shard_map/ppermute | solution.py:448
  22.6 0.0 copy-done.1
  22.6 0.0 copy-done
  22.6 0.2 shard_map.111
  22.8 1.3 %collective-permute-done.7.refs_2_ = bf16[2080,128]{1,0:T(8,128)(2,1)S(1)} collective-permute-done((bf16[2080,128]{1,0:T(8,128)(2,1)S(1)}, bf16[2080,128]{1,0:T(8,128)(2,1)S(1)}, u32[]{:S(2)}, u32[]{:S(2)}) %collective-permute-start.7) | collective-permute-done | bytes 532512 | tf_op jit(solution)/shard_map/ppermute | solution.py:448
  24.1 0.0 copy-done.2
  24.1 1.9 %shard_map.113 = (bf16[1056,512]{1,0:T(8,128)(2,1)S(1)}, f32[512,512]{1,0:T(8,128)S(1)}, bf16[160,512]{1,0:T(8,128)(2,1)S(1)}, f32[160,512]{1,0:T(8,128)S(1)}, b...) custom-call(bf16[1056,256]{1,0:T(8,128)(2,1)S(1)} %get-tuple-element.41.x, bf16[592,128]{1,0:T(8,128)(2,1)S(1)} %copy-done.2, ...), custom_call_target="tpu_custom_call" | custom-call | flops 654311424 | bytes 7000064 | tf_op jit(solution)/shard_map/pallas_call | solution.py:406
  26.0 1.2 %shard_map.114 = (bf16[128,512]{1,0:T(8,128)(2,1)S(1)}, bf16[144,512]{1,0:T(8,128)(2,1)S(1)}, bf16[144,512]{1,0:T(8,128)(2,1)S(1)}, bf16[128,512]{1,0:T(8,128)(2...) custom-call(bf16[1056,256]{1,0:T(8,128)(2,1)S(1)} %get-tuple-element.41.x, ...), custom_call_target="tpu_custom_call" | custom-call | flops 377487360 | bytes 4804608 | tf_op jit(solution)/shard_map/pallas_call | solution.py:406
  27.2 2.0 %shard_map.115 = (bf16[512,512]{1,0:T(8,128)(2,1)S(1)}, bf16[4,592,128]{2,1,0:T(8,128)(2,1)S(1)}, f32[592,128]{1,0:T(8,128)S(1)}, f32[592,128]{1,0:T(8,128)S(1)}...) custom-call(bf16[1056,256]{1,0:T(8,128)(2,1)S(1)} %get-tuple-element.41.x, ...), custom_call_target="tpu_custom_call" | custom-call | flops 738197504 | bytes 9240576 | tf_op jit(solution)/shard_map/pallas_call | solution.py:406
  29.2 0.4 collective-permute-start.8
  29.7 1.7 %collective-permute-done.8 = bf16[4,592,128]{2,1,0:T(8,128)(2,1)S(1)} collective-permute-done((bf16[4,592,128]{2,1,0:T(8,128)(2,1)S(1)}, bf16[4,592,128]{2,1,0:T(8,128)(2,1)S(1)}, u32[]{:S(2)}, u32[]{:S(2)}) %collective-permute-start.8) | collective-permute-done | bytes 606240 | tf_op jit(solution)/shard_map/ppermute | solution.py:448
  31.3 0.1 fusion.3
  31.5 4.0 %collective-permute-start.10 = (bf16[592,128]{1,0:T(8,128)(2,1)S(1)}, bf16[592,128]{1,0:T(8,128)(2,1)S(1)}, u32[]{:S(2)}, u32[]{:S(2)}) collective-permute-start(bf16[592,128]{1,0:T(8,128)(2,1)S(1)} %get-tuple-element.71), channel_id=1, source_target_pairs={{0,4},{1,5},{2,6},{3,7},{4,0},{5,1},{6,2},{7,3},{8,13},{9,12},{10,... | collective-permute-start | bytes 454664 | tf_op jit(solution)/shard_map/ppermute | solution.py:458
  35.5 0.7 %collective-permute-start.11 = (bf16[592,128]{1,0:T(8,128)(2,1)S(1)}, bf16[592,128]{1,0:T(8,128)(2,1)S(1)}, u32[]{:S(2)}, u32[]{:S(2)}) collective-permute-start(bf16[592,128]{1,0:T(8,128)(2,1)S(1)} %get-tuple-element.70), channel_id=1, source_target_pairs={{0,6},{1,7},{2,0},{3,1},{4,2},{5,3},{6,4},{7,5},{8,15},{9,14},{10,... | collective-permute-start | bytes 454664 | tf_op jit(solution)/shard_map/ppermute | solution.py:458
  36.2 1.3 %collective-permute-start.12 = (bf16[592,128]{1,0:T(8,128)(2,1)S(1)}, bf16[592,128]{1,0:T(8,128)(2,1)S(1)}, u32[]{:S(2)}, u32[]{:S(2)}) collective-permute-start(bf16[592,128]{1,0:T(8,128)(2,1)S(1)} %get-tuple-element.69), channel_id=1, source_target_pairs={{0,2},{1,3},{2,4},{3,5},{4,6},{5,7},{6,0},{7,1},{8,11},{9,10},{10,... | collective-permute-start | bytes 454664 | tf_op jit(solution)/shard_map/ppermute | solution.py:458
  37.5 0.7 %collective-permute-start.9 = (bf16[592,128]{1,0:T(8,128)(2,1)S(1)}, bf16[592,128]{1,0:T(8,128)(2,1)S(1)}, u32[]{:S(2)}, u32[]{:S(2)}) collective-permute-start(bf16[592,128]{1,0:T(8,128)(2,1)S(1)} %get-tuple-element.68), channel_id=1, source_target_pairs={{8,9},{9,8},{10,11},{11,10},{12,13},{13,12},{14,15},{15,14},{24,25... | collective-permute-start | bytes 454664 | tf_op jit(solution)/shard_map/ppermute | solution.py:458
  38.2 5.4 %collective-permute-done.10 = bf16[592,128]{1,0:T(8,128)(2,1)S(1)} collective-permute-done((bf16[592,128]{1,0:T(8,128)(2,1)S(1)}, bf16[592,128]{1,0:T(8,128)(2,1)S(1)}, u32[]{:S(2)}, u32[]{:S(2)}) %collective-permute-start.10) | collective-permute-done | bytes 151584 | tf_op jit(solution)/shard_map/ppermute | solution.py:458
  43.6 4.4 %collective-permute-done.11 = bf16[592,128]{1,0:T(8,128)(2,1)S(1)} collective-permute-done((bf16[592,128]{1,0:T(8,128)(2,1)S(1)}, bf16[592,128]{1,0:T(8,128)(2,1)S(1)}, u32[]{:S(2)}, u32[]{:S(2)}) %collective-permute-start.11) | collective-permute-done | bytes 151584 | tf_op jit(solution)/shard_map/ppermute | solution.py:458
  48.0 0.0 collective-permute-done.12
  48.0 0.0 collective-permute-done.9
  48.0 0.1 convert_add_fusion.4
  48.1 0.1 collective-permute-start.13
  48.2 1.6 %collective-permute-done.13 = f32[592,128]{1,0:T(8,128)S(1)} collective-permute-done((f32[592,128]{1,0:T(8,128)S(1)}, f32[592,128]{1,0:T(8,128)S(1)}, u32[]{:S(2)}, u32[]{:S(2)}) %collective-permute-start.13) | collective-permute-done | bytes 303136 | tf_op jit(solution)/shard_map/ppermute | solution.py:448
  49.8 0.1 collective-permute-start.14
  49.9 1.1 %shard_map.116 = (bf16[8,16,512]{2,1,0:T(8,128)(2,1)}, bf16[16,32,256]{2,1,0:T(8,128)(2,1)}) custom-call(bf16[512,512]{1,0:T(8,128)(2,1)S(1)} %get-tuple-element.52.grad_one, bf16[512,256]{1,0:T(8,128)(2,1)S(1)} %get-tuple-element.53.reduce_t, bf16[128,512]{1,0:T(8,128)(2,1)S(1)} %get-tuple-element.54.grad_sum, ...), custom_call_target="tpu_custom_call" | custom-call | flops 134217728 | bytes 1703936 | tf_op jit(solution)/shard_map/pallas_call | solution.py:406
  51.0 4.9 %collective-permute-done.14.across = bf16[592,128]{1,0:T(8,128)(2,1)S(1)} collective-permute-done((bf16[592,128]{1,0:T(8,128)(2,1)S(1)}, bf16[592,128]{1,0:T(8,128)(2,1)S(1)}, u32[]{:S(2)}, u32[]{:S(2)}) %collective-permute-start.14) | collective-permute-done | bytes 151584 | tf_op jit(solution)/shard_map/ppermute | solution.py:475
  55.8 0.8 %shard_map.117 = (f32[64,256]{1,0:T(8,128)}, f32[64,144]{1,0:T(8,128)}, f32[64,512]{1,0:T(8,128)}, f32[64,256]{1,0:T(8,128)}) custom-call(bf16[592,128]{1,0:T(8,128)(2,1)S(1)} %add_convert_fusion.total, bf16[592,128]{1,0:T(8,128)(2,1)S(1)} %collective-permute-done.14.across), custom_call_target="tpu_custom_call" | custom-call | bytes 602112 | tf_op jit(solution)/shard_map/pallas_call | solution.py:406
  (3 shorter events, 0.1 us)
Async XLA Ops:
  0.6 21.9 %copy-start.1 = (bf16[8,16,512]{2,1,0:T(8,128)(2,1)S(1)}, bf16[8,16,512]{2,1,0:T(8,128)(2,1)}, u32[]{:S(2)}) copy-start(bf16[8,16,512]{2,1,0:T(8,128)(2,1)} %cot.1) | copy-start | bytes 393220
  0.6 21.9 %copy-start = (bf16[16,32,256]{2,1,0:T(8,128)(2,1)S(1)}, bf16[16,32,256]{2,1,0:T(8,128)(2,1)}, u32[]{:S(2)}) copy-start(bf16[16,32,256]{2,1,0:T(8,128)(2,1)} %region.1) | copy-start | bytes 786436
  2.6 21.5 %copy-start.2 = (bf16[592,128]{1,0:T(8,128)(2,1)S(1)}, bf16[592,128]{1,0:T(8,128)(2,1)}, u32[]{:S(2)}) copy-start(bf16[592,128]{1,0:T(8,128)(2,1)} %get-tuple-element.42.refs_0_) | copy-start | bytes 454660
  2.6 7.8 %collective-permute-start = (bf16[128,256]{1,0:T(8,128)(2,1)}, bf16[128,256]{1,0:T(8,128)(2,1)S(1)}, u32[]{:S(2)}, u32[]{:S(2)}) collective-permute-start(bf16[128,256]{1,0:T(8,128)(2,1)} %get-tuple-element.37), channel_id=1, source_target_pairs={{0,8},{8,0},{16,24},{24,16},{1,9},{9,1},{17,25},{25,17},{2,10},{10... | collective-permute-start | bytes 196616 | tf_op jit(solution)/shard_map/ppermute | solution.py:448
  3.1 7.3 %collective-permute-start.1 = (bf16[128,256]{1,0:T(8,128)(2,1)}, bf16[128,256]{1,0:T(8,128)(2,1)S(1)}, u32[]{:S(2)}, u32[]{:S(2)}) collective-permute-start(bf16[128,256]{1,0:T(8,128)(2,1)} %get-tuple-element.37), channel_id=1, source_target_pairs={{8,16},{16,8},{9,17},{17,9},{10,18},{18,10},{11,19},{19,11},{12,20... | collective-permute-start | bytes 196616 | tf_op jit(solution)/shard_map/ppermute | solution.py:444
  3.8 9.8 %collective-permute-start.4 = (bf16[592,128]{1,0:T(8,128)(2,1)}, bf16[592,128]{1,0:T(8,128)(2,1)S(1)}, u32[]{:S(2)}, u32[]{:S(2)}) collective-permute-start(bf16[592,128]{1,0:T(8,128)(2,1)} %get-tuple-element.42.refs_0_), channel_id=1, source_target_pairs={{0,2},{1,3},{2,4},{3,5},{4,6},{5,7},{6,0},{7,1},{8,11},{9,10},{10,... | collective-permute-start | bytes 454664 | tf_op jit(solution)/shard_map/ppermute | solution.py:458
  6.4 13.4 %collective-permute-start.5 = (bf16[592,128]{1,0:T(8,128)(2,1)}, bf16[592,128]{1,0:T(8,128)(2,1)S(1)}, u32[]{:S(2)}, u32[]{:S(2)}) collective-permute-start(bf16[592,128]{1,0:T(8,128)(2,1)} %get-tuple-element.42.refs_0_), channel_id=1, source_target_pairs={{0,4},{1,5},{2,6},{3,7},{4,0},{5,1},{6,2},{7,3},{8,13},{9,12},{10,... | collective-permute-start | bytes 454664 | tf_op jit(solution)/shard_map/ppermute | solution.py:458
  9.0 10.8 %collective-permute-start.6 = (bf16[592,128]{1,0:T(8,128)(2,1)}, bf16[592,128]{1,0:T(8,128)(2,1)S(1)}, u32[]{:S(2)}, u32[]{:S(2)}) collective-permute-start(bf16[592,128]{1,0:T(8,128)(2,1)} %get-tuple-element.42.refs_0_), channel_id=1, source_target_pairs={{0,6},{1,7},{2,0},{3,1},{4,2},{5,3},{6,4},{7,5},{8,15},{9,14},{10,... | collective-permute-start | bytes 454664 | tf_op jit(solution)/shard_map/ppermute | solution.py:458
  10.4 0.9 %copy-start.3 = (bf16[560,128]{1,0:T(8,128)(2,1)S(1)}, bf16[560,128]{1,0:T(8,128)(2,1)}, u32[]{:S(2)}) copy-start(bf16[560,128]{1,0:T(8,128)(2,1)} %get-tuple-element.38.draft) | copy-start | bytes 430084
  11.3 10.3 %collective-permute-start.2 = (bf16[560,128]{1,0:T(8,128)(2,1)S(1)}, bf16[560,128]{1,0:T(8,128)(2,1)S(1)}, u32[]{:S(2)}, u32[]{:S(2)}) collective-permute-start(bf16[560,128]{1,0:T(8,128)(2,1)S(1)} %get-tuple-element.39), channel_id=1, source_target_pairs={{0,1},{1,0},{2,3},{3,2},{4,5},{5,4},{6,7},{7,6},{8,9},{9,8},{10,11... | collective-permute-start | bytes 430088 | tf_op jit(solution)/shard_map/ppermute | solution.py:448
  12.9 0.7 %collective-permute-start.3 = (bf16[256,128]{1,0:T(8,128)(2,1)S(1)}, bf16[256,128]{1,0:T(8,128)(2,1)S(1)}, u32[]{:S(2)}, u32[]{:S(2)}) collective-permute-start(bf16[256,128]{1,0:T(8,128)(2,1)S(1)} %get-tuple-element.40), channel_id=1, source_target_pairs={{1,2},{2,1},{3,4},{4,3},{5,6},{6,5},{9,10},{10,9},{11,12},{12,11},... | collective-permute-start | bytes 196616 | tf_op jit(solution)/shard_map/ppermute | solution.py:444
  21.6 2.5 %collective-permute-start.7 = (bf16[2080,128]{1,0:T(8,128)(2,1)S(1)}, bf16[2080,128]{1,0:T(8,128)(2,1)S(1)}, u32[]{:S(2)}, u32[]{:S(2)}) collective-permute-start(bf16[2080,128]{1,0:T(8,128)(2,1)S(1)} %shard_map.112.refs_1_), channel_id=1, source_target_pairs={{0,8},{8,0},{16,24},{24,16},{1,9},{9,1},{17,25},{25,17},{2,10},{10... | collective-permute-start | bytes 1597448 | tf_op jit(solution)/shard_map/ppermute | solution.py:448
  29.2 2.1 %collective-permute-start.8 = (bf16[4,592,128]{2,1,0:T(8,128)(2,1)S(1)}, bf16[4,592,128]{2,1,0:T(8,128)(2,1)S(1)}, u32[]{:S(2)}, u32[]{:S(2)}) collective-permute-start(bf16[4,592,128]{2,1,0:T(8,128)(2,1)S(1)} %get-tuple-element.60), channel_id=1, source_target_pairs={{0,8},{8,0},{16,24},{24,16},{1,9},{9,1},{17,25},{25,17},{2,10},{10... | collective-permute-start | bytes 1818632 | tf_op jit(solution)/shard_map/ppermute | solution.py:448
  31.5 12.1 %collective-permute-start.10 = (bf16[592,128]{1,0:T(8,128)(2,1)S(1)}, bf16[592,128]{1,0:T(8,128)(2,1)S(1)}, u32[]{:S(2)}, u32[]{:S(2)}) collective-permute-start(bf16[592,128]{1,0:T(8,128)(2,1)S(1)} %get-tuple-element.71), channel_id=1, source_target_pairs={{0,4},{1,5},{2,6},{3,7},{4,0},{5,1},{6,2},{7,3},{8,13},{9,12},{10,... | collective-permute-start | bytes 454664 | tf_op jit(solution)/shard_map/ppermute | solution.py:458
  35.5 12.5 %collective-permute-start.11 = (bf16[592,128]{1,0:T(8,128)(2,1)S(1)}, bf16[592,128]{1,0:T(8,128)(2,1)S(1)}, u32[]{:S(2)}, u32[]{:S(2)}) collective-permute-start(bf16[592,128]{1,0:T(8,128)(2,1)S(1)} %get-tuple-element.70), channel_id=1, source_target_pairs={{0,6},{1,7},{2,0},{3,1},{4,2},{5,3},{6,4},{7,5},{8,15},{9,14},{10,... | collective-permute-start | bytes 454664 | tf_op jit(solution)/shard_map/ppermute | solution.py:458
  36.2 11.8 %collective-permute-start.12 = (bf16[592,128]{1,0:T(8,128)(2,1)S(1)}, bf16[592,128]{1,0:T(8,128)(2,1)S(1)}, u32[]{:S(2)}, u32[]{:S(2)}) collective-permute-start(bf16[592,128]{1,0:T(8,128)(2,1)S(1)} %get-tuple-element.69), channel_id=1, source_target_pairs={{0,2},{1,3},{2,4},{3,5},{4,6},{5,7},{6,0},{7,1},{8,11},{9,10},{10,... | collective-permute-start | bytes 454664 | tf_op jit(solution)/shard_map/ppermute | solution.py:458
  37.5 10.5 %collective-permute-start.9 = (bf16[592,128]{1,0:T(8,128)(2,1)S(1)}, bf16[592,128]{1,0:T(8,128)(2,1)S(1)}, u32[]{:S(2)}, u32[]{:S(2)}) collective-permute-start(bf16[592,128]{1,0:T(8,128)(2,1)S(1)} %get-tuple-element.68), channel_id=1, source_target_pairs={{8,9},{9,8},{10,11},{11,10},{12,13},{13,12},{14,15},{15,14},{24,25... | collective-permute-start | bytes 454664 | tf_op jit(solution)/shard_map/ppermute | solution.py:458
  48.1 1.7 %collective-permute-start.13 = (f32[592,128]{1,0:T(8,128)S(1)}, f32[592,128]{1,0:T(8,128)S(1)}, u32[]{:S(2)}, u32[]{:S(2)}) collective-permute-start(f32[592,128]{1,0:T(8,128)S(1)} %convert_add_fusion.4), channel_id=1, source_target_pairs={{0,8},{8,0},{16,24},{24,16},{1,9},{9,1},{17,25},{25,17},{2,10},{10... | collective-permute-start | bytes 909320 | tf_op jit(solution)/shard_map/ppermute | solution.py:448
  49.8 6.0 %collective-permute-start.14 = (bf16[592,128]{1,0:T(8,128)(2,1)S(1)}, bf16[592,128]{1,0:T(8,128)(2,1)S(1)}, u32[]{:S(2)}, u32[]{:S(2)}) collective-permute-start(bf16[592,128]{1,0:T(8,128)(2,1)S(1)} %add_convert_fusion.total), channel_id=1, source_target_pairs={{0,16},{8,24},{16,0},{24,8},{1,17},{9,25},{17,1},{25,9},{2,18},{10... | collective-permute-start | bytes 454664 | tf_op jit(solution)/shard_map/ppermute | solution.py:475

commit v6 on v5

--- a/solution.py
+++ b/solution.py
@@ -131,7 +131,7 @@
 def put_columns(cols, row, head, tail):
     head, tail = head.astype(F32), tail.astype(F32)
     tiles = head.shape[1] // 128
-    for i, pixel in enumerate((head[0:1], head[1:2], tail[15:16])):
+    for i, pixel in enumerate((tail[15:16], head[0:1], head[1:2])):
         for v in range(tiles):
             at = (i * tiles + v) * 32 + row
             cols[at : at + 1] = pixel[:, v * 128 : (v + 1) * 128]
@@ -167,8 +167,11 @@
         put_columns(cols, to, rows[at : at + 16], rows[at + tc - 16 : at + tc])
     ends = [south[at : at + 16] for at in (3 * tc, 3 * tc + hc)]
     put_cotangent(cols, sizes.hr, jnp.concatenate(ends, axis=1))
-    beside[share:] = cols[...].astype(BF16)
-    edge[...] = cols[...].astype(BF16)
+    low = lax.rem(lax.axis_index("col"), 2)
+    skip = cols.shape[0] - edge.shape[0]
+    for out, first in ((beside.at[share:], skip * low), (edge, skip * (1 - low))):
+        first = pl.multiple_of(first, 16)
+        out[...] = cols[pl.ds(first, out.shape[0]), :].astype(BF16)
 
 
 def pass_kernel(beside, edge, *refs):
@@ -186,8 +189,7 @@
     cin, tc, tr, hc = region.shape[2], sizes.tc, sizes.tr, sizes.hc
     tiles = cin // 128
     for v in range(tiles):
-        at = (2 * tiles + v) * 32
-        left[:, v * 128 : (v + 1) * 128] = west[at : at + 32].astype(F32)
+        left[:, v * 128 : (v + 1) * 128] = west[v * 32 : (v + 1) * 32].astype(F32)
     cols[...] = jnp.zeros_like(cols)
     for v in range(cin // 128):
         lanes = slice(v * 128, (v + 1) * 128)
@@ -218,11 +220,11 @@
     cot_all[sizes.main : sizes.wide, :half] = south[3 * tc : 3 * tc + hc]
     cot_all[sizes.main : sizes.wide, half:] = south[3 * tc + hc :]
     for v in range(2 * half // 128):
-        at = 3 * tiles * 32 + v * 16
+        at = 2 * tiles * 32 + v * 16
         cot_all[sizes.wide :, v * 128 : (v + 1) * 128] = east[at : at + 16]
 
 
-def first_kernel(sizes, halves, x, *refs):
+def forward_part(sizes, halves, x, *refs):
     hidden, slope_one, hidden_two, slope_two, back, reduce_t = refs[3:9]
     pre, group_t, group, front, pre_two, beside = refs[9:]
     cin = reduce_t.shape[1]
@@ -303,7 +305,7 @@
         give[j, len(tiles) * shard :] = fold(total[theirs, rest : rest + 128]).astype(BF16)
 
 
-def second_kernel(sizes, halves, x, hidden_two, slope_two, cot, *refs):
+def middle_part(sizes, halves, x, hidden_two, slope_two, cot, *refs):
     active_three, grad_two, grad_side, own, short_t, total, expand_t, shift, beside = refs[3:]
     mid = expand_t.shape[1]
     width = expand_t.shape[0]
@@ -338,8 +340,8 @@
         grad_side[i * sizes.hc : (i + 1) * sizes.hc] = shift[i, 1 : sizes.hc + 1].astype(BF16)
 
 
-def third_kernel(
-    sizes, halves, cin, x, hidden, slope_one, back, grad_two, grad_side, late, *refs
+def backward_part(
+    sizes, halves, cin, x, hidden, slope_one, back, grad_two, grad_side, *refs
 ):
     grad_one, give = refs[:2]
     keeps = refs[2 : 2 + halves]
@@ -381,8 +383,27 @@
                     rows = slice(n * HALF + q * GW, n * HALF + (q + 1) * GW)
                     total[rows, cin : cin + 128] = sums[q]
                     total[rows, cin + 128 : cin + 256] = jnp.where(lane == 0, block, 0.0)
-    total[:, cin + 256 :] = late[...]
     split_out(halves, total, shard, cin + 128, keeps, give)
+
+
+def main_kernel(sizes, halves, cin, x, cot, own, passed, swapped, *refs):
+    active_three, grad_sum, short_t, reduce_t, grad_one, give = refs[:6]
+    keeps, refs = refs[6 : 6 + halves], refs[6 + halves :]
+    hidden, slope_one, hidden_two, slope_two, back, pre, group_t, group, front = refs[:9]
+    pre_two, beside, grad_two, grad_side, expand_t, shift, total = refs[9:]
+    weights = (own, passed, swapped)
+    forward_part(
+        sizes, halves, x, *weights, hidden, slope_one, hidden_two, slope_two, back, reduce_t,
+        pre, group_t, group, front, pre_two, beside,
+    )
+    middle_part(
+        sizes, halves, x, hidden_two, slope_two, cot, *weights, active_three, grad_two, grad_side,
+        grad_sum, short_t, total.at[:, cin + 256 :], expand_t, shift, beside,
+    )
+    backward_part(
+        sizes, halves, cin, x, hidden, slope_one, back, grad_two, grad_side, grad_one, give,
+        *keeps, total,
+    )
 
 
 def outputs_kernel(sizes, grad_one, reduce_t, grad_sum, short_t, active, block_out, region_grad, planes, spread_out):
@@ -486,6 +507,7 @@
     length = (early + late) // 128 * shard - shard + GW
     share = (length + 31) // 32 * 16
     halo = 3 * cin // 128 * 32 + width // 128 * 16
+    sent = halo - cin // 128 * 32
 
     def shape(dims, dtype=BF16):
         return jax.ShapeDtypeStruct(dims, dtype)
@@ -516,7 +538,7 @@
     rows_scratch = [scratch(4 * tile_cols, cin, dtype=BF16)] * 2
     beside, edge = call(
         functools.partial(columns_kernel, sizes),
-        (shape(draft.shape), shape((halo, 128))),
+        (shape((share + sent, 128)), shape((sent, 128))),
         rows_scratch + [scratch(halo, 128)],
         core_rows, far_rows, draft,
     )
@@ -526,8 +548,8 @@
         (shape((sizes.pixels, cin)), shape((sizes.out, width))),
         rows_scratch
         + [
-            scratch(halo, 128, dtype=BF16),
-            scratch(halo, 128, dtype=BF16),
+            scratch(sent, 128, dtype=BF16),
+            scratch(sent, 128, dtype=BF16),
             scratch(32, cin),
             scratch(cin // 128, tile_rows + 3, 8 + tile_cols, 128),
             scratch(3, cin // 128, 40, 128),
@@ -541,54 +563,37 @@
         beside, edge, *far,
     )
     blocks = [weights, passed, swap_even(passed, "row")]
-    hidden, slope_one, hidden_two, slope_two, back, reduce_t = call(
-        functools.partial(first_kernel, sizes, halves),
+    active_three, grad_sum, short_t, reduce_t, grad_one, give, *keeps = call(
+        functools.partial(main_kernel, sizes, halves, cin),
         (
-            shape((sizes.pixels, mid)),
-            shape((4 * sizes.main, mid), F32),
-            shape((sizes.out, mid)),
-            shape((sizes.out, mid), F32),
-            shape((mid // HALF, HALF, TAPS * HALF)),
+            shape((sizes.main, width)),
+            shape((sizes.main, width)),
+            shape((width, cin)),
             shape((mid, cin)),
-        ),
+            shape((4 * sizes.main, mid)),
+            shape((halves, length, 128)),
+        )
+        + (shape((length, 128), F32),) * halves,
         [
+            scratch(sizes.pixels, mid, dtype=BF16),
+            scratch(4 * sizes.main, mid),
+            scratch(sizes.out, mid, dtype=BF16),
+            scratch(sizes.out, mid),
+            scratch(mid // HALF, HALF, TAPS * HALF, dtype=BF16),
             scratch(sizes.pixels, mid),
             scratch(mid, 256, dtype=BF16),
             scratch(256, mid, dtype=BF16),
             scratch(mid // HALF, TAPS * HALF, HALF, dtype=BF16),
             scratch(sizes.out, mid),
             scratch(length, 128, dtype=BF16),
-        ],
-        x, *blocks,
-        flops=2 * sizes.pixels * cin * mid + 2 * sizes.out * TAPS * HALF * mid,
-    )
-    active_three, grad_two, grad_side, grad_sum, short_t, late_total = call(
-        functools.partial(second_kernel, sizes, halves),
-        (
-            shape((sizes.main, width)),
-            shape((sizes.wide, mid)),
-            shape((sizes.wide, mid)),
-            shape((sizes.main, width)),
-            shape((width, cin)),
-            shape((width, late), F32),
-        ),
-        [
+            scratch(sizes.wide, mid, dtype=BF16),
+            scratch(sizes.wide, mid, dtype=BF16),
             scratch(width, mid, dtype=BF16),
             scratch(sizes.hr + 1, 24, mid),
-            scratch(length, 128, dtype=BF16),
-        ],
-        x, hidden_two, slope_two, cot_all, *blocks,
-        flops=6 * sizes.out * width * (mid + cin),
-    )
-    grad_one, give, *keeps = call(
-        functools.partial(third_kernel, sizes, halves, cin),
-        (shape((4 * sizes.main, mid)), shape((halves, length, 128)))
-        + (shape((length, 128), F32),) * halves,
-        [
             scratch(mid, early + late),
         ],
-        x, hidden, slope_one, back, grad_two, grad_side, late_total,
-        flops=2 * 4 * sizes.main * cin * mid + 4 * sizes.main * TAPS * HALF * mid,
+        x, cot_all, *blocks,
+        flops=2 * sizes.pixels * cin * mid + 10 * sizes.out * TAPS * HALF * mid,
     )
     block_out, region_grad = call(
         functools.partial(outputs_kernel, sizes),

time: 56.8 us -> 55.3 us (0.974)
  waiting for transfers between devices: 27.2 us -> 24.1 us
  starting transfers between devices: 18.2 us -> 20.7 us
  Pallas kernels: 9.15 us -> 8.3 us
    ppermute x5, waiting for transfers between devices: 6.33 us -> 4.58 us  [swap_even(): lax.ppermute(x, axis, [(i, i ^ 1) for i in range(lax.axis_size(axis))])]
    ppermute x5, starting transfers between devices: 3.56 us -> 4.61 us  [swap_even(): lax.ppermute(x, axis, [(i, i ^ 1) for i in range(lax.axis_size(axis))])]
    ppermute x1, starting transfers between devices: 0.07 us -> 1.02 us  [reduce(): return (total, lax.ppermute(total, 'row', [(r, r ^ 2) for r in range(4)]))]
    ppermute x1, waiting for transfers between devices: 4.87 us -> 3.93 us  [reduce(): return (total, lax.ppermute(total, 'row', [(r, r ^ 2) for r in range(4)]))]
    pallas_call x9 -> x7, Pallas kernels: 9.15 us -> 8.3 us  [call(): pl.pallas_call(kernel, out_shape=out_shape, in_specs=[pl.BlockSpec(memory...]
where the time goes in v6:
time: 55.3 us; the launch traced here: 55.1 us
  waiting for transfers between devices  24.1 us (44%)
  starting transfers between devices  20.7 us (37%)
  Pallas kernels  8.3 us (15%)
  local copies, waits for them, and re-layouts  0.92 us (2%)
  between operations  0.76 us (1%)
    ppermute x7, waiting for transfers between devices, cross(): return lax.ppermute(x, ('row', 'col'), both(rows, cols, target))  15.6 us
    ppermute x7, starting transfers between devices, cross(): return lax.ppermute(x, ('row', 'col'), both(rows, cols, target))  13.6 us
    pallas_call x7, Pallas kernels, call(): pl.pallas_call(kernel, out_shape=out_shape, in_specs=[pl.BlockSpec(memory...  8.3 us
    ppermute x5, starting transfers between devices, swap_even(): lax.ppermute(x, axis, [(i, i ^ 1) for i in range(lax.axis_size(axis))])  4.61 us
    ppermute x5, waiting for transfers between devices, swap_even(): lax.ppermute(x, axis, [(i, i ^ 1) for i in range(lax.axis_size(axis))])  4.58 us
    ppermute x1, waiting for transfers between devices, reduce(): return (total, lax.ppermute(total, 'row', [(r, r ^ 2) for r in range(4)]))  3.93 us
    ppermute x2, starting transfers between devices, swap_odd(): return lax.ppermute(x, axis, pairs)  1.44 us
  transfers between devices with their start and end apart: 15, of which 8 were waited for; matrix products, arithmetic and copies ran while one was open for 0% of the time, Pallas kernels for 2%

profile of v6, /device:TPU:0, one launch (start us, length us, event | category | flops | bytes accessed | tf_op | source)
XLA Modules:
  0.0 55.1 jit_solution(11631467345819743476)
XLA Ops:
  0.6 1.9 %shard_map.109 = (bf16[592,128]{1,0:T(8,128)(2,1)}, bf16[128,256]{1,0:T(8,128)(2,1)}, bf16[560,128]{1,0:T(8,128)(2,1)}) custom-call(bf16[16,32,256]{2,1,0:T(8,128)(2,1)} %region.1, bf16[8,16,512]{2,1,0:T(8,128)(2,1)} %cot.1, bf16[64,256]{1,0:T(8,128)(2,1)} %bitcast.31, bf16[64,144]{1,0:T(8,128)(2,1)} %bitcast.32, bf16[64,512]{1,0:T(8,128)(2,1)} %bitcast.30, ...), custom_call_target="tpu_custom_call" | custom-call | bytes 903168 | tf_op jit(solution)/shard_map/pallas_call | solution.py:427
  2.5 0.5 collective-permute-start
  3.0 0.7 %collective-permute-start.1 = (bf16[128,256]{1,0:T(8,128)(2,1)}, bf16[128,256]{1,0:T(8,128)(2,1)S(1)}, u32[]{:S(2)}, u32[]{:S(2)}) collective-permute-start(bf16[128,256]{1,0:T(8,128)(2,1)} %get-tuple-element.29), channel_id=1, source_target_pairs={{8,16},{16,8},{9,17},{17,9},{10,18},{18,10},{11,19},{19,11},{12,20... | collective-permute-start | bytes 196616 | tf_op jit(solution)/shard_map/ppermute | solution.py:465
  3.7 2.6 %collective-permute-start.4 = (bf16[592,128]{1,0:T(8,128)(2,1)}, bf16[592,128]{1,0:T(8,128)(2,1)S(1)}, u32[]{:S(2)}, u32[]{:S(2)}) collective-permute-start(bf16[592,128]{1,0:T(8,128)(2,1)} %get-tuple-element.35.own), channel_id=1, source_target_pairs={{0,2},{1,3},{2,4},{3,5},{4,6},{5,7},{6,0},{7,1},{8,11},{9,10},{10,... | collective-permute-start | bytes 454664 | tf_op jit(solution)/shard_map/ppermute | solution.py:479
  6.3 2.6 %collective-permute-start.5 = (bf16[592,128]{1,0:T(8,128)(2,1)}, bf16[592,128]{1,0:T(8,128)(2,1)S(1)}, u32[]{:S(2)}, u32[]{:S(2)}) collective-permute-start(bf16[592,128]{1,0:T(8,128)(2,1)} %get-tuple-element.35.own), channel_id=1, source_target_pairs={{0,4},{1,5},{2,6},{3,7},{4,0},{5,1},{6,2},{7,3},{8,13},{9,12},{10,... | collective-permute-start | bytes 454664 | tf_op jit(solution)/shard_map/ppermute | solution.py:479
  8.9 1.3 %collective-permute-start.6 = (bf16[592,128]{1,0:T(8,128)(2,1)}, bf16[592,128]{1,0:T(8,128)(2,1)S(1)}, u32[]{:S(2)}, u32[]{:S(2)}) collective-permute-start(bf16[592,128]{1,0:T(8,128)(2,1)} %get-tuple-element.35.own), channel_id=1, source_target_pairs={{0,6},{1,7},{2,0},{3,1},{4,2},{5,3},{6,4},{7,5},{8,15},{9,14},{10,... | collective-permute-start | bytes 454664 | tf_op jit(solution)/shard_map/ppermute | solution.py:479
  10.3 0.0 collective-permute-done.core_rows
  10.3 0.0 collective-permute-done.1.far_rows
  10.3 0.0 copy-start.2
  10.3 0.9 %copy-done.2 = bf16[560,128]{1,0:T(8,128)(2,1)S(1)} copy-done((bf16[560,128]{1,0:T(8,128)(2,1)S(1)}, bf16[560,128]{1,0:T(8,128)(2,1)}, u32[]{:S(2)}) %copy-start.2) | copy-done | bytes 143384
  11.2 1.6 %collective-permute-start.2 = (bf16[496,128]{1,0:T(8,128)(2,1)S(1)}, bf16[496,128]{1,0:T(8,128)(2,1)S(1)}, u32[]{:S(2)}, u32[]{:S(2)}) collective-permute-start(bf16[496,128]{1,0:T(8,128)(2,1)S(1)} %get-tuple-element.31), channel_id=1, source_target_pairs={{0,1},{1,0},{2,3},{3,2},{4,5},{5,4},{6,7},{7,6},{8,9},{9,8},{10,11... | collective-permute-start | bytes 380936 | tf_op jit(solution)/shard_map/ppermute | solution.py:469
  12.8 0.0 copy-start
  12.8 0.0 copy-start.1
  12.8 0.8 %collective-permute-start.3 = (bf16[192,128]{1,0:T(8,128)(2,1)S(1)}, bf16[192,128]{1,0:T(8,128)(2,1)S(1)}, u32[]{:S(2)}, u32[]{:S(2)}) collective-permute-start(bf16[192,128]{1,0:T(8,128)(2,1)S(1)} %get-tuple-element.32), channel_id=1, source_target_pairs={{1,2},{2,1},{3,4},{4,3},{5,6},{6,5},{9,10},{10,9},{11,12},{12,11},... | collective-permute-start | bytes 147464 | tf_op jit(solution)/shard_map/ppermute | solution.py:465
  13.6 0.0 collective-permute-done.3.edge
  13.6 0.0 collective-permute-done.4.refs_0_
  13.6 6.1 %collective-permute-done.5.refs_1_ = bf16[592,128]{1,0:T(8,128)(2,1)S(1)} collective-permute-done((bf16[592,128]{1,0:T(8,128)(2,1)}, bf16[592,128]{1,0:T(8,128)(2,1)S(1)}, u32[]{:S(2)}, u32[]{:S(2)}) %collective-permute-start.5) | collective-permute-done | bytes 151584 | tf_op jit(solution)/shard_map/ppermute | solution.py:479
  19.7 0.0 collective-permute-done.6.refs_2_
  19.7 0.0 collective-permute-done.2.beside
  19.8 0.0 copy-start.3
  19.8 2.0 %collective-permute-start.7 = (bf16[2080,128]{1,0:T(8,128)(2,1)S(1)}, bf16[2080,128]{1,0:T(8,128)(2,1)S(1)}, u32[]{:S(2)}, u32[]{:S(2)}) collective-permute-start(bf16[2080,128]{1,0:T(8,128)(2,1)S(1)} %shard_map.112.passed), channel_id=1, source_target_pairs={{0,8},{8,0},{16,24},{24,16},{1,9},{9,1},{17,25},{25,17},{2,10},{10... | collective-permute-start | bytes 1597448 | tf_op jit(solution)/shard_map/ppermute | solution.py:469
  21.8 0.0 copy-done
  21.8 0.0 copy-done.1
  21.8 0.2 shard_map.111
  22.0 1.3 %collective-permute-done.7.swapped = bf16[2080,128]{1,0:T(8,128)(2,1)S(1)} collective-permute-done((bf16[2080,128]{1,0:T(8,128)(2,1)S(1)}, bf16[2080,128]{1,0:T(8,128)(2,1)S(1)}, u32[]{:S(2)}, u32[]{:S(2)}) %collective-permute-start.7) | collective-permute-done | bytes 532512 | tf_op jit(solution)/shard_map/ppermute | solution.py:469
  23.3 0.0 copy-done.3
  23.3 4.3 %shard_map.113 = (bf16[128,512]{1,0:T(8,128)(2,1)S(1)}, bf16[128,512]{1,0:T(8,128)(2,1)S(1)}, bf16[512,256]{1,0:T(8,128)(2,1)S(1)}, bf16[512,256]{1,0:T(8,128)(2...) custom-call(bf16[1056,256]{1,0:T(8,128)(2,1)S(1)} %get-tuple-element, ...), custom_call_target="tpu_custom_call" | custom-call | flops 2164260864 | bytes 5050368 | tf_op jit(solution)/shard_map/pallas_call | solution.py:427
  27.6 0.4 collective-permute-start.8
  28.1 1.7 %collective-permute-done.8 = bf16[4,592,128]{2,1,0:T(8,128)(2,1)S(1)} collective-permute-done((bf16[4,592,128]{2,1,0:T(8,128)(2,1)S(1)}, bf16[4,592,128]{2,1,0:T(8,128)(2,1)S(1)}, u32[]{:S(2)}, u32[]{:S(2)}) %collective-permute-start.8) | collective-permute-done | bytes 606240 | tf_op jit(solution)/shard_map/ppermute | solution.py:469
  29.7 0.1 fusion.3
  29.9 4.4 %collective-permute-start.10 = (bf16[592,128]{1,0:T(8,128)(2,1)S(1)}, bf16[592,128]{1,0:T(8,128)(2,1)S(1)}, u32[]{:S(2)}, u32[]{:S(2)}) collective-permute-start(bf16[592,128]{1,0:T(8,128)(2,1)S(1)} %get-tuple-element.55), channel_id=1, source_target_pairs={{0,4},{1,5},{2,6},{3,7},{4,0},{5,1},{6,2},{7,3},{8,13},{9,12},{10,... | collective-permute-start | bytes 454664 | tf_op jit(solution)/shard_map/ppermute | solution.py:479
  34.3 1.1 %collective-permute-start.11 = (bf16[592,128]{1,0:T(8,128)(2,1)S(1)}, bf16[592,128]{1,0:T(8,128)(2,1)S(1)}, u32[]{:S(2)}, u32[]{:S(2)}) collective-permute-start(bf16[592,128]{1,0:T(8,128)(2,1)S(1)} %get-tuple-element.54), channel_id=1, source_target_pairs={{0,6},{1,7},{2,0},{3,1},{4,2},{5,3},{6,4},{7,5},{8,15},{9,14},{10,... | collective-permute-start | bytes 454664 | tf_op jit(solution)/shard_map/ppermute | solution.py:479
  35.3 1.0 %collective-permute-start.12 = (bf16[592,128]{1,0:T(8,128)(2,1)S(1)}, bf16[592,128]{1,0:T(8,128)(2,1)S(1)}, u32[]{:S(2)}, u32[]{:S(2)}) collective-permute-start(bf16[592,128]{1,0:T(8,128)(2,1)S(1)} %get-tuple-element.53), channel_id=1, source_target_pairs={{0,2},{1,3},{2,4},{3,5},{4,6},{5,7},{6,0},{7,1},{8,11},{9,10},{10,... | collective-permute-start | bytes 454664 | tf_op jit(solution)/shard_map/ppermute | solution.py:479
  36.3 0.7 %collective-permute-start.9 = (bf16[592,128]{1,0:T(8,128)(2,1)S(1)}, bf16[592,128]{1,0:T(8,128)(2,1)S(1)}, u32[]{:S(2)}, u32[]{:S(2)}) collective-permute-start(bf16[592,128]{1,0:T(8,128)(2,1)S(1)} %get-tuple-element.52), channel_id=1, source_target_pairs={{8,9},{9,8},{10,11},{11,10},{12,13},{13,12},{14,15},{15,14},{24,25... | collective-permute-start | bytes 454664 | tf_op jit(solution)/shard_map/ppermute | solution.py:479
  37.0 5.4 %collective-permute-done.10 = bf16[592,128]{1,0:T(8,128)(2,1)S(1)} collective-permute-done((bf16[592,128]{1,0:T(8,128)(2,1)S(1)}, bf16[592,128]{1,0:T(8,128)(2,1)S(1)}, u32[]{:S(2)}, u32[]{:S(2)}) %collective-permute-start.10) | collective-permute-done | bytes 151584 | tf_op jit(solution)/shard_map/ppermute | solution.py:479
  42.3 0.5 collective-permute-done.11
  42.8 3.6 %collective-permute-done.12 = bf16[592,128]{1,0:T(8,128)(2,1)S(1)} collective-permute-done((bf16[592,128]{1,0:T(8,128)(2,1)S(1)}, bf16[592,128]{1,0:T(8,128)(2,1)S(1)}, u32[]{:S(2)}, u32[]{:S(2)}) %collective-permute-start.12) | collective-permute-done | bytes 151584 | tf_op jit(solution)/shard_map/ppermute | solution.py:479
  46.5 0.0 collective-permute-done.9
  46.5 0.1 convert_add_fusion.4
  46.6 0.1 collective-permute-start.13
  46.7 1.6 %collective-permute-done.13 = f32[592,128]{1,0:T(8,128)S(1)} collective-permute-done((f32[592,128]{1,0:T(8,128)S(1)}, f32[592,128]{1,0:T(8,128)S(1)}, u32[]{:S(2)}, u32[]{:S(2)}) %collective-permute-start.13) | collective-permute-done | bytes 303136 | tf_op jit(solution)/shard_map/ppermute | solution.py:469
  48.3 1.0 %collective-permute-start.14 = (bf16[592,128]{1,0:T(8,128)(2,1)S(1)}, bf16[592,128]{1,0:T(8,128)(2,1)S(1)}, u32[]{:S(2)}, u32[]{:S(2)}) collective-permute-start(bf16[592,128]{1,0:T(8,128)(2,1)S(1)} %add_convert_fusion.total), channel_id=1, source_target_pairs={{0,16},{8,24},{16,0},{24,8},{1,17},{9,25},{17,1},{25,9},{2,18},{10... | collective-permute-start | bytes 454664 | tf_op jit(solution)/shard_map/ppermute | solution.py:496
  49.3 1.1 %shard_map.114 = (bf16[8,16,512]{2,1,0:T(8,128)(2,1)}, bf16[16,32,256]{2,1,0:T(8,128)(2,1)}) custom-call(bf16[512,512]{1,0:T(8,128)(2,1)S(1)} %get-tuple-element.36.grad_one, bf16[512,256]{1,0:T(8,128)(2,1)S(1)} %get-tuple-element.37.reduce_t, bf16[128,512]{1,0:T(8,128)(2,1)S(1)} %get-tuple-element.38.grad_sum, ...), custom_call_target="tpu_custom_call" | custom-call | flops 134217728 | bytes 1703936 | tf_op jit(solution)/shard_map/pallas_call | solution.py:427
  50.4 3.9 %collective-permute-done.14.across = bf16[592,128]{1,0:T(8,128)(2,1)S(1)} collective-permute-done((bf16[592,128]{1,0:T(8,128)(2,1)S(1)}, bf16[592,128]{1,0:T(8,128)(2,1)S(1)}, u32[]{:S(2)}, u32[]{:S(2)}) %collective-permute-start.14) | collective-permute-done | bytes 151584 | tf_op jit(solution)/shard_map/ppermute | solution.py:496
  54.3 0.8 %shard_map.115 = (f32[64,256]{1,0:T(8,128)}, f32[64,144]{1,0:T(8,128)}, f32[64,512]{1,0:T(8,128)}, f32[64,256]{1,0:T(8,128)}) custom-call(bf16[592,128]{1,0:T(8,128)(2,1)S(1)} %add_convert_fusion.total, bf16[592,128]{1,0:T(8,128)(2,1)S(1)} %collective-permute-done.14.across), custom_call_target="tpu_custom_call" | custom-call | bytes 602112 | tf_op jit(solution)/shard_map/pallas_call | solution.py:427
  (3 shorter events, 0.1 us)
Async XLA Ops:
  2.5 7.8 %collective-permute-start = (bf16[128,256]{1,0:T(8,128)(2,1)}, bf16[128,256]{1,0:T(8,128)(2,1)S(1)}, u32[]{:S(2)}, u32[]{:S(2)}) collective-permute-start(bf16[128,256]{1,0:T(8,128)(2,1)} %get-tuple-element.29), channel_id=1, source_target_pairs={{0,8},{8,0},{16,24},{24,16},{1,9},{9,1},{17,25},{25,17},{2,10},{10... | collective-permute-start | bytes 196616 | tf_op jit(solution)/shard_map/ppermute | solution.py:469
  3.0 7.3 %collective-permute-start.1 = (bf16[128,256]{1,0:T(8,128)(2,1)}, bf16[128,256]{1,0:T(8,128)(2,1)S(1)}, u32[]{:S(2)}, u32[]{:S(2)}) collective-permute-start(bf16[128,256]{1,0:T(8,128)(2,1)} %get-tuple-element.29), channel_id=1, source_target_pairs={{8,16},{16,8},{9,17},{17,9},{10,18},{18,10},{11,19},{19,11},{12,20... | collective-permute-start | bytes 196616 | tf_op jit(solution)/shard_map/ppermute | solution.py:465
  3.7 9.9 %collective-permute-start.4 = (bf16[592,128]{1,0:T(8,128)(2,1)}, bf16[592,128]{1,0:T(8,128)(2,1)S(1)}, u32[]{:S(2)}, u32[]{:S(2)}) collective-permute-start(bf16[592,128]{1,0:T(8,128)(2,1)} %get-tuple-element.35.own), channel_id=1, source_target_pairs={{0,2},{1,3},{2,4},{3,5},{4,6},{5,7},{6,0},{7,1},{8,11},{9,10},{10,... | collective-permute-start | bytes 454664 | tf_op jit(solution)/shard_map/ppermute | solution.py:479
  6.3 13.4 %collective-permute-start.5 = (bf16[592,128]{1,0:T(8,128)(2,1)}, bf16[592,128]{1,0:T(8,128)(2,1)S(1)}, u32[]{:S(2)}, u32[]{:S(2)}) collective-permute-start(bf16[592,128]{1,0:T(8,128)(2,1)} %get-tuple-element.35.own), channel_id=1, source_target_pairs={{0,4},{1,5},{2,6},{3,7},{4,0},{5,1},{6,2},{7,3},{8,13},{9,12},{10,... | collective-permute-start | bytes 454664 | tf_op jit(solution)/shard_map/ppermute | solution.py:479
  8.9 10.8 %collective-permute-start.6 = (bf16[592,128]{1,0:T(8,128)(2,1)}, bf16[592,128]{1,0:T(8,128)(2,1)S(1)}, u32[]{:S(2)}, u32[]{:S(2)}) collective-permute-start(bf16[592,128]{1,0:T(8,128)(2,1)} %get-tuple-element.35.own), channel_id=1, source_target_pairs={{0,6},{1,7},{2,0},{3,1},{4,2},{5,3},{6,4},{7,5},{8,15},{9,14},{10,... | collective-permute-start | bytes 454664 | tf_op jit(solution)/shard_map/ppermute | solution.py:479
  10.3 0.9 %copy-start.2 = (bf16[560,128]{1,0:T(8,128)(2,1)S(1)}, bf16[560,128]{1,0:T(8,128)(2,1)}, u32[]{:S(2)}) copy-start(bf16[560,128]{1,0:T(8,128)(2,1)} %get-tuple-element.30.draft) | copy-start | bytes 430084
  11.2 8.5 %collective-permute-start.2 = (bf16[496,128]{1,0:T(8,128)(2,1)S(1)}, bf16[496,128]{1,0:T(8,128)(2,1)S(1)}, u32[]{:S(2)}, u32[]{:S(2)}) collective-permute-start(bf16[496,128]{1,0:T(8,128)(2,1)S(1)} %get-tuple-element.31), channel_id=1, source_target_pairs={{0,1},{1,0},{2,3},{3,2},{4,5},{5,4},{6,7},{7,6},{8,9},{9,8},{10,11... | collective-permute-start | bytes 380936 | tf_op jit(solution)/shard_map/ppermute | solution.py:469
  12.8 9.0 %copy-start = (bf16[16,32,256]{2,1,0:T(8,128)(2,1)S(1)}, bf16[16,32,256]{2,1,0:T(8,128)(2,1)}, u32[]{:S(2)}) copy-start(bf16[16,32,256]{2,1,0:T(8,128)(2,1)} %region.1) | copy-start | bytes 786436
  12.8 9.0 %copy-start.1 = (bf16[8,16,512]{2,1,0:T(8,128)(2,1)S(1)}, bf16[8,16,512]{2,1,0:T(8,128)(2,1)}, u32[]{:S(2)}) copy-start(bf16[8,16,512]{2,1,0:T(8,128)(2,1)} %cot.1) | copy-start | bytes 393220
  12.8 0.8 %collective-permute-start.3 = (bf16[192,128]{1,0:T(8,128)(2,1)S(1)}, bf16[192,128]{1,0:T(8,128)(2,1)S(1)}, u32[]{:S(2)}, u32[]{:S(2)}) collective-permute-start(bf16[192,128]{1,0:T(8,128)(2,1)S(1)} %get-tuple-element.32), channel_id=1, source_target_pairs={{1,2},{2,1},{3,4},{4,3},{5,6},{6,5},{9,10},{10,9},{11,12},{12,11},... | collective-permute-start | bytes 147464 | tf_op jit(solution)/shard_map/ppermute | solution.py:465
  19.8 3.6 %copy-start.3 = (bf16[592,128]{1,0:T(8,128)(2,1)S(1)}, bf16[592,128]{1,0:T(8,128)(2,1)}, u32[]{:S(2)}) copy-start(bf16[592,128]{1,0:T(8,128)(2,1)} %get-tuple-element.35.own) | copy-start | bytes 454660
  19.8 3.6 %collective-permute-start.7 = (bf16[2080,128]{1,0:T(8,128)(2,1)S(1)}, bf16[2080,128]{1,0:T(8,128)(2,1)S(1)}, u32[]{:S(2)}, u32[]{:S(2)}) collective-permute-start(bf16[2080,128]{1,0:T(8,128)(2,1)S(1)} %shard_map.112.passed), channel_id=1, source_target_pairs={{0,8},{8,0},{16,24},{24,16},{1,9},{9,1},{17,25},{25,17},{2,10},{10... | collective-permute-start | bytes 1597448 | tf_op jit(solution)/shard_map/ppermute | solution.py:469
  27.6 2.1 %collective-permute-start.8 = (bf16[4,592,128]{2,1,0:T(8,128)(2,1)S(1)}, bf16[4,592,128]{2,1,0:T(8,128)(2,1)S(1)}, u32[]{:S(2)}, u32[]{:S(2)}) collective-permute-start(bf16[4,592,128]{2,1,0:T(8,128)(2,1)S(1)} %get-tuple-element.44), channel_id=1, source_target_pairs={{0,8},{8,0},{16,24},{24,16},{1,9},{9,1},{17,25},{25,17},{2,10},{10... | collective-permute-start | bytes 1818632 | tf_op jit(solution)/shard_map/ppermute | solution.py:469
  29.9 12.5 %collective-permute-start.10 = (bf16[592,128]{1,0:T(8,128)(2,1)S(1)}, bf16[592,128]{1,0:T(8,128)(2,1)S(1)}, u32[]{:S(2)}, u32[]{:S(2)}) collective-permute-start(bf16[592,128]{1,0:T(8,128)(2,1)S(1)} %get-tuple-element.55), channel_id=1, source_target_pairs={{0,4},{1,5},{2,6},{3,7},{4,0},{5,1},{6,2},{7,3},{8,13},{9,12},{10,... | collective-permute-start | bytes 454664 | tf_op jit(solution)/shard_map/ppermute | solution.py:479
  34.3 8.6 %collective-permute-start.11 = (bf16[592,128]{1,0:T(8,128)(2,1)S(1)}, bf16[592,128]{1,0:T(8,128)(2,1)S(1)}, u32[]{:S(2)}, u32[]{:S(2)}) collective-permute-start(bf16[592,128]{1,0:T(8,128)(2,1)S(1)} %get-tuple-element.54), channel_id=1, source_target_pairs={{0,6},{1,7},{2,0},{3,1},{4,2},{5,3},{6,4},{7,5},{8,15},{9,14},{10,... | collective-permute-start | bytes 454664 | tf_op jit(solution)/shard_map/ppermute | solution.py:479
  35.3 11.1 %collective-permute-start.12 = (bf16[592,128]{1,0:T(8,128)(2,1)S(1)}, bf16[592,128]{1,0:T(8,128)(2,1)S(1)}, u32[]{:S(2)}, u32[]{:S(2)}) collective-permute-start(bf16[592,128]{1,0:T(8,128)(2,1)S(1)} %get-tuple-element.53), channel_id=1, source_target_pairs={{0,2},{1,3},{2,4},{3,5},{4,6},{5,7},{6,0},{7,1},{8,11},{9,10},{10,... | collective-permute-start | bytes 454664 | tf_op jit(solution)/shard_map/ppermute | solution.py:479
  36.3 10.2 %collective-permute-start.9 = (bf16[592,128]{1,0:T(8,128)(2,1)S(1)}, bf16[592,128]{1,0:T(8,128)(2,1)S(1)}, u32[]{:S(2)}, u32[]{:S(2)}) collective-permute-start(bf16[592,128]{1,0:T(8,128)(2,1)S(1)} %get-tuple-element.52), channel_id=1, source_target_pairs={{8,9},{9,8},{10,11},{11,10},{12,13},{13,12},{14,15},{15,14},{24,25... | collective-permute-start | bytes 454664 | tf_op jit(solution)/shard_map/ppermute | solution.py:479
  46.6 1.7 %collective-permute-start.13 = (f32[592,128]{1,0:T(8,128)S(1)}, f32[592,128]{1,0:T(8,128)S(1)}, u32[]{:S(2)}, u32[]{:S(2)}) collective-permute-start(f32[592,128]{1,0:T(8,128)S(1)} %convert_add_fusion.4), channel_id=1, source_target_pairs={{0,8},{8,0},{16,24},{24,16},{1,9},{9,1},{17,25},{25,17},{2,10},{10... | collective-permute-start | bytes 909320 | tf_op jit(solution)/shard_map/ppermute | solution.py:469
  48.3 6.0 %collective-permute-start.14 = (bf16[592,128]{1,0:T(8,128)(2,1)S(1)}, bf16[592,128]{1,0:T(8,128)(2,1)S(1)}, u32[]{:S(2)}, u32[]{:S(2)}) collective-permute-start(bf16[592,128]{1,0:T(8,128)(2,1)S(1)} %add_convert_fusion.total), channel_id=1, source_target_pairs={{0,16},{8,24},{16,0},{24,8},{1,17},{9,25},{17,1},{25,9},{2,18},{10... | collective-permute-start | bytes 454664 | tf_op jit(solution)/shard_map/ppermute | solution.py:496

commit v7 on v6

--- a/solution.py
+++ b/solution.py
@@ -435,8 +435,20 @@
     )(*operands)
 
 
-def finish_kernel(total, across, *outs):
-    value = total[...].astype(F32) + across[...].astype(F32)
+def chip_kernel(one, other, whole, part):
+    whole[...] = (one[...].astype(F32) + other[...].astype(F32)).astype(BF16)
+    core = lax.rem(lax.axis_index("row"), 2)
+    first = pl.multiple_of(core * (whole.shape[0] - part.shape[0]), 16)
+    part[...] = whole[pl.ds(first, part.shape[0]), :]
+
+
+def finish_kernel(whole, mine, theirs, *refs):
+    outs, across = refs[:-1], refs[-1]
+    core = lax.rem(lax.axis_index("row"), 2)
+    for ref, at in ((mine, core), (theirs, 1 - core)):
+        first = pl.multiple_of(at * (whole.shape[0] - ref.shape[0]), 16)
+        across[pl.ds(first, ref.shape[0]), :] = ref[...]
+    value = whole[...].astype(F32) + across[...].astype(F32)
     shard = outs[0].shape[0]
     at = 0
     for out in outs:
@@ -479,7 +491,7 @@
     return lax.ppermute(x, ("row", "col"), both(rows, cols, target))
 
 
-def reduce(keeps, give):
+def reduce(keeps, give, share):
     rows, halves = lax.axis_size("row"), lax.axis_size("col") // 2
     core = lax.axis_index("row") % 2
     other = swap_even(give, "row")
@@ -490,10 +502,19 @@
         if j == 0:
             came = jnp.where(core == 0, sums[0], came)
         total = came if total is None else total + came
+    part = jax.ShapeDtypeStruct((share, 128), BF16)
     if rows != 4:
-        return lax.psum(total, "row"), jnp.zeros_like(total)
-    total = (total + swap_even(total, "row")).astype(BF16)
-    return total, lax.ppermute(total, "row", [(r, r ^ 2) for r in range(4)])
+        nothing = jnp.zeros(part.shape, part.dtype)
+        return lax.psum(total, "row"), nothing, nothing
+    total = total.astype(BF16)
+    whole, part = call(
+        chip_kernel,
+        (jax.ShapeDtypeStruct(total.shape, BF16), part),
+        [],
+        total, swap_even(total, "row"),
+    )
+    across = lax.ppermute(part, "row", [(r, r ^ 2) for r in range(4)])
+    return whole, across, swap_even(across, "row")
 
 
 def per_device(region, reduce_weight, group_weight, expand_weight, shortcut_weight, cotangent):
@@ -605,12 +626,12 @@
         grad_one, reduce_t, grad_sum, short_t, active_three,
         flops=2 * 4 * sizes.main * cin * mid,
     )
-    total, across = reduce(keeps, give)
+    sums = reduce(keeps, give, share)
     grads = call(
         finish_kernel,
         tuple(shape((shard, lanes), F32) for lanes in (cin, taps, mid, cin)),
-        [],
-        total, across,
+        [scratch(length, 128, dtype=BF16)],
+        *sums,
     )
     return (block_out, region_grad, *(grad.T for grad in grads))
 

time: 55.3 us -> 54.9 us (level)
    pallas_call x7 -> x8, Pallas kernels: 8.3 us -> 8.39 us  [call(): pl.pallas_call(kernel, out_shape=out_shape, in_specs=[pl.BlockSpec(memory...]
    ppermute x5 -> x6, waiting for transfers between devices: 4.58 us -> 4.53 us  [swap_even(): lax.ppermute(x, axis, [(i, i ^ 1) for i in range(lax.axis_size(axis))])]
    ppermute x5 -> x6, starting transfers between devices: 4.61 us -> 4.62 us  [swap_even(): lax.ppermute(x, axis, [(i, i ^ 1) for i in range(lax.axis_size(axis))])]
  transfers between devices with their start and end apart: 15 -> 16, of which waited for: 8 -> 9; matrix products, arithmetic and copies ran while one was open for 0% -> 0% of each run, Pallas kernels for 2% -> 2%
where the time goes in v7:
time: 54.9 us; the launch traced here: 54.6 us
  waiting for transfers between devices  23.6 us (43%)
  starting transfers between devices  20.7 us (38%)
  Pallas kernels  8.39 us (15%)
  local copies, waits for them, and re-layouts  0.92 us (2%)
  between operations  0.76 us (1%)
    ppermute x7, waiting for transfers between devices, cross(): return lax.ppermute(x, ('row', 'col'), both(rows, cols, target))  15.6 us
    ppermute x7, starting transfers between devices, cross(): return lax.ppermute(x, ('row', 'col'), both(rows, cols, target))  13.6 us
    pallas_call x8, Pallas kernels, call(): pl.pallas_call(kernel, out_shape=out_shape, in_specs=[pl.BlockSpec(memory...  8.39 us
    ppermute x6, starting transfers between devices, swap_even(): lax.ppermute(x, axis, [(i, i ^ 1) for i in range(lax.axis_size(axis))])  4.62 us
    ppermute x6, waiting for transfers between devices, swap_even(): lax.ppermute(x, axis, [(i, i ^ 1) for i in range(lax.axis_size(axis))])  4.53 us
    ppermute x1, waiting for transfers between devices, reduce(): across = lax.ppermute(part, 'row', [(r, r ^ 2) for r in range(4)])  3.45 us
    ppermute x2, starting transfers between devices, swap_odd(): return lax.ppermute(x, axis, pairs)  1.44 us
  transfers between devices with their start and end apart: 16, of which 9 were waited for; matrix products, arithmetic and copies ran while one was open for 0% of the time, Pallas kernels for 2%

profile of v7, /device:TPU:0, one launch (start us, length us, event | category | flops | bytes accessed | tf_op | source)
XLA Modules:
  0.0 54.6 jit_solution(12660362569638140494)
XLA Ops:
  0.6 1.9 %shard_map.109 = (bf16[592,128]{1,0:T(8,128)(2,1)}, bf16[128,256]{1,0:T(8,128)(2,1)}, bf16[560,128]{1,0:T(8,128)(2,1)}) custom-call(bf16[16,32,256]{2,1,0:T(8,128)(2,1)} %region.1, bf16[8,16,512]{2,1,0:T(8,128)(2,1)} %cot.1, bf16[64,256]{1,0:T(8,128)(2,1)} %bitcast.31, bf16[64,144]{1,0:T(8,128)(2,1)} %bitcast.32, bf16[64,512]{1,0:T(8,128)(2,1)} %bitcast.30, ...), custom_call_target="tpu_custom_call" | custom-call | bytes 903168 | tf_op jit(solution)/shard_map/pallas_call | solution.py:427
  2.5 0.5 collective-permute-start
  3.0 0.7 %collective-permute-start.1 = (bf16[128,256]{1,0:T(8,128)(2,1)}, bf16[128,256]{1,0:T(8,128)(2,1)S(1)}, u32[]{:S(2)}, u32[]{:S(2)}) collective-permute-start(bf16[128,256]{1,0:T(8,128)(2,1)} %get-tuple-element.31), channel_id=1, source_target_pairs={{8,16},{16,8},{9,17},{17,9},{10,18},{18,10},{11,19},{19,11},{12,20... | collective-permute-start | bytes 196616 | tf_op jit(solution)/shard_map/ppermute | solution.py:477
  3.7 2.6 %collective-permute-start.4 = (bf16[592,128]{1,0:T(8,128)(2,1)}, bf16[592,128]{1,0:T(8,128)(2,1)S(1)}, u32[]{:S(2)}, u32[]{:S(2)}) collective-permute-start(bf16[592,128]{1,0:T(8,128)(2,1)} %get-tuple-element.37.own), channel_id=1, source_target_pairs={{0,2},{1,3},{2,4},{3,5},{4,6},{5,7},{6,0},{7,1},{8,11},{9,10},{10,... | collective-permute-start | bytes 454664 | tf_op jit(solution)/shard_map/ppermute | solution.py:491
  6.3 2.6 %collective-permute-start.5 = (bf16[592,128]{1,0:T(8,128)(2,1)}, bf16[592,128]{1,0:T(8,128)(2,1)S(1)}, u32[]{:S(2)}, u32[]{:S(2)}) collective-permute-start(bf16[592,128]{1,0:T(8,128)(2,1)} %get-tuple-element.37.own), channel_id=1, source_target_pairs={{0,4},{1,5},{2,6},{3,7},{4,0},{5,1},{6,2},{7,3},{8,13},{9,12},{10,... | collective-permute-start | bytes 454664 | tf_op jit(solution)/shard_map/ppermute | solution.py:491
  8.9 1.3 %collective-permute-start.6 = (bf16[592,128]{1,0:T(8,128)(2,1)}, bf16[592,128]{1,0:T(8,128)(2,1)S(1)}, u32[]{:S(2)}, u32[]{:S(2)}) collective-permute-start(bf16[592,128]{1,0:T(8,128)(2,1)} %get-tuple-element.37.own), channel_id=1, source_target_pairs={{0,6},{1,7},{2,0},{3,1},{4,2},{5,3},{6,4},{7,5},{8,15},{9,14},{10,... | collective-permute-start | bytes 454664 | tf_op jit(solution)/shard_map/ppermute | solution.py:491
  10.3 0.0 collective-permute-done.core_rows
  10.3 0.0 collective-permute-done.1.far_rows
  10.3 0.0 copy-start.2
  10.3 0.9 %copy-done.2 = bf16[560,128]{1,0:T(8,128)(2,1)S(1)} copy-done((bf16[560,128]{1,0:T(8,128)(2,1)S(1)}, bf16[560,128]{1,0:T(8,128)(2,1)}, u32[]{:S(2)}) %copy-start.2) | copy-done | bytes 143384
  11.2 1.6 %collective-permute-start.2 = (bf16[496,128]{1,0:T(8,128)(2,1)S(1)}, bf16[496,128]{1,0:T(8,128)(2,1)S(1)}, u32[]{:S(2)}, u32[]{:S(2)}) collective-permute-start(bf16[496,128]{1,0:T(8,128)(2,1)S(1)} %get-tuple-element.33), channel_id=1, source_target_pairs={{0,1},{1,0},{2,3},{3,2},{4,5},{5,4},{6,7},{7,6},{8,9},{9,8},{10,11... | collective-permute-start | bytes 380936 | tf_op jit(solution)/shard_map/ppermute | solution.py:481
  12.8 0.0 copy-start
  12.8 0.0 copy-start.1
  12.8 0.8 %collective-permute-start.3 = (bf16[192,128]{1,0:T(8,128)(2,1)S(1)}, bf16[192,128]{1,0:T(8,128)(2,1)S(1)}, u32[]{:S(2)}, u32[]{:S(2)}) collective-permute-start(bf16[192,128]{1,0:T(8,128)(2,1)S(1)} %get-tuple-element.34), channel_id=1, source_target_pairs={{1,2},{2,1},{3,4},{4,3},{5,6},{6,5},{9,10},{10,9},{11,12},{12,11},... | collective-permute-start | bytes 147464 | tf_op jit(solution)/shard_map/ppermute | solution.py:477
  13.6 0.0 collective-permute-done.3.edge
  13.6 0.0 collective-permute-done.4.refs_0_
  13.6 6.1 %collective-permute-done.5.refs_1_ = bf16[592,128]{1,0:T(8,128)(2,1)S(1)} collective-permute-done((bf16[592,128]{1,0:T(8,128)(2,1)}, bf16[592,128]{1,0:T(8,128)(2,1)S(1)}, u32[]{:S(2)}, u32[]{:S(2)}) %collective-permute-start.5) | collective-permute-done | bytes 151584 | tf_op jit(solution)/shard_map/ppermute | solution.py:491
  19.7 0.0 collective-permute-done.6.refs_2_
  19.7 0.0 collective-permute-done.2.beside
  19.8 0.0 copy-start.3
  19.8 2.0 %collective-permute-start.7 = (bf16[2080,128]{1,0:T(8,128)(2,1)S(1)}, bf16[2080,128]{1,0:T(8,128)(2,1)S(1)}, u32[]{:S(2)}, u32[]{:S(2)}) collective-permute-start(bf16[2080,128]{1,0:T(8,128)(2,1)S(1)} %shard_map.112.passed), channel_id=1, source_target_pairs={{0,8},{8,0},{16,24},{24,16},{1,9},{9,1},{17,25},{25,17},{2,10},{10... | collective-permute-start | bytes 1597448 | tf_op jit(solution)/shard_map/ppermute | solution.py:481
  21.8 0.0 copy-done
  21.8 0.0 copy-done.1
  21.8 0.2 shard_map.111
  22.0 1.3 %collective-permute-done.7.swapped = bf16[2080,128]{1,0:T(8,128)(2,1)S(1)} collective-permute-done((bf16[2080,128]{1,0:T(8,128)(2,1)S(1)}, bf16[2080,128]{1,0:T(8,128)(2,1)S(1)}, u32[]{:S(2)}, u32[]{:S(2)}) %collective-permute-start.7) | collective-permute-done | bytes 532512 | tf_op jit(solution)/shard_map/ppermute | solution.py:481
  23.3 0.0 copy-done.3
  23.3 4.3 %shard_map.113 = (bf16[128,512]{1,0:T(8,128)(2,1)S(1)}, bf16[128,512]{1,0:T(8,128)(2,1)S(1)}, bf16[512,256]{1,0:T(8,128)(2,1)S(1)}, bf16[512,256]{1,0:T(8,128)(2...) custom-call(bf16[1056,256]{1,0:T(8,128)(2,1)S(1)} %get-tuple-element, ...), custom_call_target="tpu_custom_call" | custom-call | flops 2164260864 | bytes 5050368 | tf_op jit(solution)/shard_map/pallas_call | solution.py:427
  27.7 0.4 collective-permute-start.8
  28.1 1.7 %collective-permute-done.8 = bf16[4,592,128]{2,1,0:T(8,128)(2,1)S(1)} collective-permute-done((bf16[4,592,128]{2,1,0:T(8,128)(2,1)S(1)}, bf16[4,592,128]{2,1,0:T(8,128)(2,1)S(1)}, u32[]{:S(2)}, u32[]{:S(2)}) %collective-permute-start.8) | collective-permute-done | bytes 606240 | tf_op jit(solution)/shard_map/ppermute | solution.py:481
  29.8 0.1 fusion.3
  29.9 4.4 %collective-permute-start.10 = (bf16[592,128]{1,0:T(8,128)(2,1)S(1)}, bf16[592,128]{1,0:T(8,128)(2,1)S(1)}, u32[]{:S(2)}, u32[]{:S(2)}) collective-permute-start(bf16[592,128]{1,0:T(8,128)(2,1)S(1)} %get-tuple-element.59), channel_id=1, source_target_pairs={{0,4},{1,5},{2,6},{3,7},{4,0},{5,1},{6,2},{7,3},{8,13},{9,12},{10,... | collective-permute-start | bytes 454664 | tf_op jit(solution)/shard_map/ppermute | solution.py:491
  34.3 1.1 %collective-permute-start.11 = (bf16[592,128]{1,0:T(8,128)(2,1)S(1)}, bf16[592,128]{1,0:T(8,128)(2,1)S(1)}, u32[]{:S(2)}, u32[]{:S(2)}) collective-permute-start(bf16[592,128]{1,0:T(8,128)(2,1)S(1)} %get-tuple-element.58), channel_id=1, source_target_pairs={{0,6},{1,7},{2,0},{3,1},{4,2},{5,3},{6,4},{7,5},{8,15},{9,14},{10,... | collective-permute-start | bytes 454664 | tf_op jit(solution)/shard_map/ppermute | solution.py:491
  35.3 1.0 %collective-permute-start.12 = (bf16[592,128]{1,0:T(8,128)(2,1)S(1)}, bf16[592,128]{1,0:T(8,128)(2,1)S(1)}, u32[]{:S(2)}, u32[]{:S(2)}) collective-permute-start(bf16[592,128]{1,0:T(8,128)(2,1)S(1)} %get-tuple-element.57), channel_id=1, source_target_pairs={{0,2},{1,3},{2,4},{3,5},{4,6},{5,7},{6,0},{7,1},{8,11},{9,10},{10,... | collective-permute-start | bytes 454664 | tf_op jit(solution)/shard_map/ppermute | solution.py:491
  36.3 0.7 %collective-permute-start.9 = (bf16[592,128]{1,0:T(8,128)(2,1)S(1)}, bf16[592,128]{1,0:T(8,128)(2,1)S(1)}, u32[]{:S(2)}, u32[]{:S(2)}) collective-permute-start(bf16[592,128]{1,0:T(8,128)(2,1)S(1)} %get-tuple-element.56), channel_id=1, source_target_pairs={{8,9},{9,8},{10,11},{11,10},{12,13},{13,12},{14,15},{15,14},{24,25... | collective-permute-start | bytes 454664 | tf_op jit(solution)/shard_map/ppermute | solution.py:491
  37.0 5.4 %collective-permute-done.10 = bf16[592,128]{1,0:T(8,128)(2,1)S(1)} collective-permute-done((bf16[592,128]{1,0:T(8,128)(2,1)S(1)}, bf16[592,128]{1,0:T(8,128)(2,1)S(1)}, u32[]{:S(2)}, u32[]{:S(2)}) %collective-permute-start.10) | collective-permute-done | bytes 151584 | tf_op jit(solution)/shard_map/ppermute | solution.py:491
  42.4 0.5 collective-permute-done.11
  42.8 3.6 %collective-permute-done.12 = bf16[592,128]{1,0:T(8,128)(2,1)S(1)} collective-permute-done((bf16[592,128]{1,0:T(8,128)(2,1)S(1)}, bf16[592,128]{1,0:T(8,128)(2,1)S(1)}, u32[]{:S(2)}, u32[]{:S(2)}) %collective-permute-start.12) | collective-permute-done | bytes 151584 | tf_op jit(solution)/shard_map/ppermute | solution.py:491
  46.5 0.0 collective-permute-done.9
  46.5 0.1 add_convert_fusion.one
  46.6 0.1 collective-permute-start.13
  46.7 1.4 %collective-permute-done.13.other = bf16[592,128]{1,0:T(8,128)(2,1)S(1)} collective-permute-done((bf16[592,128]{1,0:T(8,128)(2,1)S(1)}, bf16[592,128]{1,0:T(8,128)(2,1)S(1)}, u32[]{:S(2)}, u32[]{:S(2)}) %collective-permute-start.13) | collective-permute-done | bytes 151584 | tf_op jit(solution)/shard_map/ppermute | solution.py:481
  48.0 0.1 shard_map.115
  48.1 1.0 %collective-permute-start.14 = (bf16[304,128]{1,0:T(8,128)(2,1)S(1)}, bf16[304,128]{1,0:T(8,128)(2,1)S(1)}, u32[]{:S(2)}, u32[]{:S(2)}) collective-permute-start(bf16[304,128]{1,0:T(8,128)(2,1)S(1)} %get-tuple-element.51), channel_id=1, source_target_pairs={{0,16},{8,24},{16,0},{24,8},{1,17},{9,25},{17,1},{25,9},{2,18},{10... | collective-permute-start | bytes 233480 | tf_op jit(solution)/shard_map/ppermute | solution.py:516
  49.1 3.4 %collective-permute-done.14.mine = bf16[304,128]{1,0:T(8,128)(2,1)S(1)} collective-permute-done((bf16[304,128]{1,0:T(8,128)(2,1)S(1)}, bf16[304,128]{1,0:T(8,128)(2,1)S(1)}, u32[]{:S(2)}, u32[]{:S(2)}) %collective-permute-start.14) | collective-permute-done | bytes 77856 | tf_op jit(solution)/shard_map/ppermute | solution.py:516
  52.6 0.0 collective-permute-start.15
  52.6 1.1 %shard_map.114 = (bf16[8,16,512]{2,1,0:T(8,128)(2,1)}, bf16[16,32,256]{2,1,0:T(8,128)(2,1)}) custom-call(bf16[512,512]{1,0:T(8,128)(2,1)S(1)} %get-tuple-element.38.grad_one, bf16[512,256]{1,0:T(8,128)(2,1)S(1)} %get-tuple-element.39.reduce_t, bf16[128,512]{1,0:T(8,128)(2,1)S(1)} %get-tuple-element.40.grad_sum, ...), custom_call_target="tpu_custom_call" | custom-call | flops 134217728 | bytes 1703936 | tf_op jit(solution)/shard_map/pallas_call | solution.py:427
  53.7 0.2 collective-permute-done.15.theirs
  53.9 0.8 %shard_map.116 = (f32[64,256]{1,0:T(8,128)}, f32[64,144]{1,0:T(8,128)}, f32[64,512]{1,0:T(8,128)}, f32[64,256]{1,0:T(8,128)}) custom-call(bf16[592,128]{1,0:T(8,128)(2,1)S(1)} %get-tuple-element.50.whole, bf16[304,128]{1,0:T(8,128)(2,1)S(1)} %collective-permute-done.14.mine, bf16[304,128]{1,0:T(8,128)(2,1)S(1)} %collective-permute-done.15.theirs), custom_call_target="tpu_custom_call" | custom-call | bytes 606208 | tf_op jit(solution)/shard_map/pallas_call | solution.py:427
  (2 shorter events, 0.1 us)
Async XLA Ops:
  2.5 7.8 %collective-permute-start = (bf16[128,256]{1,0:T(8,128)(2,1)}, bf16[128,256]{1,0:T(8,128)(2,1)S(1)}, u32[]{:S(2)}, u32[]{:S(2)}) collective-permute-start(bf16[128,256]{1,0:T(8,128)(2,1)} %get-tuple-element.31), channel_id=1, source_target_pairs={{0,8},{8,0},{16,24},{24,16},{1,9},{9,1},{17,25},{25,17},{2,10},{10... | collective-permute-start | bytes 196616 | tf_op jit(solution)/shard_map/ppermute | solution.py:481
  3.0 7.3 %collective-permute-start.1 = (bf16[128,256]{1,0:T(8,128)(2,1)}, bf16[128,256]{1,0:T(8,128)(2,1)S(1)}, u32[]{:S(2)}, u32[]{:S(2)}) collective-permute-start(bf16[128,256]{1,0:T(8,128)(2,1)} %get-tuple-element.31), channel_id=1, source_target_pairs={{8,16},{16,8},{9,17},{17,9},{10,18},{18,10},{11,19},{19,11},{12,20... | collective-permute-start | bytes 196616 | tf_op jit(solution)/shard_map/ppermute | solution.py:477
  3.7 9.9 %collective-permute-start.4 = (bf16[592,128]{1,0:T(8,128)(2,1)}, bf16[592,128]{1,0:T(8,128)(2,1)S(1)}, u32[]{:S(2)}, u32[]{:S(2)}) collective-permute-start(bf16[592,128]{1,0:T(8,128)(2,1)} %get-tuple-element.37.own), channel_id=1, source_target_pairs={{0,2},{1,3},{2,4},{3,5},{4,6},{5,7},{6,0},{7,1},{8,11},{9,10},{10,... | collective-permute-start | bytes 454664 | tf_op jit(solution)/shard_map/ppermute | solution.py:491
  6.3 13.4 %collective-permute-start.5 = (bf16[592,128]{1,0:T(8,128)(2,1)}, bf16[592,128]{1,0:T(8,128)(2,1)S(1)}, u32[]{:S(2)}, u32[]{:S(2)}) collective-permute-start(bf16[592,128]{1,0:T(8,128)(2,1)} %get-tuple-element.37.own), channel_id=1, source_target_pairs={{0,4},{1,5},{2,6},{3,7},{4,0},{5,1},{6,2},{7,3},{8,13},{9,12},{10,... | collective-permute-start | bytes 454664 | tf_op jit(solution)/shard_map/ppermute | solution.py:491
  8.9 10.8 %collective-permute-start.6 = (bf16[592,128]{1,0:T(8,128)(2,1)}, bf16[592,128]{1,0:T(8,128)(2,1)S(1)}, u32[]{:S(2)}, u32[]{:S(2)}) collective-permute-start(bf16[592,128]{1,0:T(8,128)(2,1)} %get-tuple-element.37.own), channel_id=1, source_target_pairs={{0,6},{1,7},{2,0},{3,1},{4,2},{5,3},{6,4},{7,5},{8,15},{9,14},{10,... | collective-permute-start | bytes 454664 | tf_op jit(solution)/shard_map/ppermute | solution.py:491
  10.3 0.9 %copy-start.2 = (bf16[560,128]{1,0:T(8,128)(2,1)S(1)}, bf16[560,128]{1,0:T(8,128)(2,1)}, u32[]{:S(2)}) copy-start(bf16[560,128]{1,0:T(8,128)(2,1)} %get-tuple-element.32.draft) | copy-start | bytes 430084
  11.2 8.5 %collective-permute-start.2 = (bf16[496,128]{1,0:T(8,128)(2,1)S(1)}, bf16[496,128]{1,0:T(8,128)(2,1)S(1)}, u32[]{:S(2)}, u32[]{:S(2)}) collective-permute-start(bf16[496,128]{1,0:T(8,128)(2,1)S(1)} %get-tuple-element.33), channel_id=1, source_target_pairs={{0,1},{1,0},{2,3},{3,2},{4,5},{5,4},{6,7},{7,6},{8,9},{9,8},{10,11... | collective-permute-start | bytes 380936 | tf_op jit(solution)/shard_map/ppermute | solution.py:481
  12.8 9.0 %copy-start = (bf16[16,32,256]{2,1,0:T(8,128)(2,1)S(1)}, bf16[16,32,256]{2,1,0:T(8,128)(2,1)}, u32[]{:S(2)}) copy-start(bf16[16,32,256]{2,1,0:T(8,128)(2,1)} %region.1) | copy-start | bytes 786436
  12.8 9.0 %copy-start.1 = (bf16[8,16,512]{2,1,0:T(8,128)(2,1)S(1)}, bf16[8,16,512]{2,1,0:T(8,128)(2,1)}, u32[]{:S(2)}) copy-start(bf16[8,16,512]{2,1,0:T(8,128)(2,1)} %cot.1) | copy-start | bytes 393220
  12.8 0.8 %collective-permute-start.3 = (bf16[192,128]{1,0:T(8,128)(2,1)S(1)}, bf16[192,128]{1,0:T(8,128)(2,1)S(1)}, u32[]{:S(2)}, u32[]{:S(2)}) collective-permute-start(bf16[192,128]{1,0:T(8,128)(2,1)S(1)} %get-tuple-element.34), channel_id=1, source_target_pairs={{1,2},{2,1},{3,4},{4,3},{5,6},{6,5},{9,10},{10,9},{11,12},{12,11},... | collective-permute-start | bytes 147464 | tf_op jit(solution)/shard_map/ppermute | solution.py:477
  19.8 3.6 %copy-start.3 = (bf16[592,128]{1,0:T(8,128)(2,1)S(1)}, bf16[592,128]{1,0:T(8,128)(2,1)}, u32[]{:S(2)}) copy-start(bf16[592,128]{1,0:T(8,128)(2,1)} %get-tuple-element.37.own) | copy-start | bytes 454660
  19.8 3.6 %collective-permute-start.7 = (bf16[2080,128]{1,0:T(8,128)(2,1)S(1)}, bf16[2080,128]{1,0:T(8,128)(2,1)S(1)}, u32[]{:S(2)}, u32[]{:S(2)}) collective-permute-start(bf16[2080,128]{1,0:T(8,128)(2,1)S(1)} %shard_map.112.passed), channel_id=1, source_target_pairs={{0,8},{8,0},{16,24},{24,16},{1,9},{9,1},{17,25},{25,17},{2,10},{10... | collective-permute-start | bytes 1597448 | tf_op jit(solution)/shard_map/ppermute | solution.py:481
  27.7 2.1 %collective-permute-start.8 = (bf16[4,592,128]{2,1,0:T(8,128)(2,1)S(1)}, bf16[4,592,128]{2,1,0:T(8,128)(2,1)S(1)}, u32[]{:S(2)}, u32[]{:S(2)}) collective-permute-start(bf16[4,592,128]{2,1,0:T(8,128)(2,1)S(1)} %get-tuple-element.46), channel_id=1, source_target_pairs={{0,8},{8,0},{16,24},{24,16},{1,9},{9,1},{17,25},{25,17},{2,10},{10... | collective-permute-start | bytes 1818632 | tf_op jit(solution)/shard_map/ppermute | solution.py:481
  29.9 12.5 %collective-permute-start.10 = (bf16[592,128]{1,0:T(8,128)(2,1)S(1)}, bf16[592,128]{1,0:T(8,128)(2,1)S(1)}, u32[]{:S(2)}, u32[]{:S(2)}) collective-permute-start(bf16[592,128]{1,0:T(8,128)(2,1)S(1)} %get-tuple-element.59), channel_id=1, source_target_pairs={{0,4},{1,5},{2,6},{3,7},{4,0},{5,1},{6,2},{7,3},{8,13},{9,12},{10,... | collective-permute-start | bytes 454664 | tf_op jit(solution)/shard_map/ppermute | solution.py:491
  34.3 8.6 %collective-permute-start.11 = (bf16[592,128]{1,0:T(8,128)(2,1)S(1)}, bf16[592,128]{1,0:T(8,128)(2,1)S(1)}, u32[]{:S(2)}, u32[]{:S(2)}) collective-permute-start(bf16[592,128]{1,0:T(8,128)(2,1)S(1)} %get-tuple-element.58), channel_id=1, source_target_pairs={{0,6},{1,7},{2,0},{3,1},{4,2},{5,3},{6,4},{7,5},{8,15},{9,14},{10,... | collective-permute-start | bytes 454664 | tf_op jit(solution)/shard_map/ppermute | solution.py:491
  35.3 11.1 %collective-permute-start.12 = (bf16[592,128]{1,0:T(8,128)(2,1)S(1)}, bf16[592,128]{1,0:T(8,128)(2,1)S(1)}, u32[]{:S(2)}, u32[]{:S(2)}) collective-permute-start(bf16[592,128]{1,0:T(8,128)(2,1)S(1)} %get-tuple-element.57), channel_id=1, source_target_pairs={{0,2},{1,3},{2,4},{3,5},{4,6},{5,7},{6,0},{7,1},{8,11},{9,10},{10,... | collective-permute-start | bytes 454664 | tf_op jit(solution)/shard_map/ppermute | solution.py:491
  36.3 10.2 %collective-permute-start.9 = (bf16[592,128]{1,0:T(8,128)(2,1)S(1)}, bf16[592,128]{1,0:T(8,128)(2,1)S(1)}, u32[]{:S(2)}, u32[]{:S(2)}) collective-permute-start(bf16[592,128]{1,0:T(8,128)(2,1)S(1)} %get-tuple-element.56), channel_id=1, source_target_pairs={{8,9},{9,8},{10,11},{11,10},{12,13},{13,12},{14,15},{15,14},{24,25... | collective-permute-start | bytes 454664 | tf_op jit(solution)/shard_map/ppermute | solution.py:491
  46.6 1.4 %collective-permute-start.13 = (bf16[592,128]{1,0:T(8,128)(2,1)S(1)}, bf16[592,128]{1,0:T(8,128)(2,1)S(1)}, u32[]{:S(2)}, u32[]{:S(2)}) collective-permute-start(bf16[592,128]{1,0:T(8,128)(2,1)S(1)} %add_convert_fusion.one), channel_id=1, source_target_pairs={{0,8},{8,0},{16,24},{24,16},{1,9},{9,1},{17,25},{25,17},{2,10},{10... | collective-permute-start | bytes 454664 | tf_op jit(solution)/shard_map/ppermute | solution.py:481
  48.1 4.5 %collective-permute-start.14 = (bf16[304,128]{1,0:T(8,128)(2,1)S(1)}, bf16[304,128]{1,0:T(8,128)(2,1)S(1)}, u32[]{:S(2)}, u32[]{:S(2)}) collective-permute-start(bf16[304,128]{1,0:T(8,128)(2,1)S(1)} %get-tuple-element.51), channel_id=1, source_target_pairs={{0,16},{8,24},{16,0},{24,8},{1,17},{9,25},{17,1},{25,9},{2,18},{10... | collective-permute-start | bytes 233480 | tf_op jit(solution)/shard_map/ppermute | solution.py:516
  52.6 1.3 %collective-permute-start.15 = (bf16[304,128]{1,0:T(8,128)(2,1)S(1)}, bf16[304,128]{1,0:T(8,128)(2,1)S(1)}, u32[]{:S(2)}, u32[]{:S(2)}) collective-permute-start(bf16[304,128]{1,0:T(8,128)(2,1)S(1)} %collective-permute-done.14.mine), channel_id=1, source_target_pairs={{0,8},{8,0},{16,24},{24,16},{1,9},{9,1},{17,25},{25,17},{2,10},{10... | collective-permute-start | bytes 233480 | tf_op jit(solution)/shard_map/ppermute | solution.py:481

commit v8 on v7

--- a/solution.py
+++ b/solution.py
@@ -418,7 +418,7 @@
                 lanes = slice(v * 128, (v + 1) * 128)
                 spread_out[v, 2 * r + i // 2, pl.ds(i % 2, hc, stride=2)] = planes[at : at + hc, lanes]
     for v in range(cin // 128):
-        region_grad[:, :, v * 128 : (v + 1) * 128] = spread_out[v].astype(BF16)
+        region_grad[:, :, v * 128 : (v + 1) * 128] = spread_out[v, :, : sizes.tc].astype(BF16)
 
 
 def call(kernel, out_shape, scratch, *operands, flops=0, space=pltpu.VMEM, limit=VMEM_LIMIT):
@@ -572,7 +572,7 @@
             scratch(sent, 128, dtype=BF16),
             scratch(sent, 128, dtype=BF16),
             scratch(32, cin),
-            scratch(cin // 128, tile_rows + 3, 8 + tile_cols, 128),
+            scratch(cin // 128, tile_rows + 3, 16 + tile_cols, 128),
             scratch(3, cin // 128, 40, 128),
         ],
         region, cotangent, core_rows, far_rows, beside, edge,
@@ -621,7 +621,7 @@
         (shape((sizes.hr, sizes.hc, width)), shape(region.shape)),
         [
             scratch(4 * sizes.main, cin),
-            scratch(cin // 128, tile_rows, tile_cols, 128),
+            scratch(cin // 128, tile_rows, 8 + tile_cols, 128),
         ],
         grad_one, reduce_t, grad_sum, short_t, active_three,
         flops=2 * 4 * sizes.main * cin * mid,

time: 54.9 us -> 54.9 us (level)
  no operation moved by 1% of the time
where the time goes in v8:
time: 54.9 us; the launch traced here: 54.6 us
  waiting for transfers between devices  23.6 us (43%)
  starting transfers between devices  20.7 us (38%)
  Pallas kernels  8.39 us (15%)
  local copies, waits for them, and re-layouts  0.92 us (2%)
  between operations  0.76 us (1%)
    ppermute x7, waiting for transfers between devices, cross(): return lax.ppermute(x, ('row', 'col'), both(rows, cols, target))  15.6 us
    ppermute x7, starting transfers between devices, cross(): return lax.ppermute(x, ('row', 'col'), both(rows, cols, target))  13.6 us
    pallas_call x8, Pallas kernels, call(): pl.pallas_call(kernel, out_shape=out_shape, in_specs=[pl.BlockSpec(memory...  8.39 us
    ppermute x6, starting transfers between devices, swap_even(): lax.ppermute(x, axis, [(i, i ^ 1) for i in range(lax.axis_size(axis))])  4.62 us
    ppermute x6, waiting for transfers between devices, swap_even(): lax.ppermute(x, axis, [(i, i ^ 1) for i in range(lax.axis_size(axis))])  4.53 us
    ppermute x1, waiting for transfers between devices, reduce(): across = lax.ppermute(part, 'row', [(r, r ^ 2) for r in range(4)])  3.45 us
    ppermute x2, starting transfers between devices, swap_odd(): return lax.ppermute(x, axis, pairs)  1.44 us
  transfers between devices with their start and end apart: 16, of which 9 were waited for; matrix products, arithmetic and copies ran while one was open for 0% of the time, Pallas kernels for 2%

profile of v8, /device:TPU:0, one launch (start us, length us, event | category | flops | bytes accessed | tf_op | source)
XLA Modules:
  0.0 54.6 jit_solution(14433001002525928151)
XLA Ops:
  0.6 1.9 %shard_map.109 = (bf16[592,128]{1,0:T(8,128)(2,1)}, bf16[128,256]{1,0:T(8,128)(2,1)}, bf16[560,128]{1,0:T(8,128)(2,1)}) custom-call(bf16[16,32,256]{2,1,0:T(8,128)(2,1)} %region.1, bf16[8,16,512]{2,1,0:T(8,128)(2,1)} %cot.1, bf16[64,256]{1,0:T(8,128)(2,1)} %bitcast.31, bf16[64,144]{1,0:T(8,128)(2,1)} %bitcast.32, bf16[64,512]{1,0:T(8,128)(2,1)} %bitcast.30, ...), custom_call_target="tpu_custom_call" | custom-call | bytes 903168 | tf_op jit(solution)/shard_map/pallas_call | solution.py:427
  2.5 0.5 collective-permute-start
  3.0 0.7 %collective-permute-start.1 = (bf16[128,256]{1,0:T(8,128)(2,1)}, bf16[128,256]{1,0:T(8,128)(2,1)S(1)}, u32[]{:S(2)}, u32[]{:S(2)}) collective-permute-start(bf16[128,256]{1,0:T(8,128)(2,1)} %get-tuple-element.31), channel_id=1, source_target_pairs={{8,16},{16,8},{9,17},{17,9},{10,18},{18,10},{11,19},{19,11},{12,20... | collective-permute-start | bytes 196616 | tf_op jit(solution)/shard_map/ppermute | solution.py:477
  3.7 2.6 %collective-permute-start.4 = (bf16[592,128]{1,0:T(8,128)(2,1)}, bf16[592,128]{1,0:T(8,128)(2,1)S(1)}, u32[]{:S(2)}, u32[]{:S(2)}) collective-permute-start(bf16[592,128]{1,0:T(8,128)(2,1)} %get-tuple-element.37.own), channel_id=1, source_target_pairs={{0,2},{1,3},{2,4},{3,5},{4,6},{5,7},{6,0},{7,1},{8,11},{9,10},{10,... | collective-permute-start | bytes 454664 | tf_op jit(solution)/shard_map/ppermute | solution.py:491
  6.3 2.6 %collective-permute-start.5 = (bf16[592,128]{1,0:T(8,128)(2,1)}, bf16[592,128]{1,0:T(8,128)(2,1)S(1)}, u32[]{:S(2)}, u32[]{:S(2)}) collective-permute-start(bf16[592,128]{1,0:T(8,128)(2,1)} %get-tuple-element.37.own), channel_id=1, source_target_pairs={{0,4},{1,5},{2,6},{3,7},{4,0},{5,1},{6,2},{7,3},{8,13},{9,12},{10,... | collective-permute-start | bytes 454664 | tf_op jit(solution)/shard_map/ppermute | solution.py:491
  8.9 1.3 %collective-permute-start.6 = (bf16[592,128]{1,0:T(8,128)(2,1)}, bf16[592,128]{1,0:T(8,128)(2,1)S(1)}, u32[]{:S(2)}, u32[]{:S(2)}) collective-permute-start(bf16[592,128]{1,0:T(8,128)(2,1)} %get-tuple-element.37.own), channel_id=1, source_target_pairs={{0,6},{1,7},{2,0},{3,1},{4,2},{5,3},{6,4},{7,5},{8,15},{9,14},{10,... | collective-permute-start | bytes 454664 | tf_op jit(solution)/shard_map/ppermute | solution.py:491
  10.3 0.0 collective-permute-done.core_rows
  10.3 0.0 collective-permute-done.1.far_rows
  10.3 0.0 copy-start.2
  10.3 0.9 %copy-done.2 = bf16[560,128]{1,0:T(8,128)(2,1)S(1)} copy-done((bf16[560,128]{1,0:T(8,128)(2,1)S(1)}, bf16[560,128]{1,0:T(8,128)(2,1)}, u32[]{:S(2)}) %copy-start.2) | copy-done | bytes 143384
  11.2 1.6 %collective-permute-start.2 = (bf16[496,128]{1,0:T(8,128)(2,1)S(1)}, bf16[496,128]{1,0:T(8,128)(2,1)S(1)}, u32[]{:S(2)}, u32[]{:S(2)}) collective-permute-start(bf16[496,128]{1,0:T(8,128)(2,1)S(1)} %get-tuple-element.33), channel_id=1, source_target_pairs={{0,1},{1,0},{2,3},{3,2},{4,5},{5,4},{6,7},{7,6},{8,9},{9,8},{10,11... | collective-permute-start | bytes 380936 | tf_op jit(solution)/shard_map/ppermute | solution.py:481
  12.8 0.0 copy-start
  12.8 0.0 copy-start.1
  12.8 0.8 %collective-permute-start.3 = (bf16[192,128]{1,0:T(8,128)(2,1)S(1)}, bf16[192,128]{1,0:T(8,128)(2,1)S(1)}, u32[]{:S(2)}, u32[]{:S(2)}) collective-permute-start(bf16[192,128]{1,0:T(8,128)(2,1)S(1)} %get-tuple-element.34), channel_id=1, source_target_pairs={{1,2},{2,1},{3,4},{4,3},{5,6},{6,5},{9,10},{10,9},{11,12},{12,11},... | collective-permute-start | bytes 147464 | tf_op jit(solution)/shard_map/ppermute | solution.py:477
  13.6 0.0 collective-permute-done.3.edge
  13.6 0.0 collective-permute-done.4.refs_0_
  13.6 6.1 %collective-permute-done.5.refs_1_ = bf16[592,128]{1,0:T(8,128)(2,1)S(1)} collective-permute-done((bf16[592,128]{1,0:T(8,128)(2,1)}, bf16[592,128]{1,0:T(8,128)(2,1)S(1)}, u32[]{:S(2)}, u32[]{:S(2)}) %collective-permute-start.5) | collective-permute-done | bytes 151584 | tf_op jit(solution)/shard_map/ppermute | solution.py:491
  19.7 0.0 collective-permute-done.6.refs_2_
  19.7 0.0 collective-permute-done.2.beside
  19.8 0.0 copy-start.3
  19.8 2.0 %collective-permute-start.7 = (bf16[2080,128]{1,0:T(8,128)(2,1)S(1)}, bf16[2080,128]{1,0:T(8,128)(2,1)S(1)}, u32[]{:S(2)}, u32[]{:S(2)}) collective-permute-start(bf16[2080,128]{1,0:T(8,128)(2,1)S(1)} %shard_map.112.passed), channel_id=1, source_target_pairs={{0,8},{8,0},{16,24},{24,16},{1,9},{9,1},{17,25},{25,17},{2,10},{10... | collective-permute-start | bytes 1597448 | tf_op jit(solution)/shard_map/ppermute | solution.py:481
  21.8 0.0 copy-done
  21.8 0.0 copy-done.1
  21.8 0.2 shard_map.111
  22.0 1.3 %collective-permute-done.7.swapped = bf16[2080,128]{1,0:T(8,128)(2,1)S(1)} collective-permute-done((bf16[2080,128]{1,0:T(8,128)(2,1)S(1)}, bf16[2080,128]{1,0:T(8,128)(2,1)S(1)}, u32[]{:S(2)}, u32[]{:S(2)}) %collective-permute-start.7) | collective-permute-done | bytes 532512 | tf_op jit(solution)/shard_map/ppermute | solution.py:481
  23.3 0.0 copy-done.3
  23.3 4.3 %shard_map.113 = (bf16[128,512]{1,0:T(8,128)(2,1)S(1)}, bf16[128,512]{1,0:T(8,128)(2,1)S(1)}, bf16[512,256]{1,0:T(8,128)(2,1)S(1)}, bf16[512,256]{1,0:T(8,128)(2...) custom-call(bf16[1056,256]{1,0:T(8,128)(2,1)S(1)} %get-tuple-element, ...), custom_call_target="tpu_custom_call" | custom-call | flops 2164260864 | bytes 5050368 | tf_op jit(solution)/shard_map/pallas_call | solution.py:427
  27.7 0.4 collective-permute-start.8
  28.1 1.7 %collective-permute-done.8 = bf16[4,592,128]{2,1,0:T(8,128)(2,1)S(1)} collective-permute-done((bf16[4,592,128]{2,1,0:T(8,128)(2,1)S(1)}, bf16[4,592,128]{2,1,0:T(8,128)(2,1)S(1)}, u32[]{:S(2)}, u32[]{:S(2)}) %collective-permute-start.8) | collective-permute-done | bytes 606240 | tf_op jit(solution)/shard_map/ppermute | solution.py:481
  29.8 0.1 fusion.3
  29.9 4.4 %collective-permute-start.10 = (bf16[592,128]{1,0:T(8,128)(2,1)S(1)}, bf16[592,128]{1,0:T(8,128)(2,1)S(1)}, u32[]{:S(2)}, u32[]{:S(2)}) collective-permute-start(bf16[592,128]{1,0:T(8,128)(2,1)S(1)} %get-tuple-element.59), channel_id=1, source_target_pairs={{0,4},{1,5},{2,6},{3,7},{4,0},{5,1},{6,2},{7,3},{8,13},{9,12},{10,... | collective-permute-start | bytes 454664 | tf_op jit(solution)/shard_map/ppermute | solution.py:491
  34.3 1.1 %collective-permute-start.11 = (bf16[592,128]{1,0:T(8,128)(2,1)S(1)}, bf16[592,128]{1,0:T(8,128)(2,1)S(1)}, u32[]{:S(2)}, u32[]{:S(2)}) collective-permute-start(bf16[592,128]{1,0:T(8,128)(2,1)S(1)} %get-tuple-element.58), channel_id=1, source_target_pairs={{0,6},{1,7},{2,0},{3,1},{4,2},{5,3},{6,4},{7,5},{8,15},{9,14},{10,... | collective-permute-start | bytes 454664 | tf_op jit(solution)/shard_map/ppermute | solution.py:491
  35.3 1.0 %collective-permute-start.12 = (bf16[592,128]{1,0:T(8,128)(2,1)S(1)}, bf16[592,128]{1,0:T(8,128)(2,1)S(1)}, u32[]{:S(2)}, u32[]{:S(2)}) collective-permute-start(bf16[592,128]{1,0:T(8,128)(2,1)S(1)} %get-tuple-element.57), channel_id=1, source_target_pairs={{0,2},{1,3},{2,4},{3,5},{4,6},{5,7},{6,0},{7,1},{8,11},{9,10},{10,... | collective-permute-start | bytes 454664 | tf_op jit(solution)/shard_map/ppermute | solution.py:491
  36.3 0.7 %collective-permute-start.9 = (bf16[592,128]{1,0:T(8,128)(2,1)S(1)}, bf16[592,128]{1,0:T(8,128)(2,1)S(1)}, u32[]{:S(2)}, u32[]{:S(2)}) collective-permute-start(bf16[592,128]{1,0:T(8,128)(2,1)S(1)} %get-tuple-element.56), channel_id=1, source_target_pairs={{8,9},{9,8},{10,11},{11,10},{12,13},{13,12},{14,15},{15,14},{24,25... | collective-permute-start | bytes 454664 | tf_op jit(solution)/shard_map/ppermute | solution.py:491
  37.0 5.4 %collective-permute-done.10 = bf16[592,128]{1,0:T(8,128)(2,1)S(1)} collective-permute-done((bf16[592,128]{1,0:T(8,128)(2,1)S(1)}, bf16[592,128]{1,0:T(8,128)(2,1)S(1)}, u32[]{:S(2)}, u32[]{:S(2)}) %collective-permute-start.10) | collective-permute-done | bytes 151584 | tf_op jit(solution)/shard_map/ppermute | solution.py:491
  42.4 0.5 collective-permute-done.11
  42.8 3.6 %collective-permute-done.12 = bf16[592,128]{1,0:T(8,128)(2,1)S(1)} collective-permute-done((bf16[592,128]{1,0:T(8,128)(2,1)S(1)}, bf16[592,128]{1,0:T(8,128)(2,1)S(1)}, u32[]{:S(2)}, u32[]{:S(2)}) %collective-permute-start.12) | collective-permute-done | bytes 151584 | tf_op jit(solution)/shard_map/ppermute | solution.py:491
  46.5 0.0 collective-permute-done.9
  46.5 0.1 add_convert_fusion.one
  46.6 0.1 collective-permute-start.13
  46.7 1.4 %collective-permute-done.13.other = bf16[592,128]{1,0:T(8,128)(2,1)S(1)} collective-permute-done((bf16[592,128]{1,0:T(8,128)(2,1)S(1)}, bf16[592,128]{1,0:T(8,128)(2,1)S(1)}, u32[]{:S(2)}, u32[]{:S(2)}) %collective-permute-start.13) | collective-permute-done | bytes 151584 | tf_op jit(solution)/shard_map/ppermute | solution.py:481
  48.0 0.1 shard_map.115
  48.1 1.0 %collective-permute-start.14 = (bf16[304,128]{1,0:T(8,128)(2,1)S(1)}, bf16[304,128]{1,0:T(8,128)(2,1)S(1)}, u32[]{:S(2)}, u32[]{:S(2)}) collective-permute-start(bf16[304,128]{1,0:T(8,128)(2,1)S(1)} %get-tuple-element.51), channel_id=1, source_target_pairs={{0,16},{8,24},{16,0},{24,8},{1,17},{9,25},{17,1},{25,9},{2,18},{10... | collective-permute-start | bytes 233480 | tf_op jit(solution)/shard_map/ppermute | solution.py:516
  49.1 3.4 %collective-permute-done.14.mine = bf16[304,128]{1,0:T(8,128)(2,1)S(1)} collective-permute-done((bf16[304,128]{1,0:T(8,128)(2,1)S(1)}, bf16[304,128]{1,0:T(8,128)(2,1)S(1)}, u32[]{:S(2)}, u32[]{:S(2)}) %collective-permute-start.14) | collective-permute-done | bytes 77856 | tf_op jit(solution)/shard_map/ppermute | solution.py:516
  52.6 0.0 collective-permute-start.15
  52.6 1.1 %shard_map.114 = (bf16[8,16,512]{2,1,0:T(8,128)(2,1)}, bf16[16,32,256]{2,1,0:T(8,128)(2,1)}) custom-call(bf16[512,512]{1,0:T(8,128)(2,1)S(1)} %get-tuple-element.38.grad_one, bf16[512,256]{1,0:T(8,128)(2,1)S(1)} %get-tuple-element.39.reduce_t, bf16[128,512]{1,0:T(8,128)(2,1)S(1)} %get-tuple-element.40.grad_sum, ...), custom_call_target="tpu_custom_call" | custom-call | flops 134217728 | bytes 1703936 | tf_op jit(solution)/shard_map/pallas_call | solution.py:427
  53.7 0.2 collective-permute-done.15.theirs
  53.9 0.8 %shard_map.116 = (f32[64,256]{1,0:T(8,128)}, f32[64,144]{1,0:T(8,128)}, f32[64,512]{1,0:T(8,128)}, f32[64,256]{1,0:T(8,128)}) custom-call(bf16[592,128]{1,0:T(8,128)(2,1)S(1)} %get-tuple-element.50.whole, bf16[304,128]{1,0:T(8,128)(2,1)S(1)} %collective-permute-done.14.mine, bf16[304,128]{1,0:T(8,128)(2,1)S(1)} %collective-permute-done.15.theirs), custom_call_target="tpu_custom_call" | custom-call | bytes 606208 | tf_op jit(solution)/shard_map/pallas_call | solution.py:427
  (2 shorter events, 0.1 us)
Async XLA Ops:
  2.5 7.8 %collective-permute-start = (bf16[128,256]{1,0:T(8,128)(2,1)}, bf16[128,256]{1,0:T(8,128)(2,1)S(1)}, u32[]{:S(2)}, u32[]{:S(2)}) collective-permute-start(bf16[128,256]{1,0:T(8,128)(2,1)} %get-tuple-element.31), channel_id=1, source_target_pairs={{0,8},{8,0},{16,24},{24,16},{1,9},{9,1},{17,25},{25,17},{2,10},{10... | collective-permute-start | bytes 196616 | tf_op jit(solution)/shard_map/ppermute | solution.py:481
  3.0 7.3 %collective-permute-start.1 = (bf16[128,256]{1,0:T(8,128)(2,1)}, bf16[128,256]{1,0:T(8,128)(2,1)S(1)}, u32[]{:S(2)}, u32[]{:S(2)}) collective-permute-start(bf16[128,256]{1,0:T(8,128)(2,1)} %get-tuple-element.31), channel_id=1, source_target_pairs={{8,16},{16,8},{9,17},{17,9},{10,18},{18,10},{11,19},{19,11},{12,20... | collective-permute-start | bytes 196616 | tf_op jit(solution)/shard_map/ppermute | solution.py:477
  3.7 9.9 %collective-permute-start.4 = (bf16[592,128]{1,0:T(8,128)(2,1)}, bf16[592,128]{1,0:T(8,128)(2,1)S(1)}, u32[]{:S(2)}, u32[]{:S(2)}) collective-permute-start(bf16[592,128]{1,0:T(8,128)(2,1)} %get-tuple-element.37.own), channel_id=1, source_target_pairs={{0,2},{1,3},{2,4},{3,5},{4,6},{5,7},{6,0},{7,1},{8,11},{9,10},{10,... | collective-permute-start | bytes 454664 | tf_op jit(solution)/shard_map/ppermute | solution.py:491
  6.3 13.4 %collective-permute-start.5 = (bf16[592,128]{1,0:T(8,128)(2,1)}, bf16[592,128]{1,0:T(8,128)(2,1)S(1)}, u32[]{:S(2)}, u32[]{:S(2)}) collective-permute-start(bf16[592,128]{1,0:T(8,128)(2,1)} %get-tuple-element.37.own), channel_id=1, source_target_pairs={{0,4},{1,5},{2,6},{3,7},{4,0},{5,1},{6,2},{7,3},{8,13},{9,12},{10,... | collective-permute-start | bytes 454664 | tf_op jit(solution)/shard_map/ppermute | solution.py:491
  8.9 10.8 %collective-permute-start.6 = (bf16[592,128]{1,0:T(8,128)(2,1)}, bf16[592,128]{1,0:T(8,128)(2,1)S(1)}, u32[]{:S(2)}, u32[]{:S(2)}) collective-permute-start(bf16[592,128]{1,0:T(8,128)(2,1)} %get-tuple-element.37.own), channel_id=1, source_target_pairs={{0,6},{1,7},{2,0},{3,1},{4,2},{5,3},{6,4},{7,5},{8,15},{9,14},{10,... | collective-permute-start | bytes 454664 | tf_op jit(solution)/shard_map/ppermute | solution.py:491
  10.3 0.9 %copy-start.2 = (bf16[560,128]{1,0:T(8,128)(2,1)S(1)}, bf16[560,128]{1,0:T(8,128)(2,1)}, u32[]{:S(2)}) copy-start(bf16[560,128]{1,0:T(8,128)(2,1)} %get-tuple-element.32.draft) | copy-start | bytes 430084
  11.2 8.5 %collective-permute-start.2 = (bf16[496,128]{1,0:T(8,128)(2,1)S(1)}, bf16[496,128]{1,0:T(8,128)(2,1)S(1)}, u32[]{:S(2)}, u32[]{:S(2)}) collective-permute-start(bf16[496,128]{1,0:T(8,128)(2,1)S(1)} %get-tuple-element.33), channel_id=1, source_target_pairs={{0,1},{1,0},{2,3},{3,2},{4,5},{5,4},{6,7},{7,6},{8,9},{9,8},{10,11... | collective-permute-start | bytes 380936 | tf_op jit(solution)/shard_map/ppermute | solution.py:481
  12.8 9.0 %copy-start = (bf16[16,32,256]{2,1,0:T(8,128)(2,1)S(1)}, bf16[16,32,256]{2,1,0:T(8,128)(2,1)}, u32[]{:S(2)}) copy-start(bf16[16,32,256]{2,1,0:T(8,128)(2,1)} %region.1) | copy-start | bytes 786436
  12.8 9.0 %copy-start.1 = (bf16[8,16,512]{2,1,0:T(8,128)(2,1)S(1)}, bf16[8,16,512]{2,1,0:T(8,128)(2,1)}, u32[]{:S(2)}) copy-start(bf16[8,16,512]{2,1,0:T(8,128)(2,1)} %cot.1) | copy-start | bytes 393220
  12.8 0.8 %collective-permute-start.3 = (bf16[192,128]{1,0:T(8,128)(2,1)S(1)}, bf16[192,128]{1,0:T(8,128)(2,1)S(1)}, u32[]{:S(2)}, u32[]{:S(2)}) collective-permute-start(bf16[192,128]{1,0:T(8,128)(2,1)S(1)} %get-tuple-element.34), channel_id=1, source_target_pairs={{1,2},{2,1},{3,4},{4,3},{5,6},{6,5},{9,10},{10,9},{11,12},{12,11},... | collective-permute-start | bytes 147464 | tf_op jit(solution)/shard_map/ppermute | solution.py:477
  19.8 3.6 %copy-start.3 = (bf16[592,128]{1,0:T(8,128)(2,1)S(1)}, bf16[592,128]{1,0:T(8,128)(2,1)}, u32[]{:S(2)}) copy-start(bf16[592,128]{1,0:T(8,128)(2,1)} %get-tuple-element.37.own) | copy-start | bytes 454660
  19.8 3.6 %collective-permute-start.7 = (bf16[2080,128]{1,0:T(8,128)(2,1)S(1)}, bf16[2080,128]{1,0:T(8,128)(2,1)S(1)}, u32[]{:S(2)}, u32[]{:S(2)}) collective-permute-start(bf16[2080,128]{1,0:T(8,128)(2,1)S(1)} %shard_map.112.passed), channel_id=1, source_target_pairs={{0,8},{8,0},{16,24},{24,16},{1,9},{9,1},{17,25},{25,17},{2,10},{10... | collective-permute-start | bytes 1597448 | tf_op jit(solution)/shard_map/ppermute | solution.py:481
  27.7 2.1 %collective-permute-start.8 = (bf16[4,592,128]{2,1,0:T(8,128)(2,1)S(1)}, bf16[4,592,128]{2,1,0:T(8,128)(2,1)S(1)}, u32[]{:S(2)}, u32[]{:S(2)}) collective-permute-start(bf16[4,592,128]{2,1,0:T(8,128)(2,1)S(1)} %get-tuple-element.46), channel_id=1, source_target_pairs={{0,8},{8,0},{16,24},{24,16},{1,9},{9,1},{17,25},{25,17},{2,10},{10... | collective-permute-start | bytes 1818632 | tf_op jit(solution)/shard_map/ppermute | solution.py:481
  29.9 12.5 %collective-permute-start.10 = (bf16[592,128]{1,0:T(8,128)(2,1)S(1)}, bf16[592,128]{1,0:T(8,128)(2,1)S(1)}, u32[]{:S(2)}, u32[]{:S(2)}) collective-permute-start(bf16[592,128]{1,0:T(8,128)(2,1)S(1)} %get-tuple-element.59), channel_id=1, source_target_pairs={{0,4},{1,5},{2,6},{3,7},{4,0},{5,1},{6,2},{7,3},{8,13},{9,12},{10,... | collective-permute-start | bytes 454664 | tf_op jit(solution)/shard_map/ppermute | solution.py:491
  34.3 8.6 %collective-permute-start.11 = (bf16[592,128]{1,0:T(8,128)(2,1)S(1)}, bf16[592,128]{1,0:T(8,128)(2,1)S(1)}, u32[]{:S(2)}, u32[]{:S(2)}) collective-permute-start(bf16[592,128]{1,0:T(8,128)(2,1)S(1)} %get-tuple-element.58), channel_id=1, source_target_pairs={{0,6},{1,7},{2,0},{3,1},{4,2},{5,3},{6,4},{7,5},{8,15},{9,14},{10,... | collective-permute-start | bytes 454664 | tf_op jit(solution)/shard_map/ppermute | solution.py:491
  35.3 11.1 %collective-permute-start.12 = (bf16[592,128]{1,0:T(8,128)(2,1)S(1)}, bf16[592,128]{1,0:T(8,128)(2,1)S(1)}, u32[]{:S(2)}, u32[]{:S(2)}) collective-permute-start(bf16[592,128]{1,0:T(8,128)(2,1)S(1)} %get-tuple-element.57), channel_id=1, source_target_pairs={{0,2},{1,3},{2,4},{3,5},{4,6},{5,7},{6,0},{7,1},{8,11},{9,10},{10,... | collective-permute-start | bytes 454664 | tf_op jit(solution)/shard_map/ppermute | solution.py:491
  36.3 10.2 %collective-permute-start.9 = (bf16[592,128]{1,0:T(8,128)(2,1)S(1)}, bf16[592,128]{1,0:T(8,128)(2,1)S(1)}, u32[]{:S(2)}, u32[]{:S(2)}) collective-permute-start(bf16[592,128]{1,0:T(8,128)(2,1)S(1)} %get-tuple-element.56), channel_id=1, source_target_pairs={{8,9},{9,8},{10,11},{11,10},{12,13},{13,12},{14,15},{15,14},{24,25... | collective-permute-start | bytes 454664 | tf_op jit(solution)/shard_map/ppermute | solution.py:491
  46.6 1.4 %collective-permute-start.13 = (bf16[592,128]{1,0:T(8,128)(2,1)S(1)}, bf16[592,128]{1,0:T(8,128)(2,1)S(1)}, u32[]{:S(2)}, u32[]{:S(2)}) collective-permute-start(bf16[592,128]{1,0:T(8,128)(2,1)S(1)} %add_convert_fusion.one), channel_id=1, source_target_pairs={{0,8},{8,0},{16,24},{24,16},{1,9},{9,1},{17,25},{25,17},{2,10},{10... | collective-permute-start | bytes 454664 | tf_op jit(solution)/shard_map/ppermute | solution.py:481
  48.1 4.5 %collective-permute-start.14 = (bf16[304,128]{1,0:T(8,128)(2,1)S(1)}, bf16[304,128]{1,0:T(8,128)(2,1)S(1)}, u32[]{:S(2)}, u32[]{:S(2)}) collective-permute-start(bf16[304,128]{1,0:T(8,128)(2,1)S(1)} %get-tuple-element.51), channel_id=1, source_target_pairs={{0,16},{8,24},{16,0},{24,8},{1,17},{9,25},{17,1},{25,9},{2,18},{10... | collective-permute-start | bytes 233480 | tf_op jit(solution)/shard_map/ppermute | solution.py:516
  52.6 1.3 %collective-permute-start.15 = (bf16[304,128]{1,0:T(8,128)(2,1)S(1)}, bf16[304,128]{1,0:T(8,128)(2,1)S(1)}, u32[]{:S(2)}, u32[]{:S(2)}) collective-permute-start(bf16[304,128]{1,0:T(8,128)(2,1)S(1)} %collective-permute-done.14.mine), channel_id=1, source_target_pairs={{0,8},{8,0},{16,24},{24,16},{1,9},{9,1},{17,25},{25,17},{2,10},{10... | collective-permute-start | bytes 233480 | tf_op jit(solution)/shard_map/ppermute | solution.py:481

commit v9 on v8

--- a/solution.py
+++ b/solution.py
@@ -90,14 +90,14 @@
 
 
 def send_kernel(sizes, *refs):
-    given, (weights, outer, draft, cols) = refs[:6], refs[6:10]
-    local, arrived = refs[10:16], refs[16]
+    given, (sent, outer, draft, cols) = refs[:6], refs[6:10]
+    local, arrived, weights, gone = refs[10:16], refs[16], refs[17], refs[18]
     copies = [
         pltpu.make_async_copy(given[i], local[i], arrived.at[i]) for i in range(len(given))
     ]
-    for copy in copies:
+    for copy in copies[2:] + copies[:2]:
         copy.start()
-    for copy in copies:
+    for copy in copies[2:]:
         copy.wait()
     region, cot, reduce_t, group_t, expand_t, short_t = local
     shard, taps = group_t.shape
@@ -111,6 +111,10 @@
     pad = jnp.zeros((shard, 256 - taps), BF16)
     rest = jnp.concatenate([group_t[...], pad], axis=1)[:, 128:].astype(F32)
     weights[len(tiles) * shard :] = fold(rest).astype(BF16)
+    leave = pltpu.make_async_copy(weights, sent, gone)
+    leave.start()
+    for copy in copies[:2]:
+        copy.wait()
     tc, half = sizes.tc, cot.shape[2] // 2
     for i, r in enumerate((sizes.tr - 1, 0, 1)):
         outer[i * tc : (i + 1) * tc] = region[r]
@@ -126,6 +130,7 @@
     first = pl.multiple_of(core * (weights.shape[0] - share), 16)
     draft[:share] = weights[pl.ds(first, share), :]
     draft[share:] = cols[...].astype(BF16)
+    leave.wait()
 
 
 def put_columns(cols, row, head, tail):
@@ -421,14 +426,17 @@
         region_grad[:, :, v * 128 : (v + 1) * 128] = spread_out[v, :, : sizes.tc].astype(BF16)
 
 
-def call(kernel, out_shape, scratch, *operands, flops=0, space=pltpu.VMEM, limit=VMEM_LIMIT):
-    sizes = sum(o.size * o.dtype.itemsize for o in operands)
-    sizes += sum(o.size * o.dtype.itemsize for o in jax.tree.leaves(out_shape))
+def call(kernel, out_shape, scratch, *operands, flops=0, space=pltpu.VMEM, limit=VMEM_LIMIT, first=pltpu.VMEM):
+    leaves = jax.tree.leaves(out_shape)
+    sizes = sum(o.size * o.dtype.itemsize for o in [*operands, *leaves])
     return pl.pallas_call(
         kernel,
         out_shape=out_shape,
         in_specs=[pl.BlockSpec(memory_space=space)] * len(operands),
-        out_specs=jax.tree.map(lambda _: pl.BlockSpec(memory_space=pltpu.VMEM), out_shape),
+        out_specs=jax.tree.map(
+            lambda shape: pl.BlockSpec(memory_space=first if shape is leaves[0] else pltpu.VMEM),
+            out_shape,
+        ),
         scratch_shapes=scratch,
         compiler_params=pltpu.CompilerParams(vmem_limit_bytes=limit),
         cost_estimate=pl.CostEstimate(flops=flops, bytes_accessed=sizes, transcendentals=0),
@@ -548,10 +556,15 @@
         ),
         [scratch(halo, 128)]
         + [scratch(*given.shape, dtype=BF16) for given in inputs]
-        + [pltpu.SemaphoreType.DMA((len(inputs),))],
+        + [
+            pltpu.SemaphoreType.DMA((len(inputs),)),
+            scratch(length, 128, dtype=BF16),
+            pltpu.SemaphoreType.DMA,
+        ],
         *inputs,
         space=pltpu.HBM,
         limit=62 * 1024 * 1024,
+        first=pltpu.HBM,
     )
     far = [cross(weights, j) for j in range(1, halves)]
     core_rows = swap_even(outer, "row")

time: 54.9 us -> 55.4 us (level)
  no operation moved by 1% of the time
where the time goes in v9:
time: 55.4 us; the launch traced here: 55.1 us
  waiting for transfers between devices  23.6 us (43%)
  starting transfers between devices  20.7 us (37%)
  Pallas kernels  8.88 us (16%)
  local copies, waits for them, and re-layouts  0.92 us (2%)
  between operations  0.76 us (1%)
    ppermute x7, waiting for transfers between devices, cross(): return lax.ppermute(x, ('row', 'col'), both(rows, cols, target))  15.6 us
    ppermute x7, starting transfers between devices, cross(): return lax.ppermute(x, ('row', 'col'), both(rows, cols, target))  13.6 us
    pallas_call x8, Pallas kernels, call(): pl.pallas_call(kernel, out_shape=out_shape, in_specs=[pl.BlockSpec(memory...  8.88 us
    ppermute x6, starting transfers between devices, swap_even(): lax.ppermute(x, axis, [(i, i ^ 1) for i in range(lax.axis_size(axis))])  4.62 us
    ppermute x6, waiting for transfers between devices, swap_even(): lax.ppermute(x, axis, [(i, i ^ 1) for i in range(lax.axis_size(axis))])  4.54 us
    ppermute x1, waiting for transfers between devices, reduce(): across = lax.ppermute(part, 'row', [(r, r ^ 2) for r in range(4)])  3.44 us
    ppermute x2, starting transfers between devices, swap_odd(): return lax.ppermute(x, axis, pairs)  1.44 us
  transfers between devices with their start and end apart: 16, of which 9 were waited for; matrix products, arithmetic and copies ran while one was open for 0% of the time, Pallas kernels for 2%

profile of v9, /device:TPU:0, one launch (start us, length us, event | category | flops | bytes accessed | tf_op | source)
XLA Modules:
  0.0 55.1 jit_solution(1953677574290277737)
XLA Ops:
  0.6 2.4 %shard_map.109 = (bf16[592,128]{1,0:T(8,128)(2,1)}, bf16[128,256]{1,0:T(8,128)(2,1)}, bf16[560,128]{1,0:T(8,128)(2,1)}) custom-call(bf16[16,32,256]{2,1,0:T(8,128)(2,1)} %region.1, bf16[8,16,512]{2,1,0:T(8,128)(2,1)} %cot.1, bf16[64,256]{1,0:T(8,128)(2,1)} %bitcast.31, bf16[64,144]{1,0:T(8,128)(2,1)} %bitcast.32, bf16[64,512]{1,0:T(8,128)(2,1)} %bitcast.30, ...), custom_call_target="tpu_custom_call" | custom-call | bytes 903168 | tf_op jit(solution)/shard_map/pallas_call | solution.py:432
  3.0 0.5 collective-permute-start
  3.5 0.7 %collective-permute-start.1 = (bf16[128,256]{1,0:T(8,128)(2,1)}, bf16[128,256]{1,0:T(8,128)(2,1)S(1)}, u32[]{:S(2)}, u32[]{:S(2)}) collective-permute-start(bf16[128,256]{1,0:T(8,128)(2,1)} %get-tuple-element.31), channel_id=1, source_target_pairs={{8,16},{16,8},{9,17},{17,9},{10,18},{18,10},{11,19},{19,11},{12,20... | collective-permute-start | bytes 196616 | tf_op jit(solution)/shard_map/ppermute | solution.py:485
  4.2 2.6 %collective-permute-start.4 = (bf16[592,128]{1,0:T(8,128)(2,1)}, bf16[592,128]{1,0:T(8,128)(2,1)S(1)}, u32[]{:S(2)}, u32[]{:S(2)}) collective-permute-start(bf16[592,128]{1,0:T(8,128)(2,1)} %get-tuple-element.37.own), channel_id=1, source_target_pairs={{0,2},{1,3},{2,4},{3,5},{4,6},{5,7},{6,0},{7,1},{8,11},{9,10},{10,... | collective-permute-start | bytes 454664 | tf_op jit(solution)/shard_map/ppermute | solution.py:499
  6.8 2.6 %collective-permute-start.5 = (bf16[592,128]{1,0:T(8,128)(2,1)}, bf16[592,128]{1,0:T(8,128)(2,1)S(1)}, u32[]{:S(2)}, u32[]{:S(2)}) collective-permute-start(bf16[592,128]{1,0:T(8,128)(2,1)} %get-tuple-element.37.own), channel_id=1, source_target_pairs={{0,4},{1,5},{2,6},{3,7},{4,0},{5,1},{6,2},{7,3},{8,13},{9,12},{10,... | collective-permute-start | bytes 454664 | tf_op jit(solution)/shard_map/ppermute | solution.py:499
  9.4 1.3 %collective-permute-start.6 = (bf16[592,128]{1,0:T(8,128)(2,1)}, bf16[592,128]{1,0:T(8,128)(2,1)S(1)}, u32[]{:S(2)}, u32[]{:S(2)}) collective-permute-start(bf16[592,128]{1,0:T(8,128)(2,1)} %get-tuple-element.37.own), channel_id=1, source_target_pairs={{0,6},{1,7},{2,0},{3,1},{4,2},{5,3},{6,4},{7,5},{8,15},{9,14},{10,... | collective-permute-start | bytes 454664 | tf_op jit(solution)/shard_map/ppermute | solution.py:499
  10.8 0.0 collective-permute-done.core_rows
  10.8 0.0 collective-permute-done.1.far_rows
  10.8 0.0 copy-start.2
  10.8 0.9 %copy-done.2 = bf16[560,128]{1,0:T(8,128)(2,1)S(1)} copy-done((bf16[560,128]{1,0:T(8,128)(2,1)S(1)}, bf16[560,128]{1,0:T(8,128)(2,1)}, u32[]{:S(2)}) %copy-start.2) | copy-done | bytes 143384
  11.7 1.6 %collective-permute-start.2 = (bf16[496,128]{1,0:T(8,128)(2,1)S(1)}, bf16[496,128]{1,0:T(8,128)(2,1)S(1)}, u32[]{:S(2)}, u32[]{:S(2)}) collective-permute-start(bf16[496,128]{1,0:T(8,128)(2,1)S(1)} %get-tuple-element.33), channel_id=1, source_target_pairs={{0,1},{1,0},{2,3},{3,2},{4,5},{5,4},{6,7},{7,6},{8,9},{9,8},{10,11... | collective-permute-start | bytes 380936 | tf_op jit(solution)/shard_map/ppermute | solution.py:489
  13.3 0.0 copy-start
  13.3 0.0 copy-start.1
  13.3 0.8 %collective-permute-start.3 = (bf16[192,128]{1,0:T(8,128)(2,1)S(1)}, bf16[192,128]{1,0:T(8,128)(2,1)S(1)}, u32[]{:S(2)}, u32[]{:S(2)}) collective-permute-start(bf16[192,128]{1,0:T(8,128)(2,1)S(1)} %get-tuple-element.34), channel_id=1, source_target_pairs={{1,2},{2,1},{3,4},{4,3},{5,6},{6,5},{9,10},{10,9},{11,12},{12,11},... | collective-permute-start | bytes 147464 | tf_op jit(solution)/shard_map/ppermute | solution.py:485
  14.1 0.0 collective-permute-done.3.edge
  14.1 0.0 collective-permute-done.4.refs_0_
  14.1 6.1 %collective-permute-done.5.refs_1_ = bf16[592,128]{1,0:T(8,128)(2,1)S(1)} collective-permute-done((bf16[592,128]{1,0:T(8,128)(2,1)}, bf16[592,128]{1,0:T(8,128)(2,1)S(1)}, u32[]{:S(2)}, u32[]{:S(2)}) %collective-permute-start.5) | collective-permute-done | bytes 151584 | tf_op jit(solution)/shard_map/ppermute | solution.py:499
  20.2 0.0 collective-permute-done.6.refs_2_
  20.2 0.0 collective-permute-done.2.beside
  20.3 0.0 copy-start.3
  20.3 2.0 %collective-permute-start.7 = (bf16[2080,128]{1,0:T(8,128)(2,1)S(1)}, bf16[2080,128]{1,0:T(8,128)(2,1)S(1)}, u32[]{:S(2)}, u32[]{:S(2)}) collective-permute-start(bf16[2080,128]{1,0:T(8,128)(2,1)S(1)} %shard_map.112.passed), channel_id=1, source_target_pairs={{0,8},{8,0},{16,24},{24,16},{1,9},{9,1},{17,25},{25,17},{2,10},{10... | collective-permute-start | bytes 1597448 | tf_op jit(solution)/shard_map/ppermute | solution.py:489
  22.3 0.0 copy-done
  22.3 0.0 copy-done.1
  22.3 0.2 shard_map.111
  22.5 1.3 %collective-permute-done.7.swapped = bf16[2080,128]{1,0:T(8,128)(2,1)S(1)} collective-permute-done((bf16[2080,128]{1,0:T(8,128)(2,1)S(1)}, bf16[2080,128]{1,0:T(8,128)(2,1)S(1)}, u32[]{:S(2)}, u32[]{:S(2)}) %collective-permute-start.7) | collective-permute-done | bytes 532512 | tf_op jit(solution)/shard_map/ppermute | solution.py:489
  23.8 0.0 copy-done.3
  23.8 4.3 %shard_map.113 = (bf16[128,512]{1,0:T(8,128)(2,1)S(1)}, bf16[128,512]{1,0:T(8,128)(2,1)S(1)}, bf16[512,256]{1,0:T(8,128)(2,1)S(1)}, bf16[512,256]{1,0:T(8,128)(2...) custom-call(bf16[1056,256]{1,0:T(8,128)(2,1)S(1)} %get-tuple-element, ...), custom_call_target="tpu_custom_call" | custom-call | flops 2164260864 | bytes 5050368 | tf_op jit(solution)/shard_map/pallas_call | solution.py:432
  28.2 0.4 collective-permute-start.8
  28.6 1.7 %collective-permute-done.8 = bf16[4,592,128]{2,1,0:T(8,128)(2,1)S(1)} collective-permute-done((bf16[4,592,128]{2,1,0:T(8,128)(2,1)S(1)}, bf16[4,592,128]{2,1,0:T(8,128)(2,1)S(1)}, u32[]{:S(2)}, u32[]{:S(2)}) %collective-permute-start.8) | collective-permute-done | bytes 606240 | tf_op jit(solution)/shard_map/ppermute | solution.py:489
  30.2 0.1 fusion.3
  30.4 4.4 %collective-permute-start.10 = (bf16[592,128]{1,0:T(8,128)(2,1)S(1)}, bf16[592,128]{1,0:T(8,128)(2,1)S(1)}, u32[]{:S(2)}, u32[]{:S(2)}) collective-permute-start(bf16[592,128]{1,0:T(8,128)(2,1)S(1)} %get-tuple-element.59), channel_id=1, source_target_pairs={{0,4},{1,5},{2,6},{3,7},{4,0},{5,1},{6,2},{7,3},{8,13},{9,12},{10,... | collective-permute-start | bytes 454664 | tf_op jit(solution)/shard_map/ppermute | solution.py:499
  34.8 1.1 %collective-permute-start.11 = (bf16[592,128]{1,0:T(8,128)(2,1)S(1)}, bf16[592,128]{1,0:T(8,128)(2,1)S(1)}, u32[]{:S(2)}, u32[]{:S(2)}) collective-permute-start(bf16[592,128]{1,0:T(8,128)(2,1)S(1)} %get-tuple-element.58), channel_id=1, source_target_pairs={{0,6},{1,7},{2,0},{3,1},{4,2},{5,3},{6,4},{7,5},{8,15},{9,14},{10,... | collective-permute-start | bytes 454664 | tf_op jit(solution)/shard_map/ppermute | solution.py:499
  35.8 1.0 %collective-permute-start.12 = (bf16[592,128]{1,0:T(8,128)(2,1)S(1)}, bf16[592,128]{1,0:T(8,128)(2,1)S(1)}, u32[]{:S(2)}, u32[]{:S(2)}) collective-permute-start(bf16[592,128]{1,0:T(8,128)(2,1)S(1)} %get-tuple-element.57), channel_id=1, source_target_pairs={{0,2},{1,3},{2,4},{3,5},{4,6},{5,7},{6,0},{7,1},{8,11},{9,10},{10,... | collective-permute-start | bytes 454664 | tf_op jit(solution)/shard_map/ppermute | solution.py:499
  36.8 0.7 %collective-permute-start.9 = (bf16[592,128]{1,0:T(8,128)(2,1)S(1)}, bf16[592,128]{1,0:T(8,128)(2,1)S(1)}, u32[]{:S(2)}, u32[]{:S(2)}) collective-permute-start(bf16[592,128]{1,0:T(8,128)(2,1)S(1)} %get-tuple-element.56), channel_id=1, source_target_pairs={{8,9},{9,8},{10,11},{11,10},{12,13},{13,12},{14,15},{15,14},{24,25... | collective-permute-start | bytes 454664 | tf_op jit(solution)/shard_map/ppermute | solution.py:499
  37.5 5.4 %collective-permute-done.10 = bf16[592,128]{1,0:T(8,128)(2,1)S(1)} collective-permute-done((bf16[592,128]{1,0:T(8,128)(2,1)S(1)}, bf16[592,128]{1,0:T(8,128)(2,1)S(1)}, u32[]{:S(2)}, u32[]{:S(2)}) %collective-permute-start.10) | collective-permute-done | bytes 151584 | tf_op jit(solution)/shard_map/ppermute | solution.py:499
  42.8 0.5 collective-permute-done.11
  43.3 3.6 %collective-permute-done.12 = bf16[592,128]{1,0:T(8,128)(2,1)S(1)} collective-permute-done((bf16[592,128]{1,0:T(8,128)(2,1)S(1)}, bf16[592,128]{1,0:T(8,128)(2,1)S(1)}, u32[]{:S(2)}, u32[]{:S(2)}) %collective-permute-start.12) | collective-permute-done | bytes 151584 | tf_op jit(solution)/shard_map/ppermute | solution.py:499
  47.0 0.0 collective-permute-done.9
  47.0 0.1 add_convert_fusion.one
  47.1 0.1 collective-permute-start.13
  47.2 1.4 %collective-permute-done.13.other = bf16[592,128]{1,0:T(8,128)(2,1)S(1)} collective-permute-done((bf16[592,128]{1,0:T(8,128)(2,1)S(1)}, bf16[592,128]{1,0:T(8,128)(2,1)S(1)}, u32[]{:S(2)}, u32[]{:S(2)}) %collective-permute-start.13) | collective-permute-done | bytes 151584 | tf_op jit(solution)/shard_map/ppermute | solution.py:489
  48.5 0.1 shard_map.115
  48.6 1.0 %collective-permute-start.14 = (bf16[304,128]{1,0:T(8,128)(2,1)S(1)}, bf16[304,128]{1,0:T(8,128)(2,1)S(1)}, u32[]{:S(2)}, u32[]{:S(2)}) collective-permute-start(bf16[304,128]{1,0:T(8,128)(2,1)S(1)} %get-tuple-element.51), channel_id=1, source_target_pairs={{0,16},{8,24},{16,0},{24,8},{1,17},{9,25},{17,1},{25,9},{2,18},{10... | collective-permute-start | bytes 233480 | tf_op jit(solution)/shard_map/ppermute | solution.py:524
  49.6 3.4 %collective-permute-done.14.mine = bf16[304,128]{1,0:T(8,128)(2,1)S(1)} collective-permute-done((bf16[304,128]{1,0:T(8,128)(2,1)S(1)}, bf16[304,128]{1,0:T(8,128)(2,1)S(1)}, u32[]{:S(2)}, u32[]{:S(2)}) %collective-permute-start.14) | collective-permute-done | bytes 77856 | tf_op jit(solution)/shard_map/ppermute | solution.py:524
  53.1 0.0 collective-permute-start.15
  53.1 1.1 %shard_map.114 = (bf16[8,16,512]{2,1,0:T(8,128)(2,1)}, bf16[16,32,256]{2,1,0:T(8,128)(2,1)}) custom-call(bf16[512,512]{1,0:T(8,128)(2,1)S(1)} %get-tuple-element.38.grad_one, bf16[512,256]{1,0:T(8,128)(2,1)S(1)} %get-tuple-element.39.reduce_t, bf16[128,512]{1,0:T(8,128)(2,1)S(1)} %get-tuple-element.40.grad_sum, ...), custom_call_target="tpu_custom_call" | custom-call | flops 134217728 | bytes 1703936 | tf_op jit(solution)/shard_map/pallas_call | solution.py:432
  54.2 0.2 collective-permute-done.15.theirs
  54.4 0.8 %shard_map.116 = (f32[64,256]{1,0:T(8,128)}, f32[64,144]{1,0:T(8,128)}, f32[64,512]{1,0:T(8,128)}, f32[64,256]{1,0:T(8,128)}) custom-call(bf16[592,128]{1,0:T(8,128)(2,1)S(1)} %get-tuple-element.50.whole, bf16[304,128]{1,0:T(8,128)(2,1)S(1)} %collective-permute-done.14.mine, bf16[304,128]{1,0:T(8,128)(2,1)S(1)} %collective-permute-done.15.theirs), custom_call_target="tpu_custom_call" | custom-call | bytes 606208 | tf_op jit(solution)/shard_map/pallas_call | solution.py:432
  (2 shorter events, 0.1 us)
Async XLA Ops:
  3.0 7.8 %collective-permute-start = (bf16[128,256]{1,0:T(8,128)(2,1)}, bf16[128,256]{1,0:T(8,128)(2,1)S(1)}, u32[]{:S(2)}, u32[]{:S(2)}) collective-permute-start(bf16[128,256]{1,0:T(8,128)(2,1)} %get-tuple-element.31), channel_id=1, source_target_pairs={{0,8},{8,0},{16,24},{24,16},{1,9},{9,1},{17,25},{25,17},{2,10},{10... | collective-permute-start | bytes 196616 | tf_op jit(solution)/shard_map/ppermute | solution.py:489
  3.5 7.3 %collective-permute-start.1 = (bf16[128,256]{1,0:T(8,128)(2,1)}, bf16[128,256]{1,0:T(8,128)(2,1)S(1)}, u32[]{:S(2)}, u32[]{:S(2)}) collective-permute-start(bf16[128,256]{1,0:T(8,128)(2,1)} %get-tuple-element.31), channel_id=1, source_target_pairs={{8,16},{16,8},{9,17},{17,9},{10,18},{18,10},{11,19},{19,11},{12,20... | collective-permute-start | bytes 196616 | tf_op jit(solution)/shard_map/ppermute | solution.py:485
  4.2 9.9 %collective-permute-start.4 = (bf16[592,128]{1,0:T(8,128)(2,1)}, bf16[592,128]{1,0:T(8,128)(2,1)S(1)}, u32[]{:S(2)}, u32[]{:S(2)}) collective-permute-start(bf16[592,128]{1,0:T(8,128)(2,1)} %get-tuple-element.37.own), channel_id=1, source_target_pairs={{0,2},{1,3},{2,4},{3,5},{4,6},{5,7},{6,0},{7,1},{8,11},{9,10},{10,... | collective-permute-start | bytes 454664 | tf_op jit(solution)/shard_map/ppermute | solution.py:499
  6.8 13.4 %collective-permute-start.5 = (bf16[592,128]{1,0:T(8,128)(2,1)}, bf16[592,128]{1,0:T(8,128)(2,1)S(1)}, u32[]{:S(2)}, u32[]{:S(2)}) collective-permute-start(bf16[592,128]{1,0:T(8,128)(2,1)} %get-tuple-element.37.own), channel_id=1, source_target_pairs={{0,4},{1,5},{2,6},{3,7},{4,0},{5,1},{6,2},{7,3},{8,13},{9,12},{10,... | collective-permute-start | bytes 454664 | tf_op jit(solution)/shard_map/ppermute | solution.py:499
  9.4 10.8 %collective-permute-start.6 = (bf16[592,128]{1,0:T(8,128)(2,1)}, bf16[592,128]{1,0:T(8,128)(2,1)S(1)}, u32[]{:S(2)}, u32[]{:S(2)}) collective-permute-start(bf16[592,128]{1,0:T(8,128)(2,1)} %get-tuple-element.37.own), channel_id=1, source_target_pairs={{0,6},{1,7},{2,0},{3,1},{4,2},{5,3},{6,4},{7,5},{8,15},{9,14},{10,... | collective-permute-start | bytes 454664 | tf_op jit(solution)/shard_map/ppermute | solution.py:499
  10.8 0.9 %copy-start.2 = (bf16[560,128]{1,0:T(8,128)(2,1)S(1)}, bf16[560,128]{1,0:T(8,128)(2,1)}, u32[]{:S(2)}) copy-start(bf16[560,128]{1,0:T(8,128)(2,1)} %get-tuple-element.32.draft) | copy-start | bytes 430084
  11.7 8.5 %collective-permute-start.2 = (bf16[496,128]{1,0:T(8,128)(2,1)S(1)}, bf16[496,128]{1,0:T(8,128)(2,1)S(1)}, u32[]{:S(2)}, u32[]{:S(2)}) collective-permute-start(bf16[496,128]{1,0:T(8,128)(2,1)S(1)} %get-tuple-element.33), channel_id=1, source_target_pairs={{0,1},{1,0},{2,3},{3,2},{4,5},{5,4},{6,7},{7,6},{8,9},{9,8},{10,11... | collective-permute-start | bytes 380936 | tf_op jit(solution)/shard_map/ppermute | solution.py:489
  13.3 9.0 %copy-start = (bf16[16,32,256]{2,1,0:T(8,128)(2,1)S(1)}, bf16[16,32,256]{2,1,0:T(8,128)(2,1)}, u32[]{:S(2)}) copy-start(bf16[16,32,256]{2,1,0:T(8,128)(2,1)} %region.1) | copy-start | bytes 786436
  13.3 9.0 %copy-start.1 = (bf16[8,16,512]{2,1,0:T(8,128)(2,1)S(1)}, bf16[8,16,512]{2,1,0:T(8,128)(2,1)}, u32[]{:S(2)}) copy-start(bf16[8,16,512]{2,1,0:T(8,128)(2,1)} %cot.1) | copy-start | bytes 393220
  13.3 0.8 %collective-permute-start.3 = (bf16[192,128]{1,0:T(8,128)(2,1)S(1)}, bf16[192,128]{1,0:T(8,128)(2,1)S(1)}, u32[]{:S(2)}, u32[]{:S(2)}) collective-permute-start(bf16[192,128]{1,0:T(8,128)(2,1)S(1)} %get-tuple-element.34), channel_id=1, source_target_pairs={{1,2},{2,1},{3,4},{4,3},{5,6},{6,5},{9,10},{10,9},{11,12},{12,11},... | collective-permute-start | bytes 147464 | tf_op jit(solution)/shard_map/ppermute | solution.py:485
  20.3 3.6 %copy-start.3 = (bf16[592,128]{1,0:T(8,128)(2,1)S(1)}, bf16[592,128]{1,0:T(8,128)(2,1)}, u32[]{:S(2)}) copy-start(bf16[592,128]{1,0:T(8,128)(2,1)} %get-tuple-element.37.own) | copy-start | bytes 454660
  20.3 3.6 %collective-permute-start.7 = (bf16[2080,128]{1,0:T(8,128)(2,1)S(1)}, bf16[2080,128]{1,0:T(8,128)(2,1)S(1)}, u32[]{:S(2)}, u32[]{:S(2)}) collective-permute-start(bf16[2080,128]{1,0:T(8,128)(2,1)S(1)} %shard_map.112.passed), channel_id=1, source_target_pairs={{0,8},{8,0},{16,24},{24,16},{1,9},{9,1},{17,25},{25,17},{2,10},{10... | collective-permute-start | bytes 1597448 | tf_op jit(solution)/shard_map/ppermute | solution.py:489
  28.2 2.1 %collective-permute-start.8 = (bf16[4,592,128]{2,1,0:T(8,128)(2,1)S(1)}, bf16[4,592,128]{2,1,0:T(8,128)(2,1)S(1)}, u32[]{:S(2)}, u32[]{:S(2)}) collective-permute-start(bf16[4,592,128]{2,1,0:T(8,128)(2,1)S(1)} %get-tuple-element.46), channel_id=1, source_target_pairs={{0,8},{8,0},{16,24},{24,16},{1,9},{9,1},{17,25},{25,17},{2,10},{10... | collective-permute-start | bytes 1818632 | tf_op jit(solution)/shard_map/ppermute | solution.py:489
  30.4 12.5 %collective-permute-start.10 = (bf16[592,128]{1,0:T(8,128)(2,1)S(1)}, bf16[592,128]{1,0:T(8,128)(2,1)S(1)}, u32[]{:S(2)}, u32[]{:S(2)}) collective-permute-start(bf16[592,128]{1,0:T(8,128)(2,1)S(1)} %get-tuple-element.59), channel_id=1, source_target_pairs={{0,4},{1,5},{2,6},{3,7},{4,0},{5,1},{6,2},{7,3},{8,13},{9,12},{10,... | collective-permute-start | bytes 454664 | tf_op jit(solution)/shard_map/ppermute | solution.py:499
  34.8 8.6 %collective-permute-start.11 = (bf16[592,128]{1,0:T(8,128)(2,1)S(1)}, bf16[592,128]{1,0:T(8,128)(2,1)S(1)}, u32[]{:S(2)}, u32[]{:S(2)}) collective-permute-start(bf16[592,128]{1,0:T(8,128)(2,1)S(1)} %get-tuple-element.58), channel_id=1, source_target_pairs={{0,6},{1,7},{2,0},{3,1},{4,2},{5,3},{6,4},{7,5},{8,15},{9,14},{10,... | collective-permute-start | bytes 454664 | tf_op jit(solution)/shard_map/ppermute | solution.py:499
  35.8 11.1 %collective-permute-start.12 = (bf16[592,128]{1,0:T(8,128)(2,1)S(1)}, bf16[592,128]{1,0:T(8,128)(2,1)S(1)}, u32[]{:S(2)}, u32[]{:S(2)}) collective-permute-start(bf16[592,128]{1,0:T(8,128)(2,1)S(1)} %get-tuple-element.57), channel_id=1, source_target_pairs={{0,2},{1,3},{2,4},{3,5},{4,6},{5,7},{6,0},{7,1},{8,11},{9,10},{10,... | collective-permute-start | bytes 454664 | tf_op jit(solution)/shard_map/ppermute | solution.py:499
  36.8 10.2 %collective-permute-start.9 = (bf16[592,128]{1,0:T(8,128)(2,1)S(1)}, bf16[592,128]{1,0:T(8,128)(2,1)S(1)}, u32[]{:S(2)}, u32[]{:S(2)}) collective-permute-start(bf16[592,128]{1,0:T(8,128)(2,1)S(1)} %get-tuple-element.56), channel_id=1, source_target_pairs={{8,9},{9,8},{10,11},{11,10},{12,13},{13,12},{14,15},{15,14},{24,25... | collective-permute-start | bytes 454664 | tf_op jit(solution)/shard_map/ppermute | solution.py:499
  47.1 1.4 %collective-permute-start.13 = (bf16[592,128]{1,0:T(8,128)(2,1)S(1)}, bf16[592,128]{1,0:T(8,128)(2,1)S(1)}, u32[]{:S(2)}, u32[]{:S(2)}) collective-permute-start(bf16[592,128]{1,0:T(8,128)(2,1)S(1)} %add_convert_fusion.one), channel_id=1, source_target_pairs={{0,8},{8,0},{16,24},{24,16},{1,9},{9,1},{17,25},{25,17},{2,10},{10... | collective-permute-start | bytes 454664 | tf_op jit(solution)/shard_map/ppermute | solution.py:489
  48.6 4.5 %collective-permute-start.14 = (bf16[304,128]{1,0:T(8,128)(2,1)S(1)}, bf16[304,128]{1,0:T(8,128)(2,1)S(1)}, u32[]{:S(2)}, u32[]{:S(2)}) collective-permute-start(bf16[304,128]{1,0:T(8,128)(2,1)S(1)} %get-tuple-element.51), channel_id=1, source_target_pairs={{0,16},{8,24},{16,0},{24,8},{1,17},{9,25},{17,1},{25,9},{2,18},{10... | collective-permute-start | bytes 233480 | tf_op jit(solution)/shard_map/ppermute | solution.py:524
  53.1 1.3 %collective-permute-start.15 = (bf16[304,128]{1,0:T(8,128)(2,1)S(1)}, bf16[304,128]{1,0:T(8,128)(2,1)S(1)}, u32[]{:S(2)}, u32[]{:S(2)}) collective-permute-start(bf16[304,128]{1,0:T(8,128)(2,1)S(1)} %collective-permute-done.14.mine), channel_id=1, source_target_pairs={{0,8},{8,0},{16,24},{24,16},{1,9},{9,1},{17,25},{25,17},{2,10},{10... | collective-permute-start | bytes 233480 | tf_op jit(solution)/shard_map/ppermute | solution.py:489
